TPU v7x, 256 devices: a whole 4x4x8 slice. The times are simulated.
256 devices in a mesh: row: 4 (over x_lo, core), col: 16 (over z, x_hi), layer: 4 (over y).
Axes of the slice: x: 4 (x_hi: 2, x_lo: 2; x = x_hi * 2 + x_lo), y: 4, z: 8, core: 2. Of those that a mesh axis runs over, the one named last changes fastest.
Arguments:
- a_blocks: float32 [384, 12, 128, 128], P(('row', 'col'), 'layer'), may hold values from -0.5 to 0.5
- a_inner: int32 [384, 12], P(('row', 'col'), 'layer'), may hold values from 0 to 511, as said below
- b_blocks: float32 [128, 4, 16, 128, 128], P('row', 'layer', 'col'), may hold values from -6 to 6
- b_cols: int32 [128, 4, 16], P('row', 'layer', 'col'), may hold values from 0 to 511, as said below
- c_cols: int32 [384, 16], P('row', 'col'), may hold values from 0 to 511, as said below
Outputs:
- c_blocks: float32 [384, 16, 128, 128], P(('row', 'layer'), 'col')
Inputs may be any that keep to these rules, and one draw needn't show every extreme that they name: a_inner[i, a] % 4 equals a // 3; the inner indices of one row are distinct. b_cols[r, l, t] % 16 equals t; the block columns of one row of B are distinct. c_cols[i, u] % 16 equals u; the kept block columns of one row are distinct.
All inputs are finite; a program needn't handle non-finite values.
Results may differ from a plain program's by a relative error of at most 0.0003.
Values sent between devices are 32-bit elements; how exact they have to be, the bound alone decides.
No kernel may reach another device: no remote copies, remote signals or barrier semaphores. Data moves between devices by JAX's collectives and lax.ppermute only.
A program may use at most 128 MiB of HBM per device.

v0:
```python
import jax
import jax.numpy as jnp
from jax import lax
from jax.sharding import PartitionSpec as P

HIGHEST = lax.Precision.HIGHEST


def block_rows(blocks, inner_ids, kept_cols, b_stack, b_ids, layer_count):
    b_index = inner_ids // layer_count
    picked = jnp.take(b_stack, b_index, axis=0)
    picked_ids = jnp.take(b_ids, b_index, axis=0)
    matches = (picked_ids[:, :, :, None] == kept_cols[:, None, None, :]).astype(jnp.float32)
    products = jnp.einsum("raxy,rajyz->rajxz", blocks, picked, precision=HIGHEST)
    return jnp.einsum("rajc,rajxz->rcxz", matches, products, precision=HIGHEST)


def per_device(a_blocks, a_inner, b_blocks, b_cols, c_cols):
    layer_count = lax.axis_size("layer")
    gathered_b, gathered_ids = (
        lax.all_gather(b_blocks, "row", axis=0, tiled=True),
        lax.all_gather(b_cols, "row", axis=0, tiled=True),
    )
    b_stack = gathered_b[:, 0]
    b_ids = gathered_ids[:, 0]
    contrib = block_rows(
        lax.all_gather(a_blocks, "col", axis=0, tiled=True),
        lax.all_gather(a_inner, "col", axis=0, tiled=True),
        c_cols,
        b_stack,
        b_ids,
        layer_count,
    )
    return lax.psum_scatter(contrib, "layer", scatter_dimension=0, tiled=True)


def solution(mesh):
    return jax.shard_map(
        per_device,
        mesh=mesh,
        in_specs=(
            P(("row", "col"), "layer", None, None),
            P(("row", "col"), "layer"),
            P("row", "layer", "col", None, None),
            P("row", "layer", "col"),
            P("row", "col"),
        ),
        out_specs=P(("row", "layer"), "col", None, None),
        check_vma=False,
    )
```

profile of v0, /device:TPU:6, one launch (start us, length us, event | category | flops | bytes accessed | tf_op | source)
XLA Modules:
  0.0 472.7 jit_solution(3318975957626269107)
XLA Ops:
  6.5 0.0 all-gather.4.cloned.1.call-start
  6.5 0.7 all-gather.4.cloned.1.call-update
  7.3 0.0 all-gather.6.cloned.1.call-start
  7.3 0.7 all-gather.6.cloned.1.call-update
  8.0 0.0 reduce-scatter.2.cloned.1.call-start
  8.1 40.8 %all-gather = s32[16,6,3]{1,2,0:T(4,128)S(1)} all-gather(s32[1,6,3]{1,2,0:T(4,128)} %bitcast.22), channel_id=1, replica_groups=mesh['row'=4,'col'=16,'layer'=4] {'col'}, dimensions={0}, use_global_device_ids=true | all-gather | bytes 1224 | tf_op jit(solution)/shard_map/all_gather | solution.py:28
  48.9 0.1 reshape.61
  49.0 0.1 copy.13
  49.1 0.2 reshape.31
  49.3 1.3 dynamic-slice
  51.2 0.8 bitcast_dynamic-update-slice_fusion
  51.9 4.3 all-reduce
  56.3 0.0 copy-start
  56.3 2.4 gather_fusion
  58.6 0.2 gather.13
  58.8 0.1 copy.14
  58.9 0.0 copy-done
  58.9 0.1 copy.22
  59.0 0.1 copy.15
  59.2 35.7 %all-gather.4.cloned.1.call-done = f32[128,1,1,128,128]{4,3,2,1,0:T(8,128)} async-done(((f32[32,1,1,128,128]{4,3,2,1,0:T(8,128)}), f32[128,1,1,128,128]{4,3,2,1,0:T(8,128)}) %all-gather.4.cloned.1.call-update) | async-done | bytes 8388624 | tf_op jit(solution)/shard_map/all_gather | solution.py:21
  94.8 16.5 %gather_fusion.1 = f32[288,128,128]{2,1,0:T(8,128)} fusion(f32[128,128,128]{2,1,0:T(8,128)} %bitcast.20, s32[1024]{0:T(1024)S(1)} %pad_clamp_fusion), kind=kCustom, calls=%fused_computation.1 | custom fusion | bytes 37749888 | tf_op jit(solution)/shard_map/jit(_take)/gather | solution.py:11
  111.3 19.1 %copy.16 = f32[96,3,128,128]{2,3,1,0:T(8,128)} copy(f32[96,3,128,128]{3,2,1,0:T(8,128)} %bitcast.19) | data formatting | bytes 37748736 | tf_op jit(solution)/shard_map/jit(_take)/gather | solution.py:11
  130.4 216.6 %all-gather.6.cloned.1.call-done = f32[96,3,128,128]{3,2,1,0:T(8,128)} async-done(((f32[6,3,128,128]{3,2,1,0:T(8,128)}), f32[96,3,128,128]{3,2,1,0:T(8,128)}) %all-gather.6.cloned.1.call-update) | async-done | bytes 18874384 | tf_op jit(solution)/shard_map/all_gather | solution.py:27
  347.0 47.5 %fusion = f32[96,128,128]{1,2,0:T(8,128)} fusion(f32[96,3]{1,0:T(8,128)S(1)} %copy.22, f32[96,3,128,128]{3,2,1,0:T(8,128)} %all-gather.6.cloned.1.call-done, f32[96,3,128,128]{2,3,1,0:T(8,128)} %copy.16, pred[96,3]{1,0:T(8,128)(4,1)S(1)} %copy.15), kind=kOutput, calls=%fused_computation.3 | convolution fusion | flops 7260340224 | bytes 44041632 | tf_op jit(solution)/shard_map/raxy,rajyz->rajxz/dot_general | solution.py:14
  394.5 6.6 %copy.21 = f32[96,128,128]{2,1,0:T(8,128)} copy(f32[96,128,128]{1,2,0:T(8,128)} %fusion) | data formatting | bytes 12582912 | tf_op jit(solution)/shard_map/rajc,rajxz->rcxz/dot_general | solution.py:15
  401.1 0.0 reduce-scatter.2.cloned.1.call-update
  401.1 65.0 %reduce-scatter.2.cloned.1.call-done = f32[24,1,128,128]{3,2,1,0:T(8,128)} async-done(((f32[96,1,128,128]{3,2,1,0:T(8,128)}), f32[24,1,128,128]{3,2,1,0:T(8,128)}) %reduce-scatter.2.cloned.1.call-update) | async-done | bytes 1572880 | tf_op jit(solution)/shard_map/reduce_scatter | solution.py:34
  (5 shorter events, 0.1 us)
Async XLA Ops:
  6.5 88.3 %all-gather.4.cloned.1.call-start = ((), (), s32[]{:S(2)}) async-start(), calls=%async_computation.1 | async-start | bytes 10485760 | tf_op jit(solution)/shard_map/all_gather | solution.py:21
  7.3 339.8 %all-gather.6.cloned.1.call-start = ((), (), s32[]{:S(2)}) async-start(), calls=%async_computation.2 | async-start | bytes 20054016 | tf_op jit(solution)/shard_map/all_gather | solution.py:27
  8.0 458.2 %reduce-scatter.2.cloned.1.call-start = ((), (), s32[]{:S(2)}) async-start(), calls=%async_computation.3 | async-start | bytes 7864320 | tf_op jit(solution)/shard_map/reduce_scatter | solution.py:34
  56.3 2.6 copy-start
Sparse Core Ops, SparseCore 0:
  9.2 85.5 all-gather.3
  97.4 249.5 all-gather.5
  401.2 64.8 reduce-scatter.1
where the time goes:
time: 474 us; the launch traced here: 473 us
  waiting for transfers between devices  319 us (67%)
  matrix products  47.5 us (10%)
  local copies, waits for them, and re-layouts  47.4 us (10%)
  blocking collectives  45.1 us (10%)
  between operations  13.8 us (3%)
    all_gather x1, waiting for transfers between devices, per_device(): lax.all_gather(a_blocks, 'col', axis=0, tiled=True)  217 us
    reduce_scatter x1, waiting for transfers between devices, per_device(): return lax.psum_scatter(contrib, 'layer', scatter_dimension=0, tiled=True)  65 us
    dot_general x1, matrix products, block_rows(): jnp.einsum('raxy,rajyz->rajxz', blocks, picked, precision=HIGHEST)  47.5 us
    all_gather x1, blocking collectives, per_device(): lax.all_gather(a_inner, 'col', axis=0, tiled=True)  40.8 us
    all_gather x1, waiting for transfers between devices, per_device(): lax.all_gather(b_blocks, 'row', axis=0, tiled=True)  35.7 us
    gather x2, local copies, waits for them, and re-layouts, block_rows(): picked = jnp.take(b_stack, b_index, axis=0)  35.6 us
  transfers between devices with their start and end apart: 3, of which 3 were waited for; matrix products, arithmetic and copies ran while one was open for 9% of the time, Pallas kernels for 0%

commit v1 on v0

v1 whole, which is shorter than its diff:
```python
import functools

import jax
import jax.numpy as jnp
from jax import lax
from jax.experimental import pallas as pl
from jax.experimental.pallas import tpu as pltpu
from jax.sharding import Mesh, PartitionSpec as P

BS = 128
ROWS = 6
KAL = 3
NB = 32
IDX = 256
OFF_B = ROWS * KAL
OFF_C = OFF_B + NB
PASSES = ((0, 6),)


def shift(value, axes, size, step):
    return lax.ppermute(value, axes, [(i, (i + step) % size) for i in range(size)])


def shift_x(value, step):
    at = lambda x: (x % 2) * 2 + x % 4 // 2
    return lax.ppermute(value, ("xl", "xh"), [(at(x), at(x + step)) for x in range(4)])


def device_index(xl, co, z, xh):
    return (((xl * 2 + co) * 8 + z) * 2 + xh) * IDX


def split(value):
    high = value.astype(jnp.bfloat16)
    low = (value - high.astype(jnp.float32)).astype(jnp.bfloat16)
    return high, low


def product_kernel(first, rows, n_a, n_b, place, table, *refs):
    a_refs, refs = refs[:n_a], refs[n_a:]
    b_refs, refs = refs[:n_b], refs[n_b:]
    outs, (a_v, b_v, c_v, a_sem, b_sem, c_sem) = refs[:8], refs[8:]
    xl, co, z, xh, y = (place[i] for i in range(5))
    x = xh * 2 + xl
    n = rows * KAL

    copies = []
    for i, ref in enumerate(a_refs[:7]):
        step = (0, 7, 1, 6, 2, 5, 3)[i]
        copies.append(pltpu.make_async_copy(ref, a_v.at[pl.ds(step * n, n)], a_sem))
    half = n // 2
    copies.append(pltpu.make_async_copy(a_refs[7], a_v.at[pl.ds(4 * n, half)], a_sem))
    copies.append(pltpu.make_async_copy(a_refs[8], a_v.at[pl.ds(4 * n + half, n - half)], a_sem))
    for i, ref in enumerate(b_refs):
        step, lead, count = ((0, 0, NB), (3, 0, NB), (1, 0, NB), (2, 0, NB // 2), (2, NB // 2, NB // 2))[i // 2]
        there = lax.rem(x + step, 4)
        core = co if i % 2 == 0 else 1 - co
        slot = jnp.where(there // 2 == xh, 0, 1)
        start = slot * 4 * NB + (lax.rem(there, 2) * 2 + core) * NB + lead
        copies.append(pltpu.make_async_copy(ref, b_v.at[pl.ds(start, count)], b_sem))
    for copy in copies:
        copy.start()
    for copy in copies:
        copy.wait()

    def one_row(d, h, i):
        there = 2 * lax.rem(y + d, 4) + h
        chunk = lax.rem(there - z + 8, 8)
        row = first + i
        a_at = device_index(xl, co, there, xh) + row * KAL
        c_at = OFF_C + (there * 2 + xh) * ROWS + row
        kept = (table[device_index(xl, co, z, xh) + c_at], table[device_index(xl, co, z, 1 - xh) + c_at])
        total = [jnp.zeros((BS, BS), jnp.float32)] * 2
        for a in range(KAL):
            k = table[a_at + a] // 4
            owner, j = k // NB, lax.rem(k, NB)
            block_high, block_low = split(a_v[chunk * n + i * KAL + a])
            picked = jnp.concatenate((b_v[k], b_v[4 * NB + k]), axis=1)
            picked_high, picked_low = split(picked)
            dot = functools.partial(jnp.dot, preferred_element_type=jnp.float32)
            product = dot(block_high, picked_high) + (dot(block_low, picked_high) + dot(block_high, picked_low))
            for s in range(2):
                col = table[device_index(owner // 2, lax.rem(owner, 2), z, xh if s == 0 else 1 - xh) + OFF_B + j]
                match = jnp.where(col == kept[s], 1.0, 0.0).astype(jnp.float32)
                total[s] = total[s] + match * product[:, s * BS:(s + 1) * BS]
        for s in range(2):
            c_v[d * 2 + h, s, i] = total[s]

    done = []
    for d in (2, 1, 3, 0):
        for h in range(2):
            def body(i, carry, d=d, h=h):
                one_row(d, h, i)
                return carry

            lax.fori_loop(0, rows, body, 0)
            done.append(pltpu.make_async_copy(c_v.at[d * 2 + h], outs[d * 2 + h], c_sem))
            done[-1].start()
    for copy in done:
        copy.wait()


def products(first, rows, place, table, a_parts, b_parts):
    n = rows * KAL
    out = jax.ShapeDtypeStruct((2, rows, BS, BS), jnp.float32)
    anywhere = pl.BlockSpec(memory_space=pl.ANY)
    scalars = pl.BlockSpec(memory_space=pltpu.SMEM)
    return pl.pallas_call(
        functools.partial(product_kernel, first, rows, len(a_parts), len(b_parts)),
        out_shape=[out] * 8,
        in_specs=[scalars, scalars] + [anywhere] * (len(a_parts) + len(b_parts)),
        out_specs=[anywhere] * 8,
        scratch_shapes=[
            pltpu.VMEM((8 * n, BS, BS), jnp.float32),
            pltpu.VMEM((8 * NB, BS, BS), jnp.float32),
            pltpu.VMEM((8, 2, rows, BS, BS), jnp.float32),
            pltpu.SemaphoreType.DMA,
            pltpu.SemaphoreType.DMA,
            pltpu.SemaphoreType.DMA,
        ],
        compiler_params=pltpu.CompilerParams(vmem_limit_bytes=48 * 1024 * 1024),
    )(place, table, *a_parts, *b_parts)


def gather_a(blocks):
    n = blocks.shape[0]
    right = left = blocks
    parts = [blocks]
    for _ in range(3):
        right, left = shift(right, "z", 8, 1), shift(left, "z", 8, -1)
        parts += [right, left]
    parts += [shift(right[:n // 2], "z", 8, 1), shift(left[n // 2:], "z", 8, -1)]
    return parts


def gather_b(blocks):
    parts = [blocks, shift(blocks, "co", 2, 1)]
    right, left = shift_x(blocks, 1), shift_x(blocks, -1)
    far = (shift_x(right[:NB // 2], 1), shift_x(left[NB // 2:], -1))
    for part in (right, left) + far:
        parts += [part, shift(part, "co", 2, 1)]
    return parts


def scatter_sum(outs):
    far_right = shift(outs[4], "y", 4, 1)
    far_left = shift(outs[5], "y", 4, -1)
    right = (shift(outs[2] + far_right, "y", 4, 1), shift(outs[3], "y", 4, 1))
    left = (shift(outs[6], "y", 4, -1), shift(outs[7] + far_left, "y", 4, -1))
    sums = [outs[h] + right[h] + left[h] for h in range(2)]
    mine = jnp.stack([s[0] for s in sums])
    other = shift(jnp.stack([s[1] for s in sums]), "xh", 2, 1)
    return mine, other


def per_device(a_blocks, a_inner, b_blocks, b_cols, c_cols):
    place = jnp.stack([lax.axis_index(name) for name in ("xl", "co", "z", "xh", "y")])
    ids = jnp.concatenate([a_inner.reshape(-1), b_cols.reshape(-1), c_cols.reshape(-1)])
    ids = jnp.pad(ids, (0, IDX - ids.shape[0]))
    table = lax.all_gather(ids, ("xl", "co", "z", "xh"), axis=0, tiled=True)
    b_parts = gather_b(b_blocks.reshape(NB, BS, BS))
    mine, other = [], []
    for first, rows in PASSES:
        a_parts = gather_a(a_blocks[first:first + rows].reshape(rows * KAL, BS, BS))
        outs = products(first, rows, place, table, a_parts, b_parts)
        own_part, other_part = scatter_sum(outs)
        mine.append(own_part)
        other.append(other_part)
    mine, other = jnp.concatenate(mine, axis=1), jnp.concatenate(other, axis=1)
    xh = lax.axis_index("xh")
    result = jnp.stack([jnp.where(xh == 0, mine, other), jnp.where(xh == 0, other, mine)], axis=1)
    return result.reshape(4 * ROWS, 1, BS, BS)


def solution(mesh):
    fine = Mesh(mesh.devices.reshape(2, 2, 8, 2, 4), ("xl", "co", "z", "xh", "y"))
    return jax.shard_map(
        per_device,
        mesh=fine,
        in_specs=(
            P(("xl", "co", "z", "xh"), "y", None, None),
            P(("xl", "co", "z", "xh"), "y"),
            P(("xl", "co"), "y", ("z", "xh"), None, None),
            P(("xl", "co"), "y", ("z", "xh")),
            P(("xl", "co"), ("z", "xh")),
        ),
        out_specs=P(("xl", "co", "y"), ("z", "xh"), None, None),
        check_vma=False,
    )
```

time: 474 us -> 362 us (0.76)
  waiting for transfers between devices: 319 us -> 158 us
  blocking collectives: 45.1 us -> 141 us
  matrix products: 47.5 us -> 0 us
  local copies, waits for them, and re-layouts: 47.4 us -> 4.83 us
  starting transfers between devices: 0.08 us -> 31 us
  Pallas kernels: 0 us -> 26 us
  between operations: 13.8 us -> 0.28 us
    all_gather x2 -> x0, waiting for transfers between devices: 252 us -> none  [the longest x1 217 us: per_device(): lax.all_gather(a_blocks, 'col', axis=0, tiled=True)]
    ppermute x0 -> x24, waiting for transfers between devices: none -> 158 us  [the longest x20 119 us: shift(): lax.ppermute(value, axes, [(i, (i + step) % size) for i in range(size)])]
    all_gather x1, blocking collectives: 40.8 us -> 141 us  [per_device(): table = lax.all_gather(ids, ('xl', 'co', 'z', 'xh'), axis=0, tiled=True)]
    reduce_scatter x1 -> x0, waiting for transfers between devices: 65 us -> none  [per_device(): return lax.psum_scatter(contrib, 'layer', scatter_dimension=0, tiled=True)]
    dot_general x1 -> x0, matrix products: 47.5 us -> none  [block_rows(): jnp.einsum('raxy,rajyz->rajxz', blocks, picked, precision=HIGHEST)]
    gather x5 -> x0, local copies, waits for them, and re-layouts: 38.2 us -> none  [the longest x2 35.6 us: block_rows(): picked = jnp.take(b_stack, b_index, axis=0)]
    ppermute x0 -> x24, starting transfers between devices: none -> 31 us  [the longest x20 24.9 us: shift(): lax.ppermute(value, axes, [(i, (i + step) % size) for i in range(size)])]
    pallas_call x0 -> x1, Pallas kernels: none -> 26 us  [products(): pl.pallas_call(functools.partial(product_kernel, first, rows, len(a_parts...]
  transfers between devices with their start and end apart: 3 -> 24, of which waited for: 3 -> 13; matrix products, arithmetic and copies ran while one was open for 9% -> 1% of each run, Pallas kernels for 0% -> 0%
where the time goes in v1:
time: 362 us
  waiting for transfers between devices  158 us (44%)
  blocking collectives  141 us (39%)
  starting transfers between devices  31 us (9%)
  Pallas kernels  26 us (7%)
  local copies, waits for them, and re-layouts  4.83 us (1%)
    all_gather x1, blocking collectives, per_device(): table = lax.all_gather(ids, ('xl', 'co', 'z', 'xh'), axis=0, tiled=True)  141 us
    ppermute x20, waiting for transfers between devices, shift(): lax.ppermute(value, axes, [(i, (i + step) % size) for i in range(size)])  119 us
    ppermute x4, waiting for transfers between devices, shift_x(): lax.ppermute(value, ('xl', 'xh'), [(at(x), at(x + step)) for x in range(4)])  38.6 us
    pallas_call x1, Pallas kernels, products(): pl.pallas_call(functools.partial(product_kernel, first, rows, len(a_parts...  26 us
    ppermute x20, starting transfers between devices, shift(): lax.ppermute(value, axes, [(i, (i + step) % size) for i in range(size)])  24.9 us
  transfers between devices with their start and end apart: 24, of which 13 were waited for; matrix products, arithmetic and copies ran while one was open for 1% of the time, Pallas kernels for 0%

profile of v1, /device:TPU:6, one launch (start us, length us, event | category | flops | bytes accessed | tf_op | source)
XLA Modules:
  0.0 362.0 jit_solution(2451625229589890574)
XLA Ops:
  0.0 5.9 %collective-permute-start.1 = (f32[18,128,128]{2,1,0:T(8,128)}, f32[18,128,128]{2,1,0:T(8,128)S(1)}, u32[]{:S(2)}, u32[]{:S(2)}) collective-permute-start(f32[18,128,128]{2,1,0:T(8,128)} %bitcast.23), channel_id=1, source_target_pairs={{0,56},{8,0},{16,8},{24,16},{32,24},{40,32},{48,40},{56,48},{1,57}... | collective-permute-start | bytes 3538952 | tf_op jit(solution)/shard_map/ppermute | solution.py:21
  5.9 25.5 %collective-permute-done.1.refs_2_ = f32[18,128,128]{2,1,0:T(8,128)S(1)} collective-permute-done((f32[18,128,128]{2,1,0:T(8,128)}, f32[18,128,128]{2,1,0:T(8,128)S(1)}, u32[]{:S(2)}, u32[]{:S(2)}) %collective-permute-start.1) | collective-permute-done | bytes 1179680 | tf_op jit(solution)/shard_map/ppermute | solution.py:21
  31.4 3.6 collective-permute-start.3
  35.0 0.8 collective-permute-start.11
  35.8 2.4 collective-permute-start.9
  38.3 21.0 %collective-permute-done.3.refs_4_ = f32[18,128,128]{2,1,0:T(8,128)S(1)} collective-permute-done((f32[18,128,128]{2,1,0:T(8,128)S(1)}, f32[18,128,128]{2,1,0:T(8,128)S(1)}, u32[]{:S(2)}, u32[]{:S(2)}) %collective-permute-start.3) | collective-permute-done | bytes 1179680 | tf_op jit(solution)/shard_map/ppermute | solution.py:21
  59.3 3.7 %collective-permute-start.5 = (f32[18,128,128]{2,1,0:T(8,128)S(1)}, f32[18,128,128]{2,1,0:T(8,128)S(1)}, u32[]{:S(2)}, u32[]{:S(2)}) collective-permute-start(f32[18,128,128]{2,1,0:T(8,128)S(1)} %collective-permute-done.3.refs_4_), channel_id=1, source_target_pairs={{0,56},{8,0},{16,8},{24,16},{32,24},{40,32},{48,40},{56,48},{1,57}... | collective-permute-start | bytes 3538952 | tf_op jit(solution)/shard_map/ppermute | solution.py:21
  63.0 19.6 %collective-permute-done.11.refs_13_ = f32[32,128,128]{2,1,0:T(8,128)S(1)} collective-permute-done((f32[32,128,128]{2,1,0:T(8,128)}, f32[32,128,128]{2,1,0:T(8,128)S(1)}, u32[]{:S(2)}, u32[]{:S(2)}) %collective-permute-start.11) | collective-permute-done | bytes 2097184 | tf_op jit(solution)/shard_map/ppermute | solution.py:26
  82.9 2.1 slice.34
  85.1 2.8 collective-permute-start.13
  88.0 0.5 collective-permute-start.10
  88.6 18.4 %collective-permute-done.15.refs_17_ = f32[16,128,128]{2,1,0:T(8,128)} collective-permute-done((f32[16,128,128]{2,1,0:T(8,128)S(1)}, f32[16,128,128]{2,1,0:T(8,128)}, u32[]{:S(2)}, u32[]{:S(2)}) %collective-permute-start.15) | collective-permute-done | bytes 1048608 | tf_op jit(solution)/shard_map/ppermute | solution.py:26
  106.9 0.6 collective-permute-start.7
  107.5 0.6 collective-permute-done.13.refs_15_
  108.1 1.6 collective-permute-done.4.refs_5_
  109.8 0.9 slice.32
  110.7 8.3 %collective-permute-done.7.refs_8_ = f32[9,128,128]{2,1,0:T(8,128)S(1)} collective-permute-done((f32[9,128,128]{2,1,0:T(8,128)S(1)}, f32[9,128,128]{2,1,0:T(8,128)S(1)}, u32[]{:S(2)}, u32[]{:S(2)}) %collective-permute-start.7) | collective-permute-done | bytes 589856 | tf_op jit(solution)/shard_map/ppermute | solution.py:21
  119.4 141.0 %all-gather = s32[64,1,256]{2,1,0:T(1,128)S(1)} all-gather(s32[1,1,256]{2,1,0:T(1,128)S(1)} %bitcast.26), channel_id=1, replica_groups=mesh['xl'=2,'co'=2,'z'=8,'xh'=2,'y'=4] {'xl','co','z','xh'}, dimensions={0}, use_global_device_ids=true | all-gather | bytes 66560 | tf_op jit(solution)/shard_map/all_gather | solution.py:160
  260.4 26.0 %shard_map.55 = (f32[2,6,128,128]{3,2,1,0:T(8,128)S(1)}, f32[2,6,128,128]{3,2,1,0:T(8,128)S(1)}, f32[2,6,128,128]{3,2,1,0:T(8,128)S(1)}, f32[2,6,128,128]{3,2,1,...) custom-call(s32[5]{0:T(128)S(1)} %stack.38.place, ...), custom_call_target="tpu_custom_call" | custom-call | tf_op jit(solution)/shard_map/pallas_call | solution.py:108
  286.5 1.7 collective-permute-start.17
  288.1 1.7 collective-permute-start.21
  289.8 1.8 collective-permute-start.19
  291.6 14.6 %collective-permute-done.17 = f32[2,6,128,128]{3,2,1,0:T(8,128)S(1)} collective-permute-done((f32[2,6,128,128]{3,2,1,0:T(8,128)S(1)}, f32[2,6,128,128]{3,2,1,0:T(8,128)S(1)}, u32[]{:S(2)}, u32[]{:S(2)}) %collective-permute-start.17) | collective-permute-done | bytes 786464 | tf_op jit(solution)/shard_map/ppermute | solution.py:21
  306.3 0.4 collective-permute-start.18
  306.7 1.6 collective-permute-start.20
  308.7 2.9 collective-permute-start.22
  311.7 13.8 %collective-permute-done.19 = f32[2,6,128,128]{3,2,1,0:T(8,128)S(1)} collective-permute-done((f32[2,6,128,128]{3,2,1,0:T(8,128)}, f32[2,6,128,128]{3,2,1,0:T(8,128)S(1)}, u32[]{:S(2)}, u32[]{:S(2)}) %collective-permute-start.19) | collective-permute-done | bytes 786464 | tf_op jit(solution)/shard_map/ppermute | solution.py:21
  325.4 2.6 collective-permute-done.18
  328.3 13.7 %collective-permute-done.20 = f32[2,6,128,128]{3,2,1,0:T(8,128)S(1)} collective-permute-done((f32[2,6,128,128]{3,2,1,0:T(8,128)S(1)}, f32[2,6,128,128]{3,2,1,0:T(8,128)S(1)}, u32[]{:S(2)}, u32[]{:S(2)}) %collective-permute-start.20) | collective-permute-done | bytes 786464 | tf_op jit(solution)/shard_map/ppermute | solution.py:21
  342.3 0.4 collective-permute-start.23
  342.7 17.8 %collective-permute-done.23 = f32[2,6,128,128]{3,2,1,0:T(8,128)S(1)} collective-permute-done((f32[2,6,128,128]{3,2,1,0:T(8,128)S(1)}, f32[2,6,128,128]{3,2,1,0:T(8,128)S(1)}, u32[]{:S(2)}, u32[]{:S(2)}) %collective-permute-start.23) | collective-permute-done | bytes 786464 | tf_op jit(solution)/shard_map/ppermute | solution.py:21
  360.8 1.3 copy.11
  (61 shorter events, 2.2 us)
Async XLA Ops:
  0.0 31.4 %collective-permute-start.1 = (f32[18,128,128]{2,1,0:T(8,128)}, f32[18,128,128]{2,1,0:T(8,128)S(1)}, u32[]{:S(2)}, u32[]{:S(2)}) collective-permute-start(f32[18,128,128]{2,1,0:T(8,128)} %bitcast.23), channel_id=1, source_target_pairs={{0,56},{8,0},{16,8},{24,16},{32,24},{40,32},{48,40},{56,48},{1,57}... | collective-permute-start | bytes 3538952 | tf_op jit(solution)/shard_map/ppermute | solution.py:21
  5.9 32.4 %collective-permute-start = (f32[18,128,128]{2,1,0:T(8,128)}, f32[18,128,128]{2,1,0:T(8,128)S(1)}, u32[]{:S(2)}, u32[]{:S(2)}) collective-permute-start(f32[18,128,128]{2,1,0:T(8,128)} %bitcast.24), channel_id=1, source_target_pairs={{0,8},{8,16},{16,24},{24,32},{32,40},{40,48},{48,56},{56,0},{1,9},... | collective-permute-start | bytes 3538952 | tf_op jit(solution)/shard_map/ppermute | solution.py:21
  31.4 27.9 %collective-permute-start.3 = (f32[18,128,128]{2,1,0:T(8,128)S(1)}, f32[18,128,128]{2,1,0:T(8,128)S(1)}, u32[]{:S(2)}, u32[]{:S(2)}) collective-permute-start(f32[18,128,128]{2,1,0:T(8,128)S(1)} %collective-permute-done.1.refs_2_), channel_id=1, source_target_pairs={{0,56},{8,0},{16,8},{24,16},{32,24},{40,32},{48,40},{56,48},{1,57}... | collective-permute-start | bytes 3538952 | tf_op jit(solution)/shard_map/ppermute | solution.py:21
  35.0 47.6 %collective-permute-start.11 = (f32[32,128,128]{2,1,0:T(8,128)}, f32[32,128,128]{2,1,0:T(8,128)S(1)}, u32[]{:S(2)}, u32[]{:S(2)}) collective-permute-start(f32[32,128,128]{2,1,0:T(8,128)} %bitcast.19), channel_id=1, source_target_pairs={{0,132},{128,0},{4,128},{132,4},{1,133},{129,1},{5,129},{133,5},{2... | collective-permute-start | bytes 6291464 | tf_op jit(solution)/shard_map/ppermute | solution.py:26
  35.8 47.1 %collective-permute-start.9 = (f32[32,128,128]{2,1,0:T(8,128)}, f32[32,128,128]{2,1,0:T(8,128)}, u32[]{:S(2)}, u32[]{:S(2)}) collective-permute-start(f32[32,128,128]{2,1,0:T(8,128)} %bitcast.20), channel_id=1, source_target_pairs={{0,128},{128,4},{4,132},{132,0},{1,129},{129,5},{5,133},{133,1},{2... | collective-permute-start | bytes 6291464 | tf_op jit(solution)/shard_map/ppermute | solution.py:26
  38.2 49.7 %collective-permute-start.8 = (f32[32,128,128]{2,1,0:T(8,128)}, f32[32,128,128]{2,1,0:T(8,128)S(1)}, u32[]{:S(2)}, u32[]{:S(2)}) collective-permute-start(f32[32,128,128]{2,1,0:T(8,128)} %bitcast.21), channel_id=1, source_target_pairs={{0,64},{64,0},{1,65},{65,1},{2,66},{66,2},{3,67},{67,3},{4,68},{68... | collective-permute-start | bytes 6291464 | tf_op jit(solution)/shard_map/ppermute | solution.py:21
  38.2 44.6 %copy-start.5 = (f32[18,128,128]{2,1,0:T(8,128)}, f32[18,128,128]{2,1,0:T(8,128)S(1)}, u32[]{:S(2)}) copy-start(f32[18,128,128]{2,1,0:T(8,128)S(1)} %collective-permute-done.refs_1_) | copy-start | bytes 3538948
  38.2 44.6 %collective-permute-start.2 = (f32[18,128,128]{2,1,0:T(8,128)S(1)}, f32[18,128,128]{2,1,0:T(8,128)S(1)}, u32[]{:S(2)}, u32[]{:S(2)}) collective-permute-start(f32[18,128,128]{2,1,0:T(8,128)S(1)} %collective-permute-done.refs_1_), channel_id=1, source_target_pairs={{0,8},{8,16},{16,24},{24,32},{32,40},{40,48},{48,56},{56,0},{1,9},... | collective-permute-start | bytes 3538952 | tf_op jit(solution)/shard_map/ppermute | solution.py:21
  59.3 59.7 %copy-start.6 = (f32[18,128,128]{2,1,0:T(8,128)}, f32[18,128,128]{2,1,0:T(8,128)S(1)}, u32[]{:S(2)}) copy-start(f32[18,128,128]{2,1,0:T(8,128)S(1)} %collective-permute-done.3.refs_4_) | copy-start | bytes 3538948
  59.3 28.7 %collective-permute-start.5 = (f32[18,128,128]{2,1,0:T(8,128)S(1)}, f32[18,128,128]{2,1,0:T(8,128)S(1)}, u32[]{:S(2)}, u32[]{:S(2)}) collective-permute-start(f32[18,128,128]{2,1,0:T(8,128)S(1)} %collective-permute-done.3.refs_4_), channel_id=1, source_target_pairs={{0,56},{8,0},{16,8},{24,16},{32,24},{40,32},{48,40},{56,48},{1,57}... | collective-permute-start | bytes 3538952 | tf_op jit(solution)/shard_map/ppermute | solution.py:21
  82.7 24.2 %collective-permute-start.15 = (f32[16,128,128]{2,1,0:T(8,128)S(1)}, f32[16,128,128]{2,1,0:T(8,128)}, u32[]{:S(2)}, u32[]{:S(2)}) collective-permute-start(f32[16,128,128]{2,1,0:T(8,128)S(1)} %slice.35), channel_id=1, source_target_pairs={{0,132},{128,0},{4,128},{132,4},{1,133},{129,1},{5,129},{133,5},{2... | collective-permute-start | bytes 3145736 | tf_op jit(solution)/shard_map/ppermute | solution.py:26
  82.8 36.2 %copy-start.7 = (f32[18,128,128]{2,1,0:T(8,128)}, f32[18,128,128]{2,1,0:T(8,128)S(1)}, u32[]{:S(2)}) copy-start(f32[18,128,128]{2,1,0:T(8,128)S(1)} %collective-permute-done.2.refs_3_) | copy-start | bytes 3538948
  82.8 26.9 %collective-permute-start.4 = (f32[18,128,128]{2,1,0:T(8,128)S(1)}, f32[18,128,128]{2,1,0:T(8,128)S(1)}, u32[]{:S(2)}, u32[]{:S(2)}) collective-permute-start(f32[18,128,128]{2,1,0:T(8,128)S(1)} %collective-permute-done.2.refs_3_), channel_id=1, source_target_pairs={{0,8},{8,16},{16,24},{24,32},{32,40},{40,48},{48,56},{56,0},{1,9},... | collective-permute-start | bytes 3538952 | tf_op jit(solution)/shard_map/ppermute | solution.py:21
  85.1 34.0 %copy-start.9 = (s32[6,3]{0,1:T(4,128)S(1)}, s32[6,3]{0,1:T(4,128)}, u32[]{:S(2)}) copy-start(s32[6,3]{0,1:T(4,128)} %param.6) | copy-start | bytes 220
  85.1 34.2 %copy-start.10 = (s32[96,1]{0,1:T(1,128)S(1)}, s32[96,1]{0,1:T(1,128)}, u32[]{:S(2)}) copy-start(s32[96,1]{0,1:T(1,128)} %param.9) | copy-start | bytes 1156
  85.1 34.2 %copy-start.11 = (s32[32,1,1]{0,2,1:T(1,128)S(1)}, s32[32,1,1]{0,2,1:T(1,128)}, u32[]{:S(2)}) copy-start(s32[32,1,1]{0,2,1:T(1,128)} %param.8) | copy-start | bytes 388
  85.1 23.0 %collective-permute-start.13 = (f32[16,128,128]{2,1,0:T(8,128)S(1)}, f32[16,128,128]{2,1,0:T(8,128)}, u32[]{:S(2)}, u32[]{:S(2)}) collective-permute-start(f32[16,128,128]{2,1,0:T(8,128)S(1)} %slice.34), channel_id=1, source_target_pairs={{0,128},{128,4},{4,132},{132,0},{1,129},{129,5},{5,133},{133,1},{2... | collective-permute-start | bytes 3145736 | tf_op jit(solution)/shard_map/ppermute | solution.py:26
  87.9 31.1 %copy-start.3 = (f32[32,128,128]{2,1,0:T(8,128)}, f32[32,128,128]{2,1,0:T(8,128)S(1)}, u32[]{:S(2)}) copy-start(f32[32,128,128]{2,1,0:T(8,128)S(1)} %collective-permute-done.8.refs_10_) | copy-start | bytes 6291460
  87.9 172.5 %collective-permute-start.12 = (f32[32,128,128]{2,1,0:T(8,128)S(1)}, f32[32,128,128]{2,1,0:T(8,128)}, u32[]{:S(2)}, u32[]{:S(2)}) collective-permute-start(f32[32,128,128]{2,1,0:T(8,128)S(1)} %collective-permute-done.11.refs_13_), channel_id=1, source_target_pairs={{0,64},{64,0},{1,65},{65,1},{2,66},{66,2},{3,67},{67,3},{4,68},{68... | collective-permute-start | bytes 6291464 | tf_op jit(solution)/shard_map/ppermute | solution.py:21
  88.0 31.0 %copy-start.1 = (f32[18,128,128]{2,1,0:T(8,128)}, f32[18,128,128]{2,1,0:T(8,128)S(1)}, u32[]{:S(2)}) copy-start(f32[18,128,128]{2,1,0:T(8,128)S(1)} %collective-permute-done.5.refs_6_) | copy-start | bytes 3538948
  88.0 172.4 %collective-permute-start.10 = (f32[32,128,128]{2,1,0:T(8,128)}, f32[32,128,128]{2,1,0:T(8,128)}, u32[]{:S(2)}, u32[]{:S(2)}) collective-permute-start(f32[32,128,128]{2,1,0:T(8,128)} %collective-permute-done.9.refs_11_), channel_id=1, source_target_pairs={{0,64},{64,0},{1,65},{65,1},{2,66},{66,2},{3,67},{67,3},{4,68},{68... | collective-permute-start | bytes 6291464 | tf_op jit(solution)/shard_map/ppermute | solution.py:21
  106.9 12.1 %collective-permute-start.7 = (f32[9,128,128]{2,1,0:T(8,128)S(1)}, f32[9,128,128]{2,1,0:T(8,128)S(1)}, u32[]{:S(2)}, u32[]{:S(2)}) collective-permute-start(f32[9,128,128]{2,1,0:T(8,128)S(1)} %slice.33), channel_id=1, source_target_pairs={{0,56},{8,0},{16,8},{24,16},{32,24},{40,32},{48,40},{56,48},{1,57}... | collective-permute-start | bytes 1769480 | tf_op jit(solution)/shard_map/ppermute | solution.py:21
  108.1 152.3 %collective-permute-start.16 = (f32[16,128,128]{2,1,0:T(8,128)}, f32[16,128,128]{2,1,0:T(8,128)}, u32[]{:S(2)}, u32[]{:S(2)}) collective-permute-start(f32[16,128,128]{2,1,0:T(8,128)} %collective-permute-done.15.refs_17_), channel_id=1, source_target_pairs={{0,64},{64,0},{1,65},{65,1},{2,66},{66,2},{3,67},{67,3},{4,68},{68... | collective-permute-start | bytes 3145736 | tf_op jit(solution)/shard_map/ppermute | solution.py:21
  109.8 150.7 %collective-permute-start.14 = (f32[16,128,128]{2,1,0:T(8,128)}, f32[16,128,128]{2,1,0:T(8,128)}, u32[]{:S(2)}, u32[]{:S(2)}) collective-permute-start(f32[16,128,128]{2,1,0:T(8,128)} %collective-permute-done.13.refs_15_), channel_id=1, source_target_pairs={{0,64},{64,0},{1,65},{65,1},{2,66},{66,2},{3,67},{67,3},{4,68},{68... | collective-permute-start | bytes 3145736 | tf_op jit(solution)/shard_map/ppermute | solution.py:21
  119.0 141.4 %collective-permute-start.6 = (f32[9,128,128]{2,1,0:T(8,128)}, f32[9,128,128]{2,1,0:T(8,128)S(1)}, u32[]{:S(2)}, u32[]{:S(2)}) collective-permute-start(f32[9,128,128]{2,1,0:T(8,128)} %slice.32), channel_id=1, source_target_pairs={{0,8},{8,16},{16,24},{24,32},{32,40},{40,48},{48,56},{56,0},{1,9},... | collective-permute-start | bytes 1769480 | tf_op jit(solution)/shard_map/ppermute | solution.py:21
  286.5 19.7 %collective-permute-start.17 = (f32[2,6,128,128]{3,2,1,0:T(8,128)S(1)}, f32[2,6,128,128]{3,2,1,0:T(8,128)S(1)}, u32[]{:S(2)}, u32[]{:S(2)}) collective-permute-start(f32[2,6,128,128]{3,2,1,0:T(8,128)S(1)} %get-tuple-element.15), channel_id=1, source_target_pairs={{0,1},{1,2},{2,3},{3,0},{4,5},{5,6},{6,7},{7,4},{8,9},{9,10},{10,1... | collective-permute-start | bytes 2359304 | tf_op jit(solution)/shard_map/ppermute | solution.py:21
  288.1 20.5 %collective-permute-start.21 = (f32[2,6,128,128]{3,2,1,0:T(8,128)S(1)}, f32[2,6,128,128]{3,2,1,0:T(8,128)S(1)}, u32[]{:S(2)}, u32[]{:S(2)}) collective-permute-start(f32[2,6,128,128]{3,2,1,0:T(8,128)S(1)} %get-tuple-element.20), channel_id=1, source_target_pairs={{0,3},{1,0},{2,1},{3,2},{4,7},{5,4},{6,5},{7,6},{8,11},{9,8},{10,9... | collective-permute-start | bytes 2359304 | tf_op jit(solution)/shard_map/ppermute | solution.py:21
  289.8 35.7 %collective-permute-start.19 = (f32[2,6,128,128]{3,2,1,0:T(8,128)}, f32[2,6,128,128]{3,2,1,0:T(8,128)S(1)}, u32[]{:S(2)}, u32[]{:S(2)}) collective-permute-start(f32[2,6,128,128]{3,2,1,0:T(8,128)} %get-tuple-element.16), channel_id=1, source_target_pairs={{0,3},{1,0},{2,1},{3,2},{4,7},{5,4},{6,5},{7,6},{8,11},{9,8},{10,9... | collective-permute-start | bytes 2359304 | tf_op jit(solution)/shard_map/ppermute | solution.py:21
  306.3 21.8 %collective-permute-start.18 = (f32[2,6,128,128]{3,2,1,0:T(8,128)S(1)}, f32[2,6,128,128]{3,2,1,0:T(8,128)S(1)}, u32[]{:S(2)}, u32[]{:S(2)}) collective-permute-start(f32[2,6,128,128]{3,2,1,0:T(8,128)S(1)} %add.20), channel_id=1, source_target_pairs={{0,1},{1,2},{2,3},{3,0},{4,5},{5,6},{6,7},{7,4},{8,9},{9,10},{10,1... | collective-permute-start | bytes 2359304 | tf_op jit(solution)/shard_map/ppermute | solution.py:21
  306.7 35.3 %collective-permute-start.20 = (f32[2,6,128,128]{3,2,1,0:T(8,128)S(1)}, f32[2,6,128,128]{3,2,1,0:T(8,128)S(1)}, u32[]{:S(2)}, u32[]{:S(2)}) collective-permute-start(f32[2,6,128,128]{3,2,1,0:T(8,128)S(1)} %get-tuple-element.18), channel_id=1, source_target_pairs={{0,1},{1,2},{2,3},{3,0},{4,5},{5,6},{6,7},{7,4},{8,9},{9,10},{10,1... | collective-permute-start | bytes 2359304 | tf_op jit(solution)/shard_map/ppermute | solution.py:21
  308.7 33.3 %collective-permute-start.22 = (f32[2,6,128,128]{3,2,1,0:T(8,128)S(1)}, f32[2,6,128,128]{3,2,1,0:T(8,128)S(1)}, u32[]{:S(2)}, u32[]{:S(2)}) collective-permute-start(f32[2,6,128,128]{3,2,1,0:T(8,128)S(1)} %add.24), channel_id=1, source_target_pairs={{0,3},{1,0},{2,1},{3,2},{4,7},{5,4},{6,5},{7,6},{8,11},{9,8},{10,9... | collective-permute-start | bytes 2359304 | tf_op jit(solution)/shard_map/ppermute | solution.py:21
  342.3 18.2 %collective-permute-start.23 = (f32[2,6,128,128]{3,2,1,0:T(8,128)S(1)}, f32[2,6,128,128]{3,2,1,0:T(8,128)S(1)}, u32[]{:S(2)}, u32[]{:S(2)}) collective-permute-start(f32[2,6,128,128]{3,2,1,0:T(8,128)S(1)} %pad_maximum_fusion.2), channel_id=1, source_target_pairs={{0,4},{4,0},{1,5},{5,1},{2,6},{6,2},{3,7},{7,3},{8,12},{12,8},{9,1... | collective-permute-start | bytes 2359304 | tf_op jit(solution)/shard_map/ppermute | solution.py:21
  (4 other events, 64.7 us)

commit v2 on v0

v2 whole, which is shorter than its diff:
```python
import functools

import jax
import jax.numpy as jnp
from jax import lax
from jax.experimental import pallas as pl
from jax.experimental.pallas import tpu as pltpu
from jax.sharding import Mesh, PartitionSpec as P

BS = 128
ROWS = 6
KAL = 3
NB = 32
TILE = 8
def shift(value, axis, size, step):
    return lax.ppermute(value, axis, [(i, (i + step) % size) for i in range(size)])


def split(value):
    high = value.astype(jnp.bfloat16)
    low = (value - high.astype(jnp.float32)).astype(jnp.bfloat16)
    return high, low


def with_ids(blocks, *ids):
    tile = jnp.stack([jnp.pad(row.reshape(-1), (0, BS - row.size)) for row in ids])
    tile = jnp.pad(tile.astype(jnp.float32), ((0, TILE - len(ids)), (0, 0)))
    return jnp.concatenate([blocks.reshape(-1, BS), tile])


def product_kernel(spans, n_b, place, *refs):
    a_refs, refs = refs[:len(spans)], refs[len(spans):]
    b_refs, refs = refs[:n_b], refs[n_b:]
    outs, (a_v, b_v, c_v, ids_f, ids_v, table, sems) = refs[:8], refs[8:]
    xl, co, z, xh, y = (place[i] for i in range(5))
    x = xh * 2 + xl

    chunks = []
    for (step, low, high), ref in zip(spans, a_refs):
        if step not in chunks:
            chunks.append(step)
    ids, copies = [], []
    for (step, low, high), ref in zip(spans, a_refs):
        at, count = chunks.index(step) * ROWS * KAL * BS + low * KAL * BS, (high - low) * KAL * BS
        copies.append(pltpu.make_async_copy(ref.at[pl.ds(0, count)], a_v.at[pl.ds(at, count)], sems.at[11]))
        if high == ROWS:
            at = chunks.index(step) * TILE
            ids.append(pltpu.make_async_copy(ref.at[pl.ds(count, TILE)], ids_f.at[pl.ds(at, TILE)], sems.at[1]))
    back = 3 - 2 * co
    for ref, (step, core) in zip(b_refs, ((0, 0), (0, 1), (back, 0), (back, 1), (2, 0), (4 - back, 1), (4 - back, 0), (2, 1))):
        there = lax.rem(x + step, 4)
        core = lax.rem(co + core, 2)
        slot = jnp.where(there // 2 == xh, 0, 1)
        owner = slot * 4 + lax.rem(there, 2) * 2 + core
        at = pl.multiple_of(owner * NB * BS, BS)
        copies.append(pltpu.make_async_copy(ref.at[pl.ds(0, NB * BS)], b_v.at[pl.ds(at, NB * BS)], sems.at[0]))
        at = pl.multiple_of((4 + owner) * TILE, TILE)
        ids.append(pltpu.make_async_copy(ref.at[pl.ds(NB * BS, TILE)], ids_f.at[pl.ds(at, TILE)], sems.at[1]))
    for copy in ids + copies:
        copy.start()
    for copy in ids:
        copy.wait()
    ids_v[...] = ids_f[...].astype(jnp.int32)
    to_table = pltpu.make_async_copy(ids_v, table, sems.at[2])
    to_table.start()
    for copy in copies:
        copy.wait()
    to_table.wait()

    def block(ref, i):
        return ref[pl.ds(pl.multiple_of(i * BS, BS), BS), :]

    def one_row(step, ref, at, i):
        chunk = chunks.index(step)
        there = lax.rem(z + step, 8)
        c_at = (there * 2 + xh) * ROWS + i
        mine = 4 + xl * 2 + co
        kept = (table[mine * TILE + 1, c_at], table[(mine + 4) * TILE + 1, c_at])
        total = [jnp.zeros((BS, BS), jnp.float32)] * 2
        for a in range(KAL):
            k = table[chunk * TILE, i * KAL + a] // 4
            a_high, a_low = split(block(ref, at + a))
            b_high, b_low = split(jnp.concatenate((block(b_v, k), block(b_v, 4 * NB + k)), axis=1))
            product = jnp.dot(
                jnp.concatenate((a_high, a_low, a_high), axis=1),
                jnp.concatenate((b_high, b_high, b_low), axis=0),
                preferred_element_type=jnp.float32,
            )
            owner, j = k // NB, lax.rem(k, NB)
            for s in range(2):
                col = table[(4 + s * 4 + owner) * TILE, j]
                match = jnp.where(col == kept[s], 1.0, 0.0).astype(jnp.float32)
                total[s] = total[s] + match * product[:, s * BS:(s + 1) * BS]
        for s in range(2):
            c_v[chunk, s, i] = total[s]

    for (step, low, high), ref in zip(spans, a_refs):
        for i in range(low, high):
            one_row(step, a_v, (chunks.index(step) * ROWS + i) * KAL, i)
        if high == ROWS:
            layer = lax.rem(lax.rem(z + step, 8) // 2 - y + 4, 4)
            for d in range(4):
                @pl.when(layer == d)
                def _(d=d, chunk=chunks.index(step)):
                    for s in range(2):
                        pltpu.make_async_copy(c_v.at[chunk, s], outs[d * 2 + s], sems.at[3 + d * 2 + s]).start()
    for i in range(8):
        pltpu.make_async_copy(c_v.at[i // 2, i % 2], outs[i], sems.at[3 + i]).wait()


def products(place, spans, a_parts, b_parts):
    n = ROWS * KAL
    out = jax.ShapeDtypeStruct((ROWS, BS, BS), jnp.float32)
    anywhere = pl.BlockSpec(memory_space=pl.ANY)
    far_memory = pl.BlockSpec(memory_space=pl.ANY)
    return pl.pallas_call(
        functools.partial(product_kernel, spans, len(b_parts)),
        out_shape=[out] * 8,
        in_specs=[pl.BlockSpec(memory_space=pltpu.SMEM)]
        + [far_memory] * len(a_parts)
        + [far_memory] * len(b_parts),
        out_specs=[anywhere] * 8,
        scratch_shapes=[
            pltpu.VMEM((4 * n * BS, BS), jnp.float32),
            pltpu.VMEM((8 * NB * BS, BS), jnp.float32),
            pltpu.VMEM((4, 2, ROWS, BS, BS), jnp.float32),
            pltpu.VMEM((12 * TILE, BS), jnp.float32),
            pltpu.VMEM((12 * TILE, BS), jnp.int32),
            pltpu.SMEM((12 * TILE, BS), jnp.int32),
            pltpu.SemaphoreType.DMA((12,)),
        ],
        compiler_params=pltpu.CompilerParams(vmem_limit_bytes=48 * 1024 * 1024),
        cost_estimate=pl.CostEstimate(
            flops=8 * n * BS ** 3 * 6, bytes_accessed=(4 * n + 8 * NB + 8 * ROWS) * BS * BS * 4, transcendentals=0
        ),
    )(place, *a_parts, *b_parts)


def swap(value):
    return shift(value, "co", 2, 1)


def pass_on(value):
    at = lambda x, core: (x % 2) * 4 + core * 2 + x % 4 // 2
    pairs = [(at(x, core), at(x + 1 - 2 * core, core)) for x in range(4) for core in range(2)]
    return lax.ppermute(value, ("xl", "co", "xh"), pairs)


def ring_step(right, left):
    return shift(right, "z", 8, 1), shift(left, "z", 8, -1)


def gather(a, b):
    r1, l1, near, other = together(*ring_step(a, a), pass_on(b), swap(b))
    r2, l2, near_other, near_swap = together(*ring_step(r1, l1), pass_on(other), swap(near))
    r3, l3, far, near_other_swap = together(*ring_step(r2, l2), pass_on(near), swap(near_other))
    half = ROWS // 2 * KAL * BS
    r4, l4 = ring_step(r3[:half], l3[half:])
    b_parts = [b, other, near, near_other, far, near_swap, near_other_swap, swap(far)]
    return (r1, l1, r3, l3), (a, r2, l2, r4, l4), b_parts


def together(*values):
    return lax.optimization_barrier(values)


def up(value):
    return shift(value, "y", 4, 1)


def down(value):
    return shift(value, "y", 4, -1)


def per_device(a_blocks, a_inner, b_blocks, b_cols, c_cols):
    place = jnp.stack([lax.axis_index(name) for name in ("xl", "co", "z", "xh", "y")])
    odd, even, b_parts = gather(with_ids(a_blocks, a_inner), with_ids(b_blocks, b_cols, c_cols))
    p = products(place, ((7, 0, 6), (1, 0, 6), (5, 0, 6), (3, 0, 6)), odd, b_parts)
    p_far = up(p[4]), down(p[5])
    p_plain = up(p[3]), down(p[6])
    q = products(place, ((0, 0, 6), (6, 0, 6), (2, 0, 6), (4, 0, 3), (4, 3, 6)), even, b_parts)
    p2, p7, p_far, p_plain, _ = together(p[2], p[7], p_far, p_plain, q[0])
    q_far = up(q[4]), down(q[5])
    p_near = up(p2 + p_far[0]), down(p7 + p_far[1])
    q2, q3, q6, q7, q_far, p_near = together(q[2], q[3], q[6], q[7], q_far, p_near)
    p_other = shift(p[1] + p_plain[0] + p_near[1], "xh", 2, 1)
    p_mine = p[0] + p_near[0] + p_plain[1]
    q_near = up(q2 + q_far[0]), down(q7 + q_far[1])
    q_plain = up(q3), down(q6)
    q_mine = q[0] + q_near[0] + q_plain[1]
    q_other = shift(q[1] + q_plain[0] + q_near[1], "xh", 2, 1)
    own_parity = lax.axis_index("z") % 2
    own_half = lax.axis_index("xh")
    rows = []
    for parity in range(2):
        mine = jnp.where(own_parity == parity, q_mine, p_mine)
        other = jnp.where(own_parity == parity, q_other, p_other)
        rows += [jnp.where(own_half == 0, mine, other), jnp.where(own_half == 0, other, mine)]
    return jnp.stack(rows).reshape(4 * ROWS, 1, BS, BS)


def solution(mesh):
    fine = Mesh(mesh.devices.reshape(2, 2, 8, 2, 4), ("xl", "co", "z", "xh", "y"))
    return jax.shard_map(
        per_device,
        mesh=fine,
        in_specs=(
            P(("xl", "co", "z", "xh"), "y", None, None),
            P(("xl", "co", "z", "xh"), "y"),
            P(("xl", "co"), "y", ("z", "xh"), None, None),
            P(("xl", "co"), "y", ("z", "xh")),
            P(("xl", "co"), ("z", "xh")),
        ),
        out_specs=P(("xl", "co", "y"), ("z", "xh"), None, None),
        check_vma=False,
    )
```

time: 474 us -> 188 us (0.40)
  waiting for transfers between devices: 319 us -> 107 us
  matrix products: 47.5 us -> 0 us
  blocking collectives: 45.1 us -> 0 us
  local copies, waits for them, and re-layouts: 47.4 us -> 5.46 us
  starting transfers between devices: 0.08 us -> 41.4 us
  Pallas kernels: 0 us -> 26 us
  between operations: 13.8 us -> 0.19 us
  other arithmetic: 0.05 us -> 7.44 us
    all_gather x2 -> x0, waiting for transfers between devices: 252 us -> none  [the longest x1 217 us: per_device(): lax.all_gather(a_blocks, 'col', axis=0, tiled=True)]
    ppermute x0 -> x29, waiting for transfers between devices: none -> 107 us  [the longest x26 93.6 us: shift(): lax.ppermute(value, axis, [(i, (i + step) % size) for i in range(size)])]
    reduce_scatter x1 -> x0, waiting for transfers between devices: 65 us -> none  [per_device(): return lax.psum_scatter(contrib, 'layer', scatter_dimension=0, tiled=True)]
    dot_general x1 -> x0, matrix products: 47.5 us -> none  [block_rows(): jnp.einsum('raxy,rajyz->rajxz', blocks, picked, precision=HIGHEST)]
    ppermute x0 -> x29, starting transfers between devices: none -> 41.4 us  [the longest x26 36.1 us: shift(): lax.ppermute(value, axis, [(i, (i + step) % size) for i in range(size)])]
    all_gather x1 -> x0, blocking collectives: 40.8 us -> none  [per_device(): lax.all_gather(a_inner, 'col', axis=0, tiled=True)]
    gather x5 -> x0, local copies, waits for them, and re-layouts: 38.2 us -> none  [the longest x2 35.6 us: block_rows(): picked = jnp.take(b_stack, b_index, axis=0)]
    pallas_call x0 -> x2, Pallas kernels: none -> 26 us  [products(): pl.pallas_call(functools.partial(product_kernel, spans, len(b_parts)), ou...]
  transfers between devices with their start and end apart: 3 -> 29, of which waited for: 3 -> 12; matrix products, arithmetic and copies ran while one was open for 9% -> 2% of each run, Pallas kernels for 0% -> 14%
where the time goes in v2:
time: 188 us; the launch traced here: 187 us
  waiting for transfers between devices  107 us (57%)
  starting transfers between devices  41.4 us (22%)
  Pallas kernels  26 us (14%)
  other arithmetic  7.44 us (4%)
  local copies, waits for them, and re-layouts  5.46 us (3%)
    ppermute x26, waiting for transfers between devices, shift(): lax.ppermute(value, axis, [(i, (i + step) % size) for i in range(size)])  93.6 us
    ppermute x26, starting transfers between devices, shift(): lax.ppermute(value, axis, [(i, (i + step) % size) for i in range(size)])  36.1 us
    pallas_call x2, Pallas kernels, products(): pl.pallas_call(functools.partial(product_kernel, spans, len(b_parts)), ou...  26 us
    ppermute x3, waiting for transfers between devices, pass_on(): return lax.ppermute(value, ('xl', 'co', 'xh'), pairs)  13.3 us
    ppermute x3, starting transfers between devices, pass_on(): return lax.ppermute(value, ('xl', 'co', 'xh'), pairs)  5.3 us
  transfers between devices with their start and end apart: 29, of which 12 were waited for; matrix products, arithmetic and copies ran while one was open for 2% of the time, Pallas kernels for 14%

profile of v2, /device:TPU:6, one launch (start us, length us, event | category | flops | bytes accessed | tf_op | source)
XLA Modules:
  0.0 187.4 jit_solution(13689959107175179957)
XLA Ops:
  0.7 3.2 %select_maximum_fusion.refs_5_.refs_4_ = f32[4104,128]{1,0:T(8,128)} fusion(f32[2,128]{1,0:T(2,128)S(1)} %add_convert_fusion, f32[4096,128]{1,0:T(8,128)} %bitcast.26), kind=kLoop, calls=%fused_computation | loop fusion | flops 1575936 | bytes 4199424 | tf_op jit(solution)/shard_map/concatenate | solution.py:28
  3.9 2.2 %collective-permute-start.2 = (f32[4104,128]{1,0:T(8,128)}, f32[4104,128]{1,0:T(8,128)}, u32[]{:S(2)}, u32[]{:S(2)}) collective-permute-start(f32[4104,128]{1,0:T(8,128)} %select_maximum_fusion.refs_5_.refs_4_), channel_id=1, source_target_pairs={{0,128},{64,196},{128,4},{192,64},{4,132},{68,192},{132,0},{196,68... | collective-permute-start | bytes 6303752 | tf_op jit(solution)/shard_map/ppermute | solution.py:146
  6.6 4.0 %collective-permute-start.1 = (f32[2312,128]{1,0:T(8,128)S(1)}, f32[2312,128]{1,0:T(8,128)S(1)}, u32[]{:S(2)}, u32[]{:S(2)}) collective-permute-start(f32[2312,128]{1,0:T(8,128)S(1)} %select_maximum_fusion.1.refs_0_), channel_id=1, source_target_pairs={{0,56},{8,0},{16,8},{24,16},{32,24},{40,32},{48,40},{56,48},{1,57}... | collective-permute-start | bytes 3551240 | tf_op jit(solution)/shard_map/ppermute | solution.py:16
  10.7 26.6 %collective-permute-done.refs_0_ = f32[2312,128]{1,0:T(8,128)S(1)} collective-permute-done((f32[2312,128]{1,0:T(8,128)S(1)}, f32[2312,128]{1,0:T(8,128)S(1)}, u32[]{:S(2)}, u32[]{:S(2)}) %collective-permute-start) | collective-permute-done | bytes 1183776 | tf_op jit(solution)/shard_map/ppermute | solution.py:16
  37.4 1.9 %collective-permute-start.6 = (f32[4104,128]{1,0:T(8,128)}, f32[4104,128]{1,0:T(8,128)S(1)}, u32[]{:S(2)}, u32[]{:S(2)}) collective-permute-start(f32[4104,128]{1,0:T(8,128)} %collective-permute-done.3.refs_6_.refs_5_), channel_id=1, source_target_pairs={{0,128},{64,196},{128,4},{192,64},{4,132},{68,192},{132,0},{196,68... | collective-permute-start | bytes 6303752 | tf_op jit(solution)/shard_map/ppermute | solution.py:146
  39.3 3.2 %collective-permute-start.5 = (f32[2312,128]{1,0:T(8,128)S(1)}, f32[2312,128]{1,0:T(8,128)S(1)}, u32[]{:S(2)}, u32[]{:S(2)}) collective-permute-start(f32[2312,128]{1,0:T(8,128)S(1)} %collective-permute-done.1.refs_1_), channel_id=1, source_target_pairs={{0,56},{8,0},{16,8},{24,16},{32,24},{40,32},{48,40},{56,48},{1,57}... | collective-permute-start | bytes 3551240 | tf_op jit(solution)/shard_map/ppermute | solution.py:16
  43.8 24.6 %collective-permute-done.4.refs_1_ = f32[2312,128]{1,0:T(8,128)S(1)} collective-permute-done((f32[2312,128]{1,0:T(8,128)S(1)}, f32[2312,128]{1,0:T(8,128)S(1)}, u32[]{:S(2)}, u32[]{:S(2)}) %collective-permute-start.4) | collective-permute-done | bytes 1183776 | tf_op jit(solution)/shard_map/ppermute | solution.py:16
  68.4 1.4 copy-done.2
  69.8 2.4 %collective-permute-start.8 = (f32[2312,128]{1,0:T(8,128)S(1)}, f32[2312,128]{1,0:T(8,128)S(1)}, u32[]{:S(2)}, u32[]{:S(2)}) collective-permute-start(f32[2312,128]{1,0:T(8,128)S(1)} %collective-permute-done.4.refs_1_), channel_id=1, source_target_pairs={{0,8},{8,16},{16,24},{24,32},{32,40},{40,48},{48,56},{56,0},{1,9},... | collective-permute-start | bytes 3551240 | tf_op jit(solution)/shard_map/ppermute | solution.py:16
  73.1 13.3 %collective-permute-done.10.refs_9_.refs_8_ = f32[4104,128]{1,0:T(8,128)} collective-permute-done((f32[4104,128]{1,0:T(8,128)}, f32[4104,128]{1,0:T(8,128)}, u32[]{:S(2)}, u32[]{:S(2)}) %collective-permute-start.10) | collective-permute-done | bytes 2101280 | tf_op jit(solution)/shard_map/ppermute | solution.py:146
  86.4 13.1 %collective-permute-done.8.refs_2_ = f32[2312,128]{1,0:T(8,128)S(1)} collective-permute-done((f32[2312,128]{1,0:T(8,128)S(1)}, f32[2312,128]{1,0:T(8,128)S(1)}, u32[]{:S(2)}, u32[]{:S(2)}) %collective-permute-start.8) | collective-permute-done | bytes 1183776 | tf_op jit(solution)/shard_map/ppermute | solution.py:16
  100.4 1.3 copy-done.3
  102.6 1.7 collective-permute-start.12
  105.2 1.5 collective-permute-start.13
  106.8 13.1 %shard_map.56 = (f32[6,128,128]{2,1,0:T(8,128)S(1)}, f32[6,128,128]{2,1,0:T(8,128)S(1)}, f32[6,128,128]{2,1,0:T(8,128)S(1)}, f32[6,128,128]{2,1,0:T(8,128)S(1)},...) custom-call(s32[5]{0:T(128)S(1)} %stack.48.place, ...), custom_call_target="tpu_custom_call" | custom-call | flops 1811939328 | bytes 24641536 | tf_op jit(solution)/shard_map/pallas_call | solution.py:116
  119.9 1.7 collective-permute-start.17
  121.5 1.7 collective-permute-start.18
  123.6 2.9 %collective-permute-start.20 = (f32[6,128,128]{2,1,0:T(8,128)S(1)}, f32[6,128,128]{2,1,0:T(8,128)S(1)}, u32[]{:S(2)}, u32[]{:S(2)}) collective-permute-start(f32[6,128,128]{2,1,0:T(8,128)S(1)} %get-tuple-element.71), channel_id=1, source_target_pairs={{0,3},{1,0},{2,1},{3,2},{4,7},{5,4},{6,5},{7,6},{8,11},{9,8},{10,9... | collective-permute-start | bytes 1179656 | tf_op jit(solution)/shard_map/ppermute | solution.py:16
  126.4 13.0 %shard_map.55 = (f32[6,128,128]{2,1,0:T(8,128)S(1)}, f32[6,128,128]{2,1,0:T(8,128)S(1)}, f32[6,128,128]{2,1,0:T(8,128)S(1)}, f32[6,128,128]{2,1,0:T(8,128)S(1)},...) custom-call(s32[5]{0:T(128)S(1)} %stack.48.place, ...), custom_call_target="tpu_custom_call" | custom-call | flops 1811939328 | bytes 24641536 | tf_op jit(solution)/shard_map/pallas_call | solution.py:116
  139.5 3.2 %collective-permute-start.16 = (f32[6,128,128]{2,1,0:T(8,128)S(1)}, f32[6,128,128]{2,1,0:T(8,128)S(1)}, u32[]{:S(2)}, u32[]{:S(2)}) collective-permute-start(f32[6,128,128]{2,1,0:T(8,128)S(1)} %get-tuple-element.65), channel_id=1, source_target_pairs={{0,3},{1,0},{2,1},{3,2},{4,7},{5,4},{6,5},{7,6},{8,11},{9,8},{10,9... | collective-permute-start | bytes 1179656 | tf_op jit(solution)/shard_map/ppermute | solution.py:16
  142.8 1.2 collective-permute-start.22
  145.2 7.5 %collective-permute-done.15 = f32[6,128,128]{2,1,0:T(8,128)S(1)} collective-permute-done((f32[6,128,128]{2,1,0:T(8,128)S(1)}, f32[6,128,128]{2,1,0:T(8,128)S(1)}, u32[]{:S(2)}, u32[]{:S(2)}) %collective-permute-start.15) | collective-permute-done | bytes 393248 | tf_op jit(solution)/shard_map/ppermute | solution.py:16
  152.8 5.6 %collective-permute-done.22 = f32[6,128,128]{2,1,0:T(8,128)S(1)} collective-permute-done((f32[6,128,128]{2,1,0:T(8,128)S(1)}, f32[6,128,128]{2,1,0:T(8,128)S(1)}, u32[]{:S(2)}, u32[]{:S(2)}) %collective-permute-start.22) | collective-permute-done | bytes 393248 | tf_op jit(solution)/shard_map/ppermute | solution.py:16
  159.2 3.0 %collective-permute-start.26 = (f32[6,128,128]{2,1,0:T(8,128)S(1)}, f32[6,128,128]{2,1,0:T(8,128)S(1)}, u32[]{:S(2)}, u32[]{:S(2)}) collective-permute-start(f32[6,128,128]{2,1,0:T(8,128)S(1)} %add.59), channel_id=1, source_target_pairs={{0,3},{1,0},{2,1},{3,2},{4,7},{5,4},{6,5},{7,6},{8,11},{9,8},{10,9... | collective-permute-start | bytes 1179656 | tf_op jit(solution)/shard_map/ppermute | solution.py:16
  163.8 1.7 collective-permute-start.28
  165.5 3.2 %collective-permute-start.24 = (f32[6,128,128]{2,1,0:T(8,128)S(1)}, f32[6,128,128]{2,1,0:T(8,128)S(1)}, u32[]{:S(2)}, u32[]{:S(2)}) collective-permute-start(f32[6,128,128]{2,1,0:T(8,128)S(1)} %get-tuple-element.78), channel_id=1, source_target_pairs={{0,3},{1,0},{2,1},{3,2},{4,7},{5,4},{6,5},{7,6},{8,11},{9,8},{10,9... | collective-permute-start | bytes 1179656 | tf_op jit(solution)/shard_map/ppermute | solution.py:16
  168.8 2.5 %collective-permute-done.26 = f32[6,128,128]{2,1,0:T(8,128)S(1)} collective-permute-done((f32[6,128,128]{2,1,0:T(8,128)S(1)}, f32[6,128,128]{2,1,0:T(8,128)S(1)}, u32[]{:S(2)}, u32[]{:S(2)}) %collective-permute-start.26) | collective-permute-done | bytes 393248 | tf_op jit(solution)/shard_map/ppermute | solution.py:16
  171.2 4.3 %collective-permute-done.25 = f32[6,128,128]{2,1,0:T(8,128)S(1)} collective-permute-done((f32[6,128,128]{2,1,0:T(8,128)S(1)}, f32[6,128,128]{2,1,0:T(8,128)S(1)}, u32[]{:S(2)}, u32[]{:S(2)}) %collective-permute-start.25) | collective-permute-done | bytes 393248 | tf_op jit(solution)/shard_map/ppermute | solution.py:16
  176.3 1.7 collective-permute-start.27
  178.0 2.3 %collective-permute-done.23 = f32[6,128,128]{2,1,0:T(8,128)S(1)} collective-permute-done((f32[6,128,128]{2,1,0:T(8,128)}, f32[6,128,128]{2,1,0:T(8,128)S(1)}, u32[]{:S(2)}, u32[]{:S(2)}) %collective-permute-start.23) | collective-permute-done | bytes 393248 | tf_op jit(solution)/shard_map/ppermute | solution.py:16
  180.4 5.4 %collective-permute-done.27 = f32[6,128,128]{2,1,0:T(8,128)S(1)} collective-permute-done((f32[6,128,128]{2,1,0:T(8,128)}, f32[6,128,128]{2,1,0:T(8,128)S(1)}, u32[]{:S(2)}, u32[]{:S(2)}) %collective-permute-start.27) | collective-permute-done | bytes 393248 | tf_op jit(solution)/shard_map/ppermute | solution.py:16
  186.1 1.3 pad_maximum_fusion
  (67 shorter events, 11.4 us)
Async XLA Ops:
  3.9 33.4 %collective-permute-start.2 = (f32[4104,128]{1,0:T(8,128)}, f32[4104,128]{1,0:T(8,128)}, u32[]{:S(2)}, u32[]{:S(2)}) collective-permute-start(f32[4104,128]{1,0:T(8,128)} %select_maximum_fusion.refs_5_.refs_4_), channel_id=1, source_target_pairs={{0,128},{64,196},{128,4},{192,64},{4,132},{68,192},{132,0},{196,68... | collective-permute-start | bytes 6303752 | tf_op jit(solution)/shard_map/ppermute | solution.py:146
  6.1 31.2 %collective-permute-start.3 = (f32[4104,128]{1,0:T(8,128)}, f32[4104,128]{1,0:T(8,128)}, u32[]{:S(2)}, u32[]{:S(2)}) collective-permute-start(f32[4104,128]{1,0:T(8,128)} %select_maximum_fusion.refs_5_.refs_4_), channel_id=1, source_target_pairs={{0,64},{64,0},{1,65},{65,1},{2,66},{66,2},{3,67},{67,3},{4,68},{68... | collective-permute-start | bytes 6303752 | tf_op jit(solution)/shard_map/ppermute | solution.py:16
  6.4 30.9 %collective-permute-start = (f32[2312,128]{1,0:T(8,128)S(1)}, f32[2312,128]{1,0:T(8,128)S(1)}, u32[]{:S(2)}, u32[]{:S(2)}) collective-permute-start(f32[2312,128]{1,0:T(8,128)S(1)} %select_maximum_fusion.1.refs_0_), channel_id=1, source_target_pairs={{0,8},{8,16},{16,24},{24,32},{32,40},{40,48},{48,56},{56,0},{1,9},... | collective-permute-start | bytes 3551240 | tf_op jit(solution)/shard_map/ppermute | solution.py:16
  6.6 30.7 %collective-permute-start.1 = (f32[2312,128]{1,0:T(8,128)S(1)}, f32[2312,128]{1,0:T(8,128)S(1)}, u32[]{:S(2)}, u32[]{:S(2)}) collective-permute-start(f32[2312,128]{1,0:T(8,128)S(1)} %select_maximum_fusion.1.refs_0_), channel_id=1, source_target_pairs={{0,56},{8,0},{16,8},{24,16},{32,24},{40,32},{48,40},{56,48},{1,57}... | collective-permute-start | bytes 3551240 | tf_op jit(solution)/shard_map/ppermute | solution.py:16
  37.3 31.0 %collective-permute-start.7 = (f32[4104,128]{1,0:T(8,128)}, f32[4104,128]{1,0:T(8,128)}, u32[]{:S(2)}, u32[]{:S(2)}) collective-permute-start(f32[4104,128]{1,0:T(8,128)} %collective-permute-done.2.refs_7_.refs_6_), channel_id=1, source_target_pairs={{0,64},{64,0},{1,65},{65,1},{2,66},{66,2},{3,67},{67,3},{4,68},{68... | collective-permute-start | bytes 6303752 | tf_op jit(solution)/shard_map/ppermute | solution.py:16
  37.4 31.0 %collective-permute-start.6 = (f32[4104,128]{1,0:T(8,128)}, f32[4104,128]{1,0:T(8,128)S(1)}, u32[]{:S(2)}, u32[]{:S(2)}) collective-permute-start(f32[4104,128]{1,0:T(8,128)} %collective-permute-done.3.refs_6_.refs_5_), channel_id=1, source_target_pairs={{0,128},{64,196},{128,4},{192,64},{4,132},{68,192},{132,0},{196,68... | collective-permute-start | bytes 6303752 | tf_op jit(solution)/shard_map/ppermute | solution.py:146
  39.3 29.1 %collective-permute-start.4 = (f32[2312,128]{1,0:T(8,128)S(1)}, f32[2312,128]{1,0:T(8,128)S(1)}, u32[]{:S(2)}, u32[]{:S(2)}) collective-permute-start(f32[2312,128]{1,0:T(8,128)S(1)} %collective-permute-done.refs_0_), channel_id=1, source_target_pairs={{0,8},{8,16},{16,24},{24,32},{32,40},{40,48},{48,56},{56,0},{1,9},... | collective-permute-start | bytes 3551240 | tf_op jit(solution)/shard_map/ppermute | solution.py:16
  39.3 29.1 %collective-permute-start.5 = (f32[2312,128]{1,0:T(8,128)S(1)}, f32[2312,128]{1,0:T(8,128)S(1)}, u32[]{:S(2)}, u32[]{:S(2)}) collective-permute-start(f32[2312,128]{1,0:T(8,128)S(1)} %collective-permute-done.1.refs_1_), channel_id=1, source_target_pairs={{0,56},{8,0},{16,8},{24,16},{32,24},{40,32},{48,40},{56,48},{1,57}... | collective-permute-start | bytes 3551240 | tf_op jit(solution)/shard_map/ppermute | solution.py:16
  42.5 43.9 %collective-permute-start.10 = (f32[4104,128]{1,0:T(8,128)}, f32[4104,128]{1,0:T(8,128)}, u32[]{:S(2)}, u32[]{:S(2)}) collective-permute-start(f32[4104,128]{1,0:T(8,128)} %collective-permute-done.2.refs_7_.refs_6_), channel_id=1, source_target_pairs={{0,128},{64,196},{128,4},{192,64},{4,132},{68,192},{132,0},{196,68... | collective-permute-start | bytes 6303752 | tf_op jit(solution)/shard_map/ppermute | solution.py:146
  68.4 32.0 %copy-start.6 = (f32[2312,128]{1,0:T(8,128)}, f32[2312,128]{1,0:T(8,128)S(1)}, u32[]{:S(2)}) copy-start(f32[2312,128]{1,0:T(8,128)S(1)} %collective-permute-done.4.refs_1_) | copy-start | bytes 3551236
  68.4 32.0 %copy-start.7 = (f32[2312,128]{1,0:T(8,128)}, f32[2312,128]{1,0:T(8,128)S(1)}, u32[]{:S(2)}) copy-start(f32[2312,128]{1,0:T(8,128)S(1)} %collective-permute-done.5.refs_2_) | copy-start | bytes 3551236
  69.8 30.6 %collective-permute-start.11 = (f32[4104,128]{1,0:T(8,128)S(1)}, f32[4104,128]{1,0:T(8,128)S(1)}, u32[]{:S(2)}, u32[]{:S(2)}) collective-permute-start(f32[4104,128]{1,0:T(8,128)S(1)} %collective-permute-done.6.refs_8_.refs_7_), channel_id=1, source_target_pairs={{0,64},{64,0},{1,65},{65,1},{2,66},{66,2},{3,67},{67,3},{4,68},{68... | collective-permute-start | bytes 6303752 | tf_op jit(solution)/shard_map/ppermute | solution.py:16
  69.8 29.7 %collective-permute-start.8 = (f32[2312,128]{1,0:T(8,128)S(1)}, f32[2312,128]{1,0:T(8,128)S(1)}, u32[]{:S(2)}, u32[]{:S(2)}) collective-permute-start(f32[2312,128]{1,0:T(8,128)S(1)} %collective-permute-done.4.refs_1_), channel_id=1, source_target_pairs={{0,8},{8,16},{16,24},{24,32},{32,40},{40,48},{48,56},{56,0},{1,9},... | collective-permute-start | bytes 3551240 | tf_op jit(solution)/shard_map/ppermute | solution.py:16
  72.2 28.2 %collective-permute-start.9 = (f32[2312,128]{1,0:T(8,128)S(1)}, f32[2312,128]{1,0:T(8,128)S(1)}, u32[]{:S(2)}, u32[]{:S(2)}) collective-permute-start(f32[2312,128]{1,0:T(8,128)S(1)} %collective-permute-done.5.refs_2_), channel_id=1, source_target_pairs={{0,56},{8,0},{16,8},{24,16},{32,24},{40,32},{48,40},{56,48},{1,57}... | collective-permute-start | bytes 3551240 | tf_op jit(solution)/shard_map/ppermute | solution.py:16
  101.7 5.1 %collective-permute-start.14 = (f32[4104,128]{1,0:T(8,128)}, f32[4104,128]{1,0:T(8,128)}, u32[]{:S(2)}, u32[]{:S(2)}) collective-permute-start(f32[4104,128]{1,0:T(8,128)} %collective-permute-done.10.refs_9_.refs_8_), channel_id=1, source_target_pairs={{0,64},{64,0},{1,65},{65,1},{2,66},{66,2},{3,67},{67,3},{4,68},{68... | collective-permute-start | bytes 6303752 | tf_op jit(solution)/shard_map/ppermute | solution.py:16
  102.6 21.0 %collective-permute-start.12 = (f32[1152,128]{1,0:T(8,128)}, f32[1152,128]{1,0:T(8,128)}, u32[]{:S(2)}, u32[]{:S(2)}) collective-permute-start(f32[1152,128]{1,0:T(8,128)} %slice.6), channel_id=1, source_target_pairs={{0,8},{8,16},{16,24},{24,32},{32,40},{40,48},{48,56},{56,0},{1,9},... | collective-permute-start | bytes 1769480 | tf_op jit(solution)/shard_map/ppermute | solution.py:16
  105.2 21.2 %collective-permute-start.13 = (f32[1160,128]{1,0:T(8,128)}, f32[1160,128]{1,0:T(8,128)}, u32[]{:S(2)}, u32[]{:S(2)}) collective-permute-start(f32[1160,128]{1,0:T(8,128)} %slice.7), channel_id=1, source_target_pairs={{0,56},{8,0},{16,8},{24,16},{32,24},{40,32},{48,40},{56,48},{1,57}... | collective-permute-start | bytes 1781768 | tf_op jit(solution)/shard_map/ppermute | solution.py:16
  119.9 19.6 %collective-permute-start.17 = (f32[6,128,128]{2,1,0:T(8,128)S(1)}, f32[6,128,128]{2,1,0:T(8,128)S(1)}, u32[]{:S(2)}, u32[]{:S(2)}) collective-permute-start(f32[6,128,128]{2,1,0:T(8,128)S(1)} %get-tuple-element.68), channel_id=1, source_target_pairs={{0,1},{1,2},{2,3},{3,0},{4,5},{5,6},{6,7},{7,4},{8,9},{9,10},{10,1... | collective-permute-start | bytes 1179656 | tf_op jit(solution)/shard_map/ppermute | solution.py:16
  121.5 21.2 %collective-permute-start.18 = (f32[6,128,128]{2,1,0:T(8,128)S(1)}, f32[6,128,128]{2,1,0:T(8,128)S(1)}, u32[]{:S(2)}, u32[]{:S(2)}) collective-permute-start(f32[6,128,128]{2,1,0:T(8,128)S(1)} %get-tuple-element.69), channel_id=1, source_target_pairs={{0,3},{1,0},{2,1},{3,2},{4,7},{5,4},{6,5},{7,6},{8,11},{9,8},{10,9... | collective-permute-start | bytes 1179656 | tf_op jit(solution)/shard_map/ppermute | solution.py:16
  123.2 19.5 %collective-permute-start.19 = (f32[6,128,128]{2,1,0:T(8,128)S(1)}, f32[6,128,128]{2,1,0:T(8,128)S(1)}, u32[]{:S(2)}, u32[]{:S(2)}) collective-permute-start(f32[6,128,128]{2,1,0:T(8,128)S(1)} %get-tuple-element.70), channel_id=1, source_target_pairs={{0,1},{1,2},{2,3},{3,0},{4,5},{5,6},{6,7},{7,4},{8,9},{9,10},{10,1... | collective-permute-start | bytes 1179656 | tf_op jit(solution)/shard_map/ppermute | solution.py:16
  123.6 19.2 %collective-permute-start.20 = (f32[6,128,128]{2,1,0:T(8,128)S(1)}, f32[6,128,128]{2,1,0:T(8,128)S(1)}, u32[]{:S(2)}, u32[]{:S(2)}) collective-permute-start(f32[6,128,128]{2,1,0:T(8,128)S(1)} %get-tuple-element.71), channel_id=1, source_target_pairs={{0,3},{1,0},{2,1},{3,2},{4,7},{5,4},{6,5},{7,6},{8,11},{9,8},{10,9... | collective-permute-start | bytes 1179656 | tf_op jit(solution)/shard_map/ppermute | solution.py:16
  139.4 13.3 %collective-permute-start.15 = (f32[6,128,128]{2,1,0:T(8,128)S(1)}, f32[6,128,128]{2,1,0:T(8,128)S(1)}, u32[]{:S(2)}, u32[]{:S(2)}) collective-permute-start(f32[6,128,128]{2,1,0:T(8,128)S(1)} %get-tuple-element.64), channel_id=1, source_target_pairs={{0,1},{1,2},{2,3},{3,0},{4,5},{5,6},{6,7},{7,4},{8,9},{9,10},{10,1... | collective-permute-start | bytes 1179656 | tf_op jit(solution)/shard_map/ppermute | solution.py:16
  139.5 13.2 %collective-permute-start.16 = (f32[6,128,128]{2,1,0:T(8,128)S(1)}, f32[6,128,128]{2,1,0:T(8,128)S(1)}, u32[]{:S(2)}, u32[]{:S(2)}) collective-permute-start(f32[6,128,128]{2,1,0:T(8,128)S(1)} %get-tuple-element.65), channel_id=1, source_target_pairs={{0,3},{1,0},{2,1},{3,2},{4,7},{5,4},{6,5},{7,6},{8,11},{9,8},{10,9... | collective-permute-start | bytes 1179656 | tf_op jit(solution)/shard_map/ppermute | solution.py:16
  142.8 15.6 %collective-permute-start.22 = (f32[6,128,128]{2,1,0:T(8,128)S(1)}, f32[6,128,128]{2,1,0:T(8,128)S(1)}, u32[]{:S(2)}, u32[]{:S(2)}) collective-permute-start(f32[6,128,128]{2,1,0:T(8,128)S(1)} %add.52), channel_id=1, source_target_pairs={{0,3},{1,0},{2,1},{3,2},{4,7},{5,4},{6,5},{7,6},{8,11},{9,8},{10,9... | collective-permute-start | bytes 1179656 | tf_op jit(solution)/shard_map/ppermute | solution.py:16
  144.1 15.1 %collective-permute-start.21 = (f32[6,128,128]{2,1,0:T(8,128)S(1)}, f32[6,128,128]{2,1,0:T(8,128)S(1)}, u32[]{:S(2)}, u32[]{:S(2)}) collective-permute-start(f32[6,128,128]{2,1,0:T(8,128)S(1)} %add.51), channel_id=1, source_target_pairs={{0,1},{1,2},{2,3},{3,0},{4,5},{5,6},{6,7},{7,4},{8,9},{9,10},{10,1... | collective-permute-start | bytes 1179656 | tf_op jit(solution)/shard_map/ppermute | solution.py:16
  159.2 12.1 %collective-permute-start.26 = (f32[6,128,128]{2,1,0:T(8,128)S(1)}, f32[6,128,128]{2,1,0:T(8,128)S(1)}, u32[]{:S(2)}, u32[]{:S(2)}) collective-permute-start(f32[6,128,128]{2,1,0:T(8,128)S(1)} %add.59), channel_id=1, source_target_pairs={{0,3},{1,0},{2,1},{3,2},{4,7},{5,4},{6,5},{7,6},{8,11},{9,8},{10,9... | collective-permute-start | bytes 1179656 | tf_op jit(solution)/shard_map/ppermute | solution.py:16
  162.2 13.3 %collective-permute-start.25 = (f32[6,128,128]{2,1,0:T(8,128)S(1)}, f32[6,128,128]{2,1,0:T(8,128)S(1)}, u32[]{:S(2)}, u32[]{:S(2)}) collective-permute-start(f32[6,128,128]{2,1,0:T(8,128)S(1)} %get-tuple-element.83), channel_id=1, source_target_pairs={{0,1},{1,2},{2,3},{3,0},{4,5},{5,6},{6,7},{7,4},{8,9},{9,10},{10,1... | collective-permute-start | bytes 1179656 | tf_op jit(solution)/shard_map/ppermute | solution.py:16
  163.0 17.3 %collective-permute-start.23 = (f32[6,128,128]{2,1,0:T(8,128)}, f32[6,128,128]{2,1,0:T(8,128)S(1)}, u32[]{:S(2)}, u32[]{:S(2)}) collective-permute-start(f32[6,128,128]{2,1,0:T(8,128)} %add.53), channel_id=1, source_target_pairs={{0,1},{1,2},{2,3},{3,0},{4,5},{5,6},{6,7},{7,4},{8,9},{9,10},{10,1... | collective-permute-start | bytes 1179656 | tf_op jit(solution)/shard_map/ppermute | solution.py:16
  163.0 22.8 %copy-start.1 = (f32[6,128,128]{2,1,0:T(8,128)S(1)}, f32[6,128,128]{2,1,0:T(8,128)}, u32[]{:S(2)}) copy-start(f32[6,128,128]{2,1,0:T(8,128)} %copy-done) | copy-start | bytes 1179652
  163.8 16.5 %collective-permute-start.28 = (f32[6,128,128]{2,1,0:T(8,128)}, f32[6,128,128]{2,1,0:T(8,128)S(1)}, u32[]{:S(2)}, u32[]{:S(2)}) collective-permute-start(f32[6,128,128]{2,1,0:T(8,128)} %add_add_fusion), channel_id=1, source_target_pairs={{0,4},{4,0},{1,5},{5,1},{2,6},{6,2},{3,7},{7,3},{8,12},{12,8},{9,1... | collective-permute-start | bytes 1179656 | tf_op jit(solution)/shard_map/ppermute | solution.py:16
  165.5 14.8 %collective-permute-start.24 = (f32[6,128,128]{2,1,0:T(8,128)S(1)}, f32[6,128,128]{2,1,0:T(8,128)S(1)}, u32[]{:S(2)}, u32[]{:S(2)}) collective-permute-start(f32[6,128,128]{2,1,0:T(8,128)S(1)} %get-tuple-element.78), channel_id=1, source_target_pairs={{0,3},{1,0},{2,1},{3,2},{4,7},{5,4},{6,5},{7,6},{8,11},{9,8},{10,9... | collective-permute-start | bytes 1179656 | tf_op jit(solution)/shard_map/ppermute | solution.py:16
  176.3 9.5 %collective-permute-start.27 = (f32[6,128,128]{2,1,0:T(8,128)}, f32[6,128,128]{2,1,0:T(8,128)S(1)}, u32[]{:S(2)}, u32[]{:S(2)}) collective-permute-start(f32[6,128,128]{2,1,0:T(8,128)} %add_add_fusion.1), channel_id=1, source_target_pairs={{0,4},{4,0},{1,5},{5,1},{2,6},{6,2},{3,7},{7,3},{8,12},{12,8},{9,1... | collective-permute-start | bytes 1179656 | tf_op jit(solution)/shard_map/ppermute | solution.py:16
  (7 other events, 43.0 us)

commit v3 on v2

v3 whole, which is shorter than its diff:
```python
import functools

import jax
import jax.numpy as jnp
from jax import lax
from jax.experimental import pallas as pl
from jax.experimental.pallas import tpu as pltpu
from jax.sharding import Mesh, PartitionSpec as P

BS = 128
ROWS = 6
KAL = 3
NB = 32
TILE = 8
PAIRED = {(2, 0): (0, 0), (1, 1): (0, ROWS), (2, 1): (1, 0), (3, 0): (1, ROWS), (0, 0): (2, 0), (0, 1): (3, 0), (1, 0): (4, 0), (3, 1): (5, 0)}
SINGLE = {(d, s): (2 * d + s, 0) for d in range(4) for s in range(2)}


def shift(value, axis, size, step):
    return lax.ppermute(value, axis, [(i, (i + step) % size) for i in range(size)])


def split(value):
    high = value.astype(jnp.bfloat16)
    low = (value - high.astype(jnp.float32)).astype(jnp.bfloat16)
    return high, low


def with_ids(blocks, *ids):
    tile = jnp.stack([jnp.pad(row.reshape(-1), (0, BS - row.size)) for row in ids])
    tile = jnp.pad(tile.astype(jnp.float32), ((0, TILE - len(ids)), (0, 0)))
    return jnp.concatenate([blocks.reshape(-1, BS), tile])


def product_kernel(spans, routes, n_b, place, *refs):
    a_refs, refs = refs[:4], refs[4:]
    b_refs, refs = refs[:n_b], refs[n_b:]
    outs, (a_v, b_v, c_v, ids_f, ids_v, table, sems) = refs[:-7], refs[-7:]
    xl, co, z, xh, y = (place[i] for i in range(5))
    x = xh * 2 + xl

    ids, copies, chunks = [], [], []
    size = ROWS * KAL * BS
    for chunk, ref in enumerate(a_refs):
        chunks.append(pltpu.make_async_copy(ref.at[pl.ds(0, size)], a_v.at[pl.ds(chunk * size, size)], sems.at[11 + chunk]))
        ids.append(pltpu.make_async_copy(ref.at[pl.ds(size, TILE)], ids_f.at[pl.ds(chunk * TILE, TILE)], sems.at[1]))
    back = 3 - 2 * co
    for ref, (step, core) in zip(b_refs, ((0, 0), (0, 1), (back, 0), (back, 1), (2, 0), (4 - back, 1), (4 - back, 0), (2, 1))):
        there = lax.rem(x + step, 4)
        core = lax.rem(co + core, 2)
        slot = jnp.where(there // 2 == xh, 0, 1)
        owner = slot * 4 + lax.rem(there, 2) * 2 + core
        at = pl.multiple_of(owner * NB * BS, BS)
        copies.append(pltpu.make_async_copy(ref.at[pl.ds(0, NB * BS)], b_v.at[pl.ds(at, NB * BS)], sems.at[0]))
        at = pl.multiple_of((4 + owner) * TILE, TILE)
        ids.append(pltpu.make_async_copy(ref.at[pl.ds(NB * BS, TILE)], ids_f.at[pl.ds(at, TILE)], sems.at[1]))
    for copy in ids + copies + chunks:
        copy.start()
    for copy in ids:
        copy.wait()
    ids_v[...] = ids_f[...].astype(jnp.int32)
    to_table = pltpu.make_async_copy(ids_v, table, sems.at[2])
    to_table.start()
    for copy in copies:
        copy.wait()
    to_table.wait()

    def block(ref, i):
        return ref[pl.ds(pl.multiple_of(i * BS, BS), BS), :]

    def one_row(chunk, there, i):
        c_at = (there * 2 + xh) * ROWS + i
        mine = 4 + xl * 2 + co
        kept = (table[mine * TILE + 1, c_at], table[(mine + 4) * TILE + 1, c_at])
        total = [jnp.zeros((BS, BS), jnp.float32)] * 2
        for a in range(KAL):
            k = table[chunk * TILE, i * KAL + a] // 4
            a_high, a_low = split(block(a_v, (chunk * ROWS + i) * KAL + a))
            b_high, b_low = split(jnp.concatenate((block(b_v, k), block(b_v, 4 * NB + k)), axis=1))
            product = jnp.dot(
                jnp.concatenate((a_high, a_low, a_high), axis=1),
                jnp.concatenate((b_high, b_high, b_low), axis=0),
                preferred_element_type=jnp.float32,
            )
            owner, j = k // NB, lax.rem(k, NB)
            for s in range(2):
                col = table[(4 + s * 4 + owner) * TILE, j]
                match = jnp.where(col == kept[s], 1.0, 0.0).astype(jnp.float32)
                total[s] = total[s] + match * product[:, s * BS:(s + 1) * BS]
        for s in range(2):
            c_v[chunk, s, i] = total[s]

    def place_of(d, s):
        out, at = routes[d, s]
        return outs[out].at[pl.ds(at, ROWS)]

    for chunk, (distance, kept_core) in enumerate(spans):
        there = lax.rem(z + jnp.where(co == kept_core, 8 - distance, distance), 8)
        chunks[chunk].wait()
        for i in range(ROWS):
            one_row(chunk, there, i)
        layer = lax.rem(there // 2 - y + 4, 4)
        for d in range(4):
            @pl.when(layer == d)
            def _(d=d, chunk=chunk):
                for s in range(2):
                    pltpu.make_async_copy(c_v.at[chunk, s], place_of(d, s), sems.at[3 + d * 2 + s]).start()
    for i in range(8):
        pltpu.make_async_copy(c_v.at[i // 2, i % 2], place_of(i // 2, i % 2), sems.at[3 + i]).wait()


def products(place, spans, routes, a_parts, b_parts):
    n = ROWS * KAL
    places = list(routes.values())
    out_rows = [ROWS + max(at for out, at in places if out == i) for i in range(1 + max(places)[0])]
    anywhere = pl.BlockSpec(memory_space=pl.ANY)
    far_memory = pl.BlockSpec(memory_space=pl.ANY)
    return pl.pallas_call(
        functools.partial(product_kernel, spans, routes, len(b_parts)),
        out_shape=[jax.ShapeDtypeStruct((rows, BS, BS), jnp.float32) for rows in out_rows],
        in_specs=[pl.BlockSpec(memory_space=pltpu.SMEM)]
        + [far_memory] * len(a_parts)
        + [far_memory] * len(b_parts),
        out_specs=[anywhere] * len(out_rows),
        scratch_shapes=[
            pltpu.VMEM((4 * n * BS, BS), jnp.float32),
            pltpu.VMEM((8 * NB * BS, BS), jnp.float32),
            pltpu.VMEM((4, 2, ROWS, BS, BS), jnp.float32),
            pltpu.VMEM((12 * TILE, BS), jnp.float32),
            pltpu.VMEM((12 * TILE, BS), jnp.int32),
            pltpu.SMEM((12 * TILE, BS), jnp.int32),
            pltpu.SemaphoreType.DMA((15,)),
        ],
        compiler_params=pltpu.CompilerParams(vmem_limit_bytes=58 * 1024 * 1024),
        cost_estimate=pl.CostEstimate(
            flops=8 * n * BS ** 3 * 6, bytes_accessed=(4 * n + 8 * NB + 8 * ROWS) * BS * BS * 4, transcendentals=0
        ),
    )(place, *a_parts, *b_parts)


def swap(value):
    return shift(value, "co", 2, 1)


def pass_on(value):
    at = lambda x, core: (x % 2) * 4 + core * 2 + x % 4 // 2
    pairs = [(at(x, core), at(x + 1 - 2 * core, core)) for x in range(4) for core in range(2)]
    return lax.ppermute(value, ("xl", "co", "xh"), pairs)


def pass_z(value):
    pairs = [(core * 8 + z, core * 8 + (z + 1 - 2 * core) % 8) for z in range(8) for core in range(2)]
    return lax.ppermute(value, ("co", "z"), pairs)


def gather(a, b):
    own, other = [a], [swap(a)]
    for _ in range(2):
        own.append(pass_z(own[-1]))
        other.append(pass_z(other[-1]))
    b_other = swap(b)
    near, near_other, own[2], other[2] = together(pass_on(b), pass_on(b_other), own[2], other[2])
    far = pass_on(near)
    own.append(pass_z(own[2]))
    other.append(pass_z(other[2]))
    last = pass_z(own[3])
    near, near_other, own[3] = together(near, near_other, own[3])
    far, own[3] = together(far, own[3])
    odd = (own[1], swap(other[1]), own[3], swap(other[3]))
    even = (a, own[2], swap(other[2]), last)
    return odd, even, [b, b_other, near, near_other, far, swap(near), swap(near_other), swap(far)]


def together(*values):
    return lax.optimization_barrier(values)


def up(value):
    return shift(value, "y", 4, 1)


def down(value):
    return shift(value, "y", 4, -1)


def per_device(a_blocks, a_inner, b_blocks, b_cols, c_cols):
    place = jnp.stack([lax.axis_index(name) for name in ("xl", "co", "z", "xh", "y")])
    odd, even, b_parts = gather(with_ids(a_blocks, a_inner), with_ids(b_blocks, b_cols, c_cols))
    p = products(place, ((1, 0), (1, 1), (3, 0), (3, 1)), PAIRED, odd, b_parts)
    p_up, p_down, p_0, p_1, p_near_0, p_near_1 = p
    p_up, p_down = up(p_up), down(p_down)
    q = products(place, ((0, 0), (2, 0), (2, 1), (4, 0)), SINGLE, even, b_parts)
    p_up, p_down, _ = together(p_up, p_down, q[0])
    p_near_0, p_near_1 = up(p_near_0 + p_up[:ROWS]), down(p_near_1 + p_down[:ROWS])
    q_far_1, q_plain_1, q_far_0 = down(q[5]), up(q[3]), up(q[4])
    q7, q6, q_far_1, p_near_0, p_near_1 = together(q[7], q[6], q_far_1, p_near_0, p_near_1)
    p_other = shift(p_1 + p_up[ROWS:] + p_near_1, "xh", 2, 1)
    p_mine = p_0 + p_near_0 + p_down[ROWS:]
    q_near_1, q_plain_0 = down(q7 + q_far_1), down(q6)
    q_other = shift(q[1] + q_plain_1 + q_near_1, "xh", 2, 1)
    q_near_0 = up(q[2] + q_far_0)
    q_mine = q[0] + q_near_0 + q_plain_0
    own_parity = lax.axis_index("z") % 2
    own_half = lax.axis_index("xh")
    rows = []
    for parity in range(2):
        mine = jnp.where(own_parity == parity, q_mine, p_mine)
        other = jnp.where(own_parity == parity, q_other, p_other)
        rows += [jnp.where(own_half == 0, mine, other), jnp.where(own_half == 0, other, mine)]
    return jnp.stack(rows).reshape(4 * ROWS, 1, BS, BS)


def solution(mesh):
    fine = Mesh(mesh.devices.reshape(2, 2, 8, 2, 4), ("xl", "co", "z", "xh", "y"))
    return jax.shard_map(
        per_device,
        mesh=fine,
        in_specs=(
            P(("xl", "co", "z", "xh"), "y", None, None),
            P(("xl", "co", "z", "xh"), "y"),
            P(("xl", "co"), "y", ("z", "xh"), None, None),
            P(("xl", "co"), "y", ("z", "xh")),
            P(("xl", "co"), ("z", "xh")),
        ),
        out_specs=P(("xl", "co", "y"), ("z", "xh"), None, None),
        check_vma=False,
    )
```

time: 188 us -> 180 us (0.957)
  starting transfers between devices: 41.4 us -> 35.3 us
  waiting for transfers between devices: 107 us -> 112 us
  local copies, waits for them, and re-layouts: 5.46 us -> 1.57 us
  Pallas kernels: 26 us -> 22.3 us
    ppermute x0 -> x7, waiting for transfers between devices: none -> 73.5 us  [pass_z(): return lax.ppermute(value, ('co', 'z'), pairs)]
    ppermute x26 -> x20, waiting for transfers between devices: 93.6 us -> 30.6 us  [shift(): lax.ppermute(value, axis, [(i, (i + step) % size) for i in range(size)])]
    ppermute x26 -> x20, starting transfers between devices: 36.1 us -> 27.9 us  [shift(): lax.ppermute(value, axis, [(i, (i + step) % size) for i in range(size)])]
    ppermute x3, waiting for transfers between devices: 13.3 us -> 7.84 us  [pass_on(): return lax.ppermute(value, ('xl', 'co', 'xh'), pairs)]
    ppermute x0 -> x7, starting transfers between devices: none -> 4.97 us  [pass_z(): return lax.ppermute(value, ('co', 'z'), pairs)]
    pallas_call x2, Pallas kernels: 26 us -> 22.3 us  [products(): pl.pallas_call(functools.partial(product_kernel, spans, routes, len(b_par...]
    ppermute x3, starting transfers between devices: 5.3 us -> 2.45 us  [pass_on(): return lax.ppermute(value, ('xl', 'co', 'xh'), pairs)]
    unnamed x21 -> x31, local copies, waits for them, and re-layouts: 2.89 us -> 0.15 us
  transfers between devices with their start and end apart: 29 -> 30, of which waited for: 12 -> 17; matrix products, arithmetic and copies ran while one was open for 2% -> 3% of each run, Pallas kernels for 14% -> 12%
where the time goes in v3:
time: 180 us; the launch traced here: 179 us
  waiting for transfers between devices  112 us (62%)
  starting transfers between devices  35.3 us (20%)
  Pallas kernels  22.3 us (12%)
  other arithmetic  7.71 us (4%)
    ppermute x7, waiting for transfers between devices, pass_z(): return lax.ppermute(value, ('co', 'z'), pairs)  73.5 us
    ppermute x20, waiting for transfers between devices, shift(): lax.ppermute(value, axis, [(i, (i + step) % size) for i in range(size)])  30.6 us
    ppermute x20, starting transfers between devices, shift(): lax.ppermute(value, axis, [(i, (i + step) % size) for i in range(size)])  27.9 us
    pallas_call x2, Pallas kernels, products(): pl.pallas_call(functools.partial(product_kernel, spans, routes, len(b_par...  22.3 us
    ppermute x3, waiting for transfers between devices, pass_on(): return lax.ppermute(value, ('xl', 'co', 'xh'), pairs)  7.84 us
    ppermute x7, starting transfers between devices, pass_z(): return lax.ppermute(value, ('co', 'z'), pairs)  4.97 us
  transfers between devices with their start and end apart: 30, of which 17 were waited for; matrix products, arithmetic and copies ran while one was open for 3% of the time, Pallas kernels for 12%

profile of v3, /device:TPU:6, one launch (start us, length us, event | category | flops | bytes accessed | tf_op | source)
XLA Modules:
  0.0 179.1 jit_solution(2487204139065136337)
XLA Ops:
  0.7 1.7 select_maximum_fusion.refs_4_
  2.7 1.8 %select_maximum_fusion.1.refs_0_ = f32[2312,128]{1,0:T(8,128)S(1)} fusion(f32[1,128]{1,0:T(1,128)S(1)} %convert_bitcast_fusion, f32[2304,128]{1,0:T(8,128)} %bitcast.27), kind=kLoop, calls=%fused_computation.3 | loop fusion | flops 887808 | bytes 2363904 | tf_op jit(solution)/shard_map/concatenate | solution.py:32
  4.7 2.0 %collective-permute-start.3 = (f32[2312,128]{1,0:T(8,128)S(1)}, f32[2312,128]{1,0:T(8,128)S(1)}, u32[]{:S(2)}, u32[]{:S(2)}) collective-permute-start(f32[2312,128]{1,0:T(8,128)S(1)} %select_maximum_fusion.1.refs_0_), channel_id=1, source_target_pairs={{0,8},{64,120},{8,16},{72,64},{16,24},{80,72},{24,32},{88,80},{32,... | collective-permute-start | bytes 3551240 | tf_op jit(solution)/shard_map/ppermute | solution.py:153
  6.6 1.7 collective-permute-done.5
  8.4 1.9 %collective-permute-start.6 = (f32[2312,128]{1,0:T(8,128)S(1)}, f32[2312,128]{1,0:T(8,128)S(1)}, u32[]{:S(2)}, u32[]{:S(2)}) collective-permute-start(f32[2312,128]{1,0:T(8,128)S(1)} %collective-permute-done.5), channel_id=1, source_target_pairs={{0,8},{64,120},{8,16},{72,64},{16,24},{80,72},{24,32},{88,80},{32,... | collective-permute-start | bytes 3551240 | tf_op jit(solution)/shard_map/ppermute | solution.py:153
  10.8 1.5 collective-permute-start.2
  12.3 12.5 %collective-permute-done.3.refs_0_ = f32[2312,128]{1,0:T(8,128)S(1)} collective-permute-done((f32[2312,128]{1,0:T(8,128)S(1)}, f32[2312,128]{1,0:T(8,128)S(1)}, u32[]{:S(2)}, u32[]{:S(2)}) %collective-permute-start.3) | collective-permute-done | bytes 1183776 | tf_op jit(solution)/shard_map/ppermute | solution.py:153
  24.8 12.7 %collective-permute-done.6 = f32[2312,128]{1,0:T(8,128)S(1)} collective-permute-done((f32[2312,128]{1,0:T(8,128)S(1)}, f32[2312,128]{1,0:T(8,128)S(1)}, u32[]{:S(2)}, u32[]{:S(2)}) %collective-permute-start.6) | collective-permute-done | bytes 1183776 | tf_op jit(solution)/shard_map/ppermute | solution.py:153
  37.5 12.7 %collective-permute-done.4.refs_1_ = f32[2312,128]{1,0:T(8,128)S(1)} collective-permute-done((f32[2312,128]{1,0:T(8,128)S(1)}, f32[2312,128]{1,0:T(8,128)S(1)}, u32[]{:S(2)}, u32[]{:S(2)}) %collective-permute-start.4) | collective-permute-done | bytes 1183776 | tf_op jit(solution)/shard_map/ppermute | solution.py:153
  50.2 12.8 %collective-permute-done.7 = f32[2312,128]{1,0:T(8,128)} collective-permute-done((f32[2312,128]{1,0:T(8,128)S(1)}, f32[2312,128]{1,0:T(8,128)}, u32[]{:S(2)}, u32[]{:S(2)}) %collective-permute-start.7) | collective-permute-done | bytes 1183776 | tf_op jit(solution)/shard_map/ppermute | solution.py:153
  64.5 16.5 %collective-permute-done.9.refs_2_ = f32[2312,128]{1,0:T(8,128)} collective-permute-done((f32[2312,128]{1,0:T(8,128)S(1)}, f32[2312,128]{1,0:T(8,128)}, u32[]{:S(2)}, u32[]{:S(2)}) %collective-permute-start.9) | collective-permute-done | bytes 1183776 | tf_op jit(solution)/shard_map/ppermute | solution.py:153
  81.5 7.8 %collective-permute-done.11.refs_8_ = f32[4104,128]{1,0:T(8,128)} collective-permute-done((f32[4104,128]{1,0:T(8,128)}, f32[4104,128]{1,0:T(8,128)}, u32[]{:S(2)}, u32[]{:S(2)}) %collective-permute-start.11) | collective-permute-done | bytes 2101280 | tf_op jit(solution)/shard_map/ppermute | solution.py:148
  89.9 3.7 %collective-permute-done.19 = f32[2312,128]{1,0:T(8,128)S(1)} collective-permute-done((f32[2312,128]{1,0:T(8,128)}, f32[2312,128]{1,0:T(8,128)S(1)}, u32[]{:S(2)}, u32[]{:S(2)}) %collective-permute-start.19) | collective-permute-done | bytes 1183776 | tf_op jit(solution)/shard_map/ppermute | solution.py:153
  93.6 1.8 collective-permute-done.18.refs_1_
  95.7 1.3 collective-permute-done.20.refs_3_
  97.7 11.2 %shard_map.56 = (f32[12,128,128]{2,1,0:T(8,128)}, f32[12,128,128]{2,1,0:T(8,128)}, f32[6,128,128]{2,1,0:T(8,128)}, f32[6,128,128]{2,1,0:T(8,128)}, f32[6,128,128]{2,1,0:T(8,128)}, /*index=5*/f32[6,128,128]{2,1,0:T(8,128)}) custom-call(s32[5]{0:T(128)} %stack.48.place, f32[2312,128]{1,0:T(8,128)} %copy-done.3, f32[2312,128]{1,0:T(8,128)} %collective-permute-done.18.refs_1_, ...), custom_call_target="tpu_custom_call" | custom-call | flops 1811939328 | bytes 24641536 | tf_op jit(solution)/shard_map/pallas_call | solution.py:118
  108.9 1.7 collective-permute-start.21
  110.6 1.7 collective-permute-start.22
  112.2 2.6 %collective-permute-done.10.refs_3_ = f32[2312,128]{1,0:T(8,128)} collective-permute-done((f32[2312,128]{1,0:T(8,128)}, f32[2312,128]{1,0:T(8,128)}, u32[]{:S(2)}, u32[]{:S(2)}) %collective-permute-start.10) | collective-permute-done | bytes 1183776 | tf_op jit(solution)/shard_map/ppermute | solution.py:153
  114.8 11.2 %shard_map.55 = (f32[6,128,128]{2,1,0:T(8,128)}, f32[6,128,128]{2,1,0:T(8,128)}, f32[6,128,128]{2,1,0:T(8,128)}, f32[6,128,128]{2,1,0:T(8,128)}, f32[6,128,128]{...) custom-call(s32[5]{0:T(128)} %stack.48.place, f32[2312,128]{1,0:T(8,128)} %copy-done.1, ...), custom_call_target="tpu_custom_call" | custom-call | flops 1811939328 | bytes 24641536 | tf_op jit(solution)/shard_map/pallas_call | solution.py:118
  126.0 3.1 %collective-permute-start.17 = (f32[6,128,128]{2,1,0:T(8,128)}, f32[6,128,128]{2,1,0:T(8,128)S(1)}, u32[]{:S(2)}, u32[]{:S(2)}) collective-permute-start(f32[6,128,128]{2,1,0:T(8,128)} %get-tuple-element.48), channel_id=1, source_target_pairs={{0,3},{1,0},{2,1},{3,2},{4,7},{5,4},{6,5},{7,6},{8,11},{9,8},{10,9... | collective-permute-start | bytes 1179656 | tf_op jit(solution)/shard_map/ppermute | solution.py:20
  129.8 2.8 %collective-permute-start.24 = (f32[6,128,128]{2,1,0:T(8,128)S(1)}, f32[6,128,128]{2,1,0:T(8,128)S(1)}, u32[]{:S(2)}, u32[]{:S(2)}) collective-permute-start(f32[6,128,128]{2,1,0:T(8,128)S(1)} %slice_add_fusion.1), channel_id=1, source_target_pairs={{0,3},{1,0},{2,1},{3,2},{4,7},{5,4},{6,5},{7,6},{8,11},{9,8},{10,9... | collective-permute-start | bytes 1179656 | tf_op jit(solution)/shard_map/ppermute | solution.py:20
  134.8 4.2 %collective-permute-done.17 = f32[6,128,128]{2,1,0:T(8,128)S(1)} collective-permute-done((f32[6,128,128]{2,1,0:T(8,128)}, f32[6,128,128]{2,1,0:T(8,128)S(1)}, u32[]{:S(2)}, u32[]{:S(2)}) %collective-permute-start.17) | collective-permute-done | bytes 393248 | tf_op jit(solution)/shard_map/ppermute | solution.py:20
  139.0 8.3 %collective-permute-done.24 = f32[6,128,128]{2,1,0:T(8,128)S(1)} collective-permute-done((f32[6,128,128]{2,1,0:T(8,128)S(1)}, f32[6,128,128]{2,1,0:T(8,128)S(1)}, u32[]{:S(2)}, u32[]{:S(2)}) %collective-permute-start.24) | collective-permute-done | bytes 393248 | tf_op jit(solution)/shard_map/ppermute | solution.py:20
  147.3 3.8 %collective-permute-start.27 = (f32[6,128,128]{2,1,0:T(8,128)S(1)}, f32[6,128,128]{2,1,0:T(8,128)S(1)}, u32[]{:S(2)}, u32[]{:S(2)}) collective-permute-start(f32[6,128,128]{2,1,0:T(8,128)S(1)} %add.59), channel_id=1, source_target_pairs={{0,3},{1,0},{2,1},{3,2},{4,7},{5,4},{6,5},{7,6},{8,11},{9,8},{10,9... | collective-permute-start | bytes 1179656 | tf_op jit(solution)/shard_map/ppermute | solution.py:20
  151.1 2.9 %collective-permute-done.15 = f32[6,128,128]{2,1,0:T(8,128)S(1)} collective-permute-done((f32[6,128,128]{2,1,0:T(8,128)S(1)}, f32[6,128,128]{2,1,0:T(8,128)S(1)}, u32[]{:S(2)}, u32[]{:S(2)}) %collective-permute-start.15) | collective-permute-done | bytes 393248 | tf_op jit(solution)/shard_map/ppermute | solution.py:20
  155.6 4.4 %collective-permute-start.29 = (f32[6,128,128]{2,1,0:T(8,128)}, f32[6,128,128]{2,1,0:T(8,128)S(1)}, u32[]{:S(2)}, u32[]{:S(2)}) collective-permute-start(f32[6,128,128]{2,1,0:T(8,128)} %add_add_fusion), channel_id=1, source_target_pairs={{0,4},{4,0},{1,5},{5,1},{2,6},{6,2},{3,7},{7,3},{8,12},{12,8},{9,1... | collective-permute-start | bytes 1179656 | tf_op jit(solution)/shard_map/ppermute | solution.py:20
  160.0 3.2 %collective-permute-start.25 = (f32[6,128,128]{2,1,0:T(8,128)}, f32[6,128,128]{2,1,0:T(8,128)S(1)}, u32[]{:S(2)}, u32[]{:S(2)}) collective-permute-start(f32[6,128,128]{2,1,0:T(8,128)} %get-tuple-element.56), channel_id=1, source_target_pairs={{0,3},{1,0},{2,1},{3,2},{4,7},{5,4},{6,5},{7,6},{8,11},{9,8},{10,9... | collective-permute-start | bytes 1179656 | tf_op jit(solution)/shard_map/ppermute | solution.py:20
  164.0 3.6 %collective-permute-start.28 = (f32[6,128,128]{2,1,0:T(8,128)}, f32[6,128,128]{2,1,0:T(8,128)S(1)}, u32[]{:S(2)}, u32[]{:S(2)}) collective-permute-start(f32[6,128,128]{2,1,0:T(8,128)} %add_add_fusion.1), channel_id=1, source_target_pairs={{0,4},{4,0},{1,5},{5,1},{2,6},{6,2},{3,7},{7,3},{8,12},{12,8},{9,1... | collective-permute-start | bytes 1179656 | tf_op jit(solution)/shard_map/ppermute | solution.py:20
  167.6 3.2 %collective-permute-done.16 = f32[6,128,128]{2,1,0:T(8,128)S(1)} collective-permute-done((f32[6,128,128]{2,1,0:T(8,128)}, f32[6,128,128]{2,1,0:T(8,128)S(1)}, u32[]{:S(2)}, u32[]{:S(2)}) %collective-permute-start.16) | collective-permute-done | bytes 393248 | tf_op jit(solution)/shard_map/ppermute | solution.py:20
  170.9 6.6 %collective-permute-done.28 = f32[6,128,128]{2,1,0:T(8,128)S(1)} collective-permute-done((f32[6,128,128]{2,1,0:T(8,128)}, f32[6,128,128]{2,1,0:T(8,128)S(1)}, u32[]{:S(2)}, u32[]{:S(2)}) %collective-permute-start.28) | collective-permute-done | bytes 393248 | tf_op jit(solution)/shard_map/ppermute | solution.py:20
  177.8 1.3 pad_maximum_fusion
  (77 shorter events, 11.0 us)
Async XLA Ops:
  2.4 95.3 %copy-start = (f32[4104,128]{1,0:T(8,128)}, f32[4104,128]{1,0:T(8,128)S(1)}, u32[]{:S(2)}) copy-start(f32[4104,128]{1,0:T(8,128)S(1)} %select_maximum_fusion.refs_4_) | copy-start | bytes 6303748
  2.4 8.3 %collective-permute-start.1 = (f32[4104,128]{1,0:T(8,128)S(1)}, f32[4104,128]{1,0:T(8,128)}, u32[]{:S(2)}, u32[]{:S(2)}) collective-permute-start(f32[4104,128]{1,0:T(8,128)S(1)} %select_maximum_fusion.refs_4_), channel_id=1, source_target_pairs={{0,64},{64,0},{1,65},{65,1},{2,66},{66,2},{3,67},{67,3},{4,68},{68... | collective-permute-start | bytes 6303752 | tf_op jit(solution)/shard_map/ppermute | solution.py:20
  4.5 104.4 %copy-start.1 = (f32[2312,128]{1,0:T(8,128)}, f32[2312,128]{1,0:T(8,128)S(1)}, u32[]{:S(2)}) copy-start(f32[2312,128]{1,0:T(8,128)S(1)} %select_maximum_fusion.1.refs_0_) | copy-start | bytes 3551236
  4.5 3.8 %collective-permute-start.5 = (f32[2312,128]{1,0:T(8,128)S(1)}, f32[2312,128]{1,0:T(8,128)S(1)}, u32[]{:S(2)}, u32[]{:S(2)}) collective-permute-start(f32[2312,128]{1,0:T(8,128)S(1)} %select_maximum_fusion.1.refs_0_), channel_id=1, source_target_pairs={{0,64},{64,0},{1,65},{65,1},{2,66},{66,2},{3,67},{67,3},{4,68},{68... | collective-permute-start | bytes 3551240 | tf_op jit(solution)/shard_map/ppermute | solution.py:20
  4.7 20.1 %collective-permute-start.3 = (f32[2312,128]{1,0:T(8,128)S(1)}, f32[2312,128]{1,0:T(8,128)S(1)}, u32[]{:S(2)}, u32[]{:S(2)}) collective-permute-start(f32[2312,128]{1,0:T(8,128)S(1)} %select_maximum_fusion.1.refs_0_), channel_id=1, source_target_pairs={{0,8},{64,120},{8,16},{72,64},{16,24},{80,72},{24,32},{88,80},{32,... | collective-permute-start | bytes 3551240 | tf_op jit(solution)/shard_map/ppermute | solution.py:153
  8.4 29.1 %collective-permute-start.6 = (f32[2312,128]{1,0:T(8,128)S(1)}, f32[2312,128]{1,0:T(8,128)S(1)}, u32[]{:S(2)}, u32[]{:S(2)}) collective-permute-start(f32[2312,128]{1,0:T(8,128)S(1)} %collective-permute-done.5), channel_id=1, source_target_pairs={{0,8},{64,120},{8,16},{72,64},{16,24},{80,72},{24,32},{88,80},{32,... | collective-permute-start | bytes 3551240 | tf_op jit(solution)/shard_map/ppermute | solution.py:153
  10.3 27.2 %collective-permute-start = (f32[4104,128]{1,0:T(8,128)S(1)}, f32[4104,128]{1,0:T(8,128)}, u32[]{:S(2)}, u32[]{:S(2)}) collective-permute-start(f32[4104,128]{1,0:T(8,128)S(1)} %select_maximum_fusion.refs_4_), channel_id=1, source_target_pairs={{0,128},{64,196},{128,4},{192,64},{4,132},{68,192},{132,0},{196,68... | collective-permute-start | bytes 6303752 | tf_op jit(solution)/shard_map/ppermute | solution.py:148
  10.8 52.2 %collective-permute-start.2 = (f32[4104,128]{1,0:T(8,128)}, f32[4104,128]{1,0:T(8,128)}, u32[]{:S(2)}, u32[]{:S(2)}) collective-permute-start(f32[4104,128]{1,0:T(8,128)} %collective-permute-done.1.refs_5_), channel_id=1, source_target_pairs={{0,128},{64,196},{128,4},{192,64},{4,132},{68,192},{132,0},{196,68... | collective-permute-start | bytes 6303752 | tf_op jit(solution)/shard_map/ppermute | solution.py:148
  24.8 25.4 %collective-permute-start.4 = (f32[2312,128]{1,0:T(8,128)S(1)}, f32[2312,128]{1,0:T(8,128)S(1)}, u32[]{:S(2)}, u32[]{:S(2)}) collective-permute-start(f32[2312,128]{1,0:T(8,128)S(1)} %collective-permute-done.3.refs_0_), channel_id=1, source_target_pairs={{0,8},{64,120},{8,16},{72,64},{16,24},{80,72},{24,32},{88,80},{32,... | collective-permute-start | bytes 3551240 | tf_op jit(solution)/shard_map/ppermute | solution.py:153
  37.5 25.5 %collective-permute-start.7 = (f32[2312,128]{1,0:T(8,128)S(1)}, f32[2312,128]{1,0:T(8,128)}, u32[]{:S(2)}, u32[]{:S(2)}) collective-permute-start(f32[2312,128]{1,0:T(8,128)S(1)} %collective-permute-done.6), channel_id=1, source_target_pairs={{0,8},{64,120},{8,16},{72,64},{16,24},{80,72},{24,32},{88,80},{32,... | collective-permute-start | bytes 3551240 | tf_op jit(solution)/shard_map/ppermute | solution.py:153
  63.0 26.4 %collective-permute-start.11 = (f32[4104,128]{1,0:T(8,128)}, f32[4104,128]{1,0:T(8,128)}, u32[]{:S(2)}, u32[]{:S(2)}) collective-permute-start(f32[4104,128]{1,0:T(8,128)} %collective-permute-done.refs_6_), channel_id=1, source_target_pairs={{0,128},{64,196},{128,4},{192,64},{4,132},{68,192},{132,0},{196,68... | collective-permute-start | bytes 6303752 | tf_op jit(solution)/shard_map/ppermute | solution.py:148
  63.5 17.6 %collective-permute-start.9 = (f32[2312,128]{1,0:T(8,128)S(1)}, f32[2312,128]{1,0:T(8,128)}, u32[]{:S(2)}, u32[]{:S(2)}) collective-permute-start(f32[2312,128]{1,0:T(8,128)S(1)} %collective-permute-done.4.refs_1_), channel_id=1, source_target_pairs={{0,8},{64,120},{8,16},{72,64},{16,24},{80,72},{24,32},{88,80},{32,... | collective-permute-start | bytes 3551240 | tf_op jit(solution)/shard_map/ppermute | solution.py:153
  63.5 30.1 %collective-permute-start.19 = (f32[2312,128]{1,0:T(8,128)}, f32[2312,128]{1,0:T(8,128)S(1)}, u32[]{:S(2)}, u32[]{:S(2)}) collective-permute-start(f32[2312,128]{1,0:T(8,128)} %collective-permute-done.7), channel_id=1, source_target_pairs={{0,8},{64,120},{8,16},{72,64},{16,24},{80,72},{24,32},{88,80},{32,... | collective-permute-start | bytes 3551240 | tf_op jit(solution)/shard_map/ppermute | solution.py:153
  81.0 16.7 %collective-permute-start.12 = (f32[4104,128]{1,0:T(8,128)}, f32[4104,128]{1,0:T(8,128)}, u32[]{:S(2)}, u32[]{:S(2)}) collective-permute-start(f32[4104,128]{1,0:T(8,128)} %collective-permute-done.refs_6_), channel_id=1, source_target_pairs={{0,64},{64,0},{1,65},{65,1},{2,66},{66,2},{3,67},{67,3},{4,68},{68... | collective-permute-start | bytes 6303752 | tf_op jit(solution)/shard_map/ppermute | solution.py:20
  81.0 16.7 %collective-permute-start.13 = (f32[4104,128]{1,0:T(8,128)}, f32[4104,128]{1,0:T(8,128)}, u32[]{:S(2)}, u32[]{:S(2)}) collective-permute-start(f32[4104,128]{1,0:T(8,128)} %collective-permute-done.2.refs_7_), channel_id=1, source_target_pairs={{0,64},{64,0},{1,65},{65,1},{2,66},{66,2},{3,67},{67,3},{4,68},{68... | collective-permute-start | bytes 6303752 | tf_op jit(solution)/shard_map/ppermute | solution.py:20
  89.4 8.4 %collective-permute-start.14 = (f32[4104,128]{1,0:T(8,128)}, f32[4104,128]{1,0:T(8,128)}, u32[]{:S(2)}, u32[]{:S(2)}) collective-permute-start(f32[4104,128]{1,0:T(8,128)} %collective-permute-done.11.refs_8_), channel_id=1, source_target_pairs={{0,64},{64,0},{1,65},{65,1},{2,66},{66,2},{3,67},{67,3},{4,68},{68... | collective-permute-start | bytes 6303752 | tf_op jit(solution)/shard_map/ppermute | solution.py:20
  89.7 5.6 %collective-permute-start.18 = (f32[2312,128]{1,0:T(8,128)S(1)}, f32[2312,128]{1,0:T(8,128)}, u32[]{:S(2)}, u32[]{:S(2)}) collective-permute-start(f32[2312,128]{1,0:T(8,128)S(1)} %collective-permute-done.6), channel_id=1, source_target_pairs={{0,64},{64,0},{1,65},{65,1},{2,66},{66,2},{3,67},{67,3},{4,68},{68... | collective-permute-start | bytes 3551240 | tf_op jit(solution)/shard_map/ppermute | solution.py:20
  93.6 3.5 %collective-permute-start.20 = (f32[2312,128]{1,0:T(8,128)S(1)}, f32[2312,128]{1,0:T(8,128)}, u32[]{:S(2)}, u32[]{:S(2)}) collective-permute-start(f32[2312,128]{1,0:T(8,128)S(1)} %collective-permute-done.19), channel_id=1, source_target_pairs={{0,64},{64,0},{1,65},{65,1},{2,66},{66,2},{3,67},{67,3},{4,68},{68... | collective-permute-start | bytes 3551240 | tf_op jit(solution)/shard_map/ppermute | solution.py:20
  95.4 16.9 %collective-permute-start.8 = (f32[2312,128]{1,0:T(8,128)}, f32[2312,128]{1,0:T(8,128)}, u32[]{:S(2)}, u32[]{:S(2)}) collective-permute-start(f32[2312,128]{1,0:T(8,128)} %collective-permute-done.7), channel_id=1, source_target_pairs={{0,64},{64,0},{1,65},{65,1},{2,66},{66,2},{3,67},{67,3},{4,68},{68... | collective-permute-start | bytes 3551240 | tf_op jit(solution)/shard_map/ppermute | solution.py:20
  97.0 17.8 %collective-permute-start.10 = (f32[2312,128]{1,0:T(8,128)}, f32[2312,128]{1,0:T(8,128)}, u32[]{:S(2)}, u32[]{:S(2)}) collective-permute-start(f32[2312,128]{1,0:T(8,128)} %collective-permute-done.9.refs_2_), channel_id=1, source_target_pairs={{0,8},{64,120},{8,16},{72,64},{16,24},{80,72},{24,32},{88,80},{32,... | collective-permute-start | bytes 3551240 | tf_op jit(solution)/shard_map/ppermute | solution.py:153
  108.9 20.2 %collective-permute-start.21 = (f32[12,128,128]{2,1,0:T(8,128)}, f32[12,128,128]{2,1,0:T(8,128)S(1)}, u32[]{:S(2)}, u32[]{:S(2)}) collective-permute-start(f32[12,128,128]{2,1,0:T(8,128)} %get-tuple-element.51), channel_id=1, source_target_pairs={{0,1},{1,2},{2,3},{3,0},{4,5},{5,6},{6,7},{7,4},{8,9},{9,10},{10,1... | collective-permute-start | bytes 2359304 | tf_op jit(solution)/shard_map/ppermute | solution.py:20
  110.6 19.1 %collective-permute-start.22 = (f32[12,128,128]{2,1,0:T(8,128)}, f32[12,128,128]{2,1,0:T(8,128)S(1)}, u32[]{:S(2)}, u32[]{:S(2)}) collective-permute-start(f32[12,128,128]{2,1,0:T(8,128)} %get-tuple-element.52), channel_id=1, source_target_pairs={{0,3},{1,0},{2,1},{3,2},{4,7},{5,4},{6,5},{7,6},{8,11},{9,8},{10,9... | collective-permute-start | bytes 2359304 | tf_op jit(solution)/shard_map/ppermute | solution.py:20
  126.0 13.0 %collective-permute-start.17 = (f32[6,128,128]{2,1,0:T(8,128)}, f32[6,128,128]{2,1,0:T(8,128)S(1)}, u32[]{:S(2)}, u32[]{:S(2)}) collective-permute-start(f32[6,128,128]{2,1,0:T(8,128)} %get-tuple-element.48), channel_id=1, source_target_pairs={{0,3},{1,0},{2,1},{3,2},{4,7},{5,4},{6,5},{7,6},{8,11},{9,8},{10,9... | collective-permute-start | bytes 1179656 | tf_op jit(solution)/shard_map/ppermute | solution.py:20
  129.8 17.5 %collective-permute-start.24 = (f32[6,128,128]{2,1,0:T(8,128)S(1)}, f32[6,128,128]{2,1,0:T(8,128)S(1)}, u32[]{:S(2)}, u32[]{:S(2)}) collective-permute-start(f32[6,128,128]{2,1,0:T(8,128)S(1)} %slice_add_fusion.1), channel_id=1, source_target_pairs={{0,3},{1,0},{2,1},{3,2},{4,7},{5,4},{6,5},{7,6},{8,11},{9,8},{10,9... | collective-permute-start | bytes 1179656 | tf_op jit(solution)/shard_map/ppermute | solution.py:20
  132.6 14.7 %collective-permute-start.23 = (f32[6,128,128]{2,1,0:T(8,128)S(1)}, f32[6,128,128]{2,1,0:T(8,128)S(1)}, u32[]{:S(2)}, u32[]{:S(2)}) collective-permute-start(f32[6,128,128]{2,1,0:T(8,128)S(1)} %slice_add_fusion.2), channel_id=1, source_target_pairs={{0,1},{1,2},{2,3},{3,0},{4,5},{5,6},{6,7},{7,4},{8,9},{9,10},{10,1... | collective-permute-start | bytes 1179656 | tf_op jit(solution)/shard_map/ppermute | solution.py:20
  132.7 21.3 %collective-permute-start.15 = (f32[6,128,128]{2,1,0:T(8,128)S(1)}, f32[6,128,128]{2,1,0:T(8,128)S(1)}, u32[]{:S(2)}, u32[]{:S(2)}) collective-permute-start(f32[6,128,128]{2,1,0:T(8,128)S(1)} %copy-done.14), channel_id=1, source_target_pairs={{0,1},{1,2},{2,3},{3,0},{4,5},{5,6},{6,7},{7,4},{8,9},{9,10},{10,1... | collective-permute-start | bytes 1179656 | tf_op jit(solution)/shard_map/ppermute | solution.py:20
  133.6 29.6 %collective-permute-start.26 = (f32[6,128,128]{2,1,0:T(8,128)S(1)}, f32[6,128,128]{2,1,0:T(8,128)S(1)}, u32[]{:S(2)}, u32[]{:S(2)}) collective-permute-start(f32[6,128,128]{2,1,0:T(8,128)S(1)} %copy-done.13), channel_id=1, source_target_pairs={{0,1},{1,2},{2,3},{3,0},{4,5},{5,6},{6,7},{7,4},{8,9},{9,10},{10,1... | collective-permute-start | bytes 1179656 | tf_op jit(solution)/shard_map/ppermute | solution.py:20
  147.3 15.9 %collective-permute-start.27 = (f32[6,128,128]{2,1,0:T(8,128)S(1)}, f32[6,128,128]{2,1,0:T(8,128)S(1)}, u32[]{:S(2)}, u32[]{:S(2)}) collective-permute-start(f32[6,128,128]{2,1,0:T(8,128)S(1)} %add.59), channel_id=1, source_target_pairs={{0,3},{1,0},{2,1},{3,2},{4,7},{5,4},{6,5},{7,6},{8,11},{9,8},{10,9... | collective-permute-start | bytes 1179656 | tf_op jit(solution)/shard_map/ppermute | solution.py:20
  154.8 16.1 %collective-permute-start.16 = (f32[6,128,128]{2,1,0:T(8,128)}, f32[6,128,128]{2,1,0:T(8,128)S(1)}, u32[]{:S(2)}, u32[]{:S(2)}) collective-permute-start(f32[6,128,128]{2,1,0:T(8,128)} %add.51), channel_id=1, source_target_pairs={{0,1},{1,2},{2,3},{3,0},{4,5},{5,6},{6,7},{7,4},{8,9},{9,10},{10,1... | collective-permute-start | bytes 1179656 | tf_op jit(solution)/shard_map/ppermute | solution.py:20
  155.6 15.2 %collective-permute-start.29 = (f32[6,128,128]{2,1,0:T(8,128)}, f32[6,128,128]{2,1,0:T(8,128)S(1)}, u32[]{:S(2)}, u32[]{:S(2)}) collective-permute-start(f32[6,128,128]{2,1,0:T(8,128)} %add_add_fusion), channel_id=1, source_target_pairs={{0,4},{4,0},{1,5},{5,1},{2,6},{6,2},{3,7},{7,3},{8,12},{12,8},{9,1... | collective-permute-start | bytes 1179656 | tf_op jit(solution)/shard_map/ppermute | solution.py:20
  160.0 10.9 %collective-permute-start.25 = (f32[6,128,128]{2,1,0:T(8,128)}, f32[6,128,128]{2,1,0:T(8,128)S(1)}, u32[]{:S(2)}, u32[]{:S(2)}) collective-permute-start(f32[6,128,128]{2,1,0:T(8,128)} %get-tuple-element.56), channel_id=1, source_target_pairs={{0,3},{1,0},{2,1},{3,2},{4,7},{5,4},{6,5},{7,6},{8,11},{9,8},{10,9... | collective-permute-start | bytes 1179656 | tf_op jit(solution)/shard_map/ppermute | solution.py:20
  164.0 13.4 %collective-permute-start.28 = (f32[6,128,128]{2,1,0:T(8,128)}, f32[6,128,128]{2,1,0:T(8,128)S(1)}, u32[]{:S(2)}, u32[]{:S(2)}) collective-permute-start(f32[6,128,128]{2,1,0:T(8,128)} %add_add_fusion.1), channel_id=1, source_target_pairs={{0,4},{4,0},{1,5},{5,1},{2,6},{6,2},{3,7},{7,3},{8,12},{12,8},{9,1... | collective-permute-start | bytes 1179656 | tf_op jit(solution)/shard_map/ppermute | solution.py:20
  (13 other events, 255.7 us)

commit v4 on v3

--- a/solution.py
+++ b/solution.py
@@ -193,7 +193,7 @@
     p_up, p_down, _ = together(p_up, p_down, q[0])
     p_near_0, p_near_1 = up(p_near_0 + p_up[:ROWS]), down(p_near_1 + p_down[:ROWS])
     q_far_1, q_plain_1, q_far_0 = down(q[5]), up(q[3]), up(q[4])
-    q7, q6, q_far_1, p_near_0, p_near_1 = together(q[7], q[6], q_far_1, p_near_0, p_near_1)
+    q7, q6, q_far_1 = together(q[7], q[6], q_far_1)
     p_other = shift(p_1 + p_up[ROWS:] + p_near_1, "xh", 2, 1)
     p_mine = p_0 + p_near_0 + p_down[ROWS:]
     q_near_1, q_plain_0 = down(q7 + q_far_1), down(q6)

time: 180 us -> 178 us (0.989)
  starting transfers between devices: 35.3 us -> 28.8 us
  waiting for transfers between devices: 112 us -> 115 us
    ppermute x20, starting transfers between devices: 27.9 us -> 21.3 us  [shift(): lax.ppermute(value, axis, [(i, (i + step) % size) for i in range(size)])]
    ppermute x20, waiting for transfers between devices: 30.6 us -> 34 us  [shift(): lax.ppermute(value, axis, [(i, (i + step) % size) for i in range(size)])]
  transfers between devices with their start and end apart: 30 -> 30, of which waited for: 17 -> 17; matrix products, arithmetic and copies ran while one was open for 3% -> 4% of each run, Pallas kernels for 12% -> 13%
where the time goes in v4:
time: 178 us; the launch traced here: 177 us
  waiting for transfers between devices  115 us (65%)
  starting transfers between devices  28.8 us (16%)
  Pallas kernels  22.3 us (13%)
  other arithmetic  8.9 us (5%)
    ppermute x7, waiting for transfers between devices, pass_z(): return lax.ppermute(value, ('co', 'z'), pairs)  73.5 us
    ppermute x20, waiting for transfers between devices, shift(): lax.ppermute(value, axis, [(i, (i + step) % size) for i in range(size)])  34 us
    pallas_call x2, Pallas kernels, products(): pl.pallas_call(functools.partial(product_kernel, spans, routes, len(b_par...  22.3 us
    ppermute x20, starting transfers between devices, shift(): lax.ppermute(value, axis, [(i, (i + step) % size) for i in range(size)])  21.3 us
    ppermute x3, waiting for transfers between devices, pass_on(): return lax.ppermute(value, ('xl', 'co', 'xh'), pairs)  7.84 us
    ppermute x7, starting transfers between devices, pass_z(): return lax.ppermute(value, ('co', 'z'), pairs)  4.97 us
  transfers between devices with their start and end apart: 30, of which 17 were waited for; matrix products, arithmetic and copies ran while one was open for 4% of the time, Pallas kernels for 13%

profile of v4, /device:TPU:6, one launch (start us, length us, event | category | flops | bytes accessed | tf_op | source)
XLA Modules:
  0.0 177.1 jit_solution(18437335541024807898)
XLA Ops:
  0.7 1.7 select_maximum_fusion.refs_4_
  2.7 1.8 %select_maximum_fusion.1.refs_0_ = f32[2312,128]{1,0:T(8,128)S(1)} fusion(f32[1,128]{1,0:T(1,128)S(1)} %convert_bitcast_fusion, f32[2304,128]{1,0:T(8,128)} %bitcast.27), kind=kLoop, calls=%fused_computation.3 | loop fusion | flops 887808 | bytes 2363904 | tf_op jit(solution)/shard_map/concatenate | solution.py:32
  4.7 2.0 %collective-permute-start.3 = (f32[2312,128]{1,0:T(8,128)S(1)}, f32[2312,128]{1,0:T(8,128)S(1)}, u32[]{:S(2)}, u32[]{:S(2)}) collective-permute-start(f32[2312,128]{1,0:T(8,128)S(1)} %select_maximum_fusion.1.refs_0_), channel_id=1, source_target_pairs={{0,8},{64,120},{8,16},{72,64},{16,24},{80,72},{24,32},{88,80},{32,... | collective-permute-start | bytes 3551240 | tf_op jit(solution)/shard_map/ppermute | solution.py:153
  6.6 1.7 collective-permute-done.5
  8.4 1.9 %collective-permute-start.6 = (f32[2312,128]{1,0:T(8,128)S(1)}, f32[2312,128]{1,0:T(8,128)S(1)}, u32[]{:S(2)}, u32[]{:S(2)}) collective-permute-start(f32[2312,128]{1,0:T(8,128)S(1)} %collective-permute-done.5), channel_id=1, source_target_pairs={{0,8},{64,120},{8,16},{72,64},{16,24},{80,72},{24,32},{88,80},{32,... | collective-permute-start | bytes 3551240 | tf_op jit(solution)/shard_map/ppermute | solution.py:153
  10.8 1.5 collective-permute-start.2
  12.3 12.5 %collective-permute-done.3.refs_0_ = f32[2312,128]{1,0:T(8,128)S(1)} collective-permute-done((f32[2312,128]{1,0:T(8,128)S(1)}, f32[2312,128]{1,0:T(8,128)S(1)}, u32[]{:S(2)}, u32[]{:S(2)}) %collective-permute-start.3) | collective-permute-done | bytes 1183776 | tf_op jit(solution)/shard_map/ppermute | solution.py:153
  24.8 12.7 %collective-permute-done.6 = f32[2312,128]{1,0:T(8,128)S(1)} collective-permute-done((f32[2312,128]{1,0:T(8,128)S(1)}, f32[2312,128]{1,0:T(8,128)S(1)}, u32[]{:S(2)}, u32[]{:S(2)}) %collective-permute-start.6) | collective-permute-done | bytes 1183776 | tf_op jit(solution)/shard_map/ppermute | solution.py:153
  37.5 12.7 %collective-permute-done.4.refs_1_ = f32[2312,128]{1,0:T(8,128)S(1)} collective-permute-done((f32[2312,128]{1,0:T(8,128)S(1)}, f32[2312,128]{1,0:T(8,128)S(1)}, u32[]{:S(2)}, u32[]{:S(2)}) %collective-permute-start.4) | collective-permute-done | bytes 1183776 | tf_op jit(solution)/shard_map/ppermute | solution.py:153
  50.2 12.8 %collective-permute-done.7 = f32[2312,128]{1,0:T(8,128)} collective-permute-done((f32[2312,128]{1,0:T(8,128)S(1)}, f32[2312,128]{1,0:T(8,128)}, u32[]{:S(2)}, u32[]{:S(2)}) %collective-permute-start.7) | collective-permute-done | bytes 1183776 | tf_op jit(solution)/shard_map/ppermute | solution.py:153
  64.5 16.5 %collective-permute-done.9.refs_2_ = f32[2312,128]{1,0:T(8,128)} collective-permute-done((f32[2312,128]{1,0:T(8,128)S(1)}, f32[2312,128]{1,0:T(8,128)}, u32[]{:S(2)}, u32[]{:S(2)}) %collective-permute-start.9) | collective-permute-done | bytes 1183776 | tf_op jit(solution)/shard_map/ppermute | solution.py:153
  81.5 7.8 %collective-permute-done.11.refs_8_ = f32[4104,128]{1,0:T(8,128)} collective-permute-done((f32[4104,128]{1,0:T(8,128)}, f32[4104,128]{1,0:T(8,128)}, u32[]{:S(2)}, u32[]{:S(2)}) %collective-permute-start.11) | collective-permute-done | bytes 2101280 | tf_op jit(solution)/shard_map/ppermute | solution.py:148
  89.9 3.7 %collective-permute-done.20 = f32[2312,128]{1,0:T(8,128)S(1)} collective-permute-done((f32[2312,128]{1,0:T(8,128)}, f32[2312,128]{1,0:T(8,128)S(1)}, u32[]{:S(2)}, u32[]{:S(2)}) %collective-permute-start.20) | collective-permute-done | bytes 1183776 | tf_op jit(solution)/shard_map/ppermute | solution.py:153
  93.6 1.8 collective-permute-done.19.refs_1_
  95.7 1.3 collective-permute-done.21.refs_3_
  97.7 11.2 %shard_map.56 = (f32[12,128,128]{2,1,0:T(8,128)}, f32[12,128,128]{2,1,0:T(8,128)}, f32[6,128,128]{2,1,0:T(8,128)}, f32[6,128,128]{2,1,0:T(8,128)}, f32[6,128,128]{2,1,0:T(8,128)}, /*index=5*/f32[6,128,128]{2,1,0:T(8,128)}) custom-call(s32[5]{0:T(128)} %stack.48.place, f32[2312,128]{1,0:T(8,128)} %copy-done.3, f32[2312,128]{1,0:T(8,128)} %collective-permute-done.19.refs_1_, ...), custom_call_target="tpu_custom_call" | custom-call | flops 1811939328 | bytes 24641536 | tf_op jit(solution)/shard_map/pallas_call | solution.py:118
  108.9 1.6 collective-permute-start.22
  110.5 1.7 collective-permute-start.23
  112.2 2.6 %collective-permute-done.10.refs_3_ = f32[2312,128]{1,0:T(8,128)} collective-permute-done((f32[2312,128]{1,0:T(8,128)}, f32[2312,128]{1,0:T(8,128)}, u32[]{:S(2)}, u32[]{:S(2)}) %collective-permute-start.10) | collective-permute-done | bytes 1183776 | tf_op jit(solution)/shard_map/ppermute | solution.py:153
  114.8 11.2 %shard_map.55 = (f32[6,128,128]{2,1,0:T(8,128)}, f32[6,128,128]{2,1,0:T(8,128)}, f32[6,128,128]{2,1,0:T(8,128)}, f32[6,128,128]{2,1,0:T(8,128)}, f32[6,128,128]{...) custom-call(s32[5]{0:T(128)} %stack.48.place, f32[2312,128]{1,0:T(8,128)} %copy-done.1, ...), custom_call_target="tpu_custom_call" | custom-call | flops 1811939328 | bytes 24641536 | tf_op jit(solution)/shard_map/pallas_call | solution.py:118
  126.0 3.1 %collective-permute-start.17 = (f32[6,128,128]{2,1,0:T(8,128)}, f32[6,128,128]{2,1,0:T(8,128)S(1)}, u32[]{:S(2)}, u32[]{:S(2)}) collective-permute-start(f32[6,128,128]{2,1,0:T(8,128)} %get-tuple-element.46), channel_id=1, source_target_pairs={{0,3},{1,0},{2,1},{3,2},{4,7},{5,4},{6,5},{7,6},{8,11},{9,8},{10,9... | collective-permute-start | bytes 1179656 | tf_op jit(solution)/shard_map/ppermute | solution.py:20
  129.7 9.2 %collective-permute-done.17 = f32[6,128,128]{2,1,0:T(8,128)S(1)} collective-permute-done((f32[6,128,128]{2,1,0:T(8,128)}, f32[6,128,128]{2,1,0:T(8,128)S(1)}, u32[]{:S(2)}, u32[]{:S(2)}) %collective-permute-start.17) | collective-permute-done | bytes 393248 | tf_op jit(solution)/shard_map/ppermute | solution.py:20
  140.0 3.7 %collective-permute-start.26 = (f32[6,128,128]{2,1,0:T(8,128)S(1)}, f32[6,128,128]{2,1,0:T(8,128)S(1)}, u32[]{:S(2)}, u32[]{:S(2)}) collective-permute-start(f32[6,128,128]{2,1,0:T(8,128)S(1)} %add.58), channel_id=1, source_target_pairs={{0,3},{1,0},{2,1},{3,2},{4,7},{5,4},{6,5},{7,6},{8,11},{9,8},{10,9... | collective-permute-start | bytes 1179656 | tf_op jit(solution)/shard_map/ppermute | solution.py:20
  144.9 2.0 %collective-permute-start.16 = (f32[6,128,128]{2,1,0:T(8,128)}, f32[6,128,128]{2,1,0:T(8,128)S(1)}, u32[]{:S(2)}, u32[]{:S(2)}) collective-permute-start(f32[6,128,128]{2,1,0:T(8,128)} %add.51), channel_id=1, source_target_pairs={{0,1},{1,2},{2,3},{3,0},{4,5},{5,6},{6,7},{7,4},{8,9},{9,10},{10,1... | collective-permute-start | bytes 1179656 | tf_op jit(solution)/shard_map/ppermute | solution.py:20
  148.1 5.0 %collective-permute-done.26 = f32[6,128,128]{2,1,0:T(8,128)S(1)} collective-permute-done((f32[6,128,128]{2,1,0:T(8,128)S(1)}, f32[6,128,128]{2,1,0:T(8,128)S(1)}, u32[]{:S(2)}, u32[]{:S(2)}) %collective-permute-start.26) | collective-permute-done | bytes 393248 | tf_op jit(solution)/shard_map/ppermute | solution.py:20
  154.0 2.2 %collective-permute-start.27 = (f32[6,128,128]{2,1,0:T(8,128)}, f32[6,128,128]{2,1,0:T(8,128)S(1)}, u32[]{:S(2)}, u32[]{:S(2)}) collective-permute-start(f32[6,128,128]{2,1,0:T(8,128)} %add_add_fusion.1), channel_id=1, source_target_pairs={{0,4},{4,0},{1,5},{5,1},{2,6},{6,2},{3,7},{7,3},{8,12},{12,8},{9,1... | collective-permute-start | bytes 1179656 | tf_op jit(solution)/shard_map/ppermute | solution.py:20
  156.2 5.4 %collective-permute-done.28 = f32[6,128,128]{2,1,0:T(8,128)S(1)} collective-permute-done((f32[6,128,128]{2,1,0:T(8,128)S(1)}, f32[6,128,128]{2,1,0:T(8,128)S(1)}, u32[]{:S(2)}, u32[]{:S(2)}) %collective-permute-start.28) | collective-permute-done | bytes 393248 | tf_op jit(solution)/shard_map/ppermute | solution.py:20
  162.6 3.3 %collective-permute-start.29 = (f32[6,128,128]{2,1,0:T(8,128)}, f32[6,128,128]{2,1,0:T(8,128)S(1)}, u32[]{:S(2)}, u32[]{:S(2)}) collective-permute-start(f32[6,128,128]{2,1,0:T(8,128)} %get-tuple-element.68), channel_id=1, source_target_pairs={{0,4},{4,0},{1,5},{5,1},{2,6},{6,2},{3,7},{7,3},{8,12},{12,8},{9,1... | collective-permute-start | bytes 1179656 | tf_op jit(solution)/shard_map/ppermute | solution.py:20
  165.9 3.4 %collective-permute-done.18 = f32[6,128,128]{2,1,0:T(8,128)S(1)} collective-permute-done((f32[6,128,128]{2,1,0:T(8,128)}, f32[6,128,128]{2,1,0:T(8,128)S(1)}, u32[]{:S(2)}, u32[]{:S(2)}) %collective-permute-start.18) | collective-permute-done | bytes 393248 | tf_op jit(solution)/shard_map/ppermute | solution.py:20
  169.2 4.9 %collective-permute-done.24 = f32[6,128,128]{2,1,0:T(8,128)S(1)} collective-permute-done((f32[6,128,128]{2,1,0:T(8,128)}, f32[6,128,128]{2,1,0:T(8,128)S(1)}, u32[]{:S(2)}, u32[]{:S(2)}) %collective-permute-start.24) | collective-permute-done | bytes 393248 | tf_op jit(solution)/shard_map/ppermute | solution.py:20
  174.1 1.3 collective-permute-done.29
  175.8 1.3 pad_maximum_fusion
  (70 shorter events, 11.6 us)
Async XLA Ops:
  2.4 95.3 %copy-start = (f32[4104,128]{1,0:T(8,128)}, f32[4104,128]{1,0:T(8,128)S(1)}, u32[]{:S(2)}) copy-start(f32[4104,128]{1,0:T(8,128)S(1)} %select_maximum_fusion.refs_4_) | copy-start | bytes 6303748
  2.4 8.3 %collective-permute-start.1 = (f32[4104,128]{1,0:T(8,128)S(1)}, f32[4104,128]{1,0:T(8,128)}, u32[]{:S(2)}, u32[]{:S(2)}) collective-permute-start(f32[4104,128]{1,0:T(8,128)S(1)} %select_maximum_fusion.refs_4_), channel_id=1, source_target_pairs={{0,64},{64,0},{1,65},{65,1},{2,66},{66,2},{3,67},{67,3},{4,68},{68... | collective-permute-start | bytes 6303752 | tf_op jit(solution)/shard_map/ppermute | solution.py:20
  4.5 104.4 %copy-start.1 = (f32[2312,128]{1,0:T(8,128)}, f32[2312,128]{1,0:T(8,128)S(1)}, u32[]{:S(2)}) copy-start(f32[2312,128]{1,0:T(8,128)S(1)} %select_maximum_fusion.1.refs_0_) | copy-start | bytes 3551236
  4.5 3.8 %collective-permute-start.5 = (f32[2312,128]{1,0:T(8,128)S(1)}, f32[2312,128]{1,0:T(8,128)S(1)}, u32[]{:S(2)}, u32[]{:S(2)}) collective-permute-start(f32[2312,128]{1,0:T(8,128)S(1)} %select_maximum_fusion.1.refs_0_), channel_id=1, source_target_pairs={{0,64},{64,0},{1,65},{65,1},{2,66},{66,2},{3,67},{67,3},{4,68},{68... | collective-permute-start | bytes 3551240 | tf_op jit(solution)/shard_map/ppermute | solution.py:20
  4.7 20.1 %collective-permute-start.3 = (f32[2312,128]{1,0:T(8,128)S(1)}, f32[2312,128]{1,0:T(8,128)S(1)}, u32[]{:S(2)}, u32[]{:S(2)}) collective-permute-start(f32[2312,128]{1,0:T(8,128)S(1)} %select_maximum_fusion.1.refs_0_), channel_id=1, source_target_pairs={{0,8},{64,120},{8,16},{72,64},{16,24},{80,72},{24,32},{88,80},{32,... | collective-permute-start | bytes 3551240 | tf_op jit(solution)/shard_map/ppermute | solution.py:153
  8.4 29.1 %collective-permute-start.6 = (f32[2312,128]{1,0:T(8,128)S(1)}, f32[2312,128]{1,0:T(8,128)S(1)}, u32[]{:S(2)}, u32[]{:S(2)}) collective-permute-start(f32[2312,128]{1,0:T(8,128)S(1)} %collective-permute-done.5), channel_id=1, source_target_pairs={{0,8},{64,120},{8,16},{72,64},{16,24},{80,72},{24,32},{88,80},{32,... | collective-permute-start | bytes 3551240 | tf_op jit(solution)/shard_map/ppermute | solution.py:153
  10.3 27.2 %collective-permute-start = (f32[4104,128]{1,0:T(8,128)S(1)}, f32[4104,128]{1,0:T(8,128)}, u32[]{:S(2)}, u32[]{:S(2)}) collective-permute-start(f32[4104,128]{1,0:T(8,128)S(1)} %select_maximum_fusion.refs_4_), channel_id=1, source_target_pairs={{0,128},{64,196},{128,4},{192,64},{4,132},{68,192},{132,0},{196,68... | collective-permute-start | bytes 6303752 | tf_op jit(solution)/shard_map/ppermute | solution.py:148
  10.8 52.2 %collective-permute-start.2 = (f32[4104,128]{1,0:T(8,128)}, f32[4104,128]{1,0:T(8,128)}, u32[]{:S(2)}, u32[]{:S(2)}) collective-permute-start(f32[4104,128]{1,0:T(8,128)} %collective-permute-done.1.refs_5_), channel_id=1, source_target_pairs={{0,128},{64,196},{128,4},{192,64},{4,132},{68,192},{132,0},{196,68... | collective-permute-start | bytes 6303752 | tf_op jit(solution)/shard_map/ppermute | solution.py:148
  24.8 25.4 %collective-permute-start.4 = (f32[2312,128]{1,0:T(8,128)S(1)}, f32[2312,128]{1,0:T(8,128)S(1)}, u32[]{:S(2)}, u32[]{:S(2)}) collective-permute-start(f32[2312,128]{1,0:T(8,128)S(1)} %collective-permute-done.3.refs_0_), channel_id=1, source_target_pairs={{0,8},{64,120},{8,16},{72,64},{16,24},{80,72},{24,32},{88,80},{32,... | collective-permute-start | bytes 3551240 | tf_op jit(solution)/shard_map/ppermute | solution.py:153
  37.5 25.5 %collective-permute-start.7 = (f32[2312,128]{1,0:T(8,128)S(1)}, f32[2312,128]{1,0:T(8,128)}, u32[]{:S(2)}, u32[]{:S(2)}) collective-permute-start(f32[2312,128]{1,0:T(8,128)S(1)} %collective-permute-done.6), channel_id=1, source_target_pairs={{0,8},{64,120},{8,16},{72,64},{16,24},{80,72},{24,32},{88,80},{32,... | collective-permute-start | bytes 3551240 | tf_op jit(solution)/shard_map/ppermute | solution.py:153
  63.0 26.4 %collective-permute-start.11 = (f32[4104,128]{1,0:T(8,128)}, f32[4104,128]{1,0:T(8,128)}, u32[]{:S(2)}, u32[]{:S(2)}) collective-permute-start(f32[4104,128]{1,0:T(8,128)} %collective-permute-done.refs_6_), channel_id=1, source_target_pairs={{0,128},{64,196},{128,4},{192,64},{4,132},{68,192},{132,0},{196,68... | collective-permute-start | bytes 6303752 | tf_op jit(solution)/shard_map/ppermute | solution.py:148
  63.5 17.6 %collective-permute-start.9 = (f32[2312,128]{1,0:T(8,128)S(1)}, f32[2312,128]{1,0:T(8,128)}, u32[]{:S(2)}, u32[]{:S(2)}) collective-permute-start(f32[2312,128]{1,0:T(8,128)S(1)} %collective-permute-done.4.refs_1_), channel_id=1, source_target_pairs={{0,8},{64,120},{8,16},{72,64},{16,24},{80,72},{24,32},{88,80},{32,... | collective-permute-start | bytes 3551240 | tf_op jit(solution)/shard_map/ppermute | solution.py:153
  63.5 30.1 %collective-permute-start.20 = (f32[2312,128]{1,0:T(8,128)}, f32[2312,128]{1,0:T(8,128)S(1)}, u32[]{:S(2)}, u32[]{:S(2)}) collective-permute-start(f32[2312,128]{1,0:T(8,128)} %collective-permute-done.7), channel_id=1, source_target_pairs={{0,8},{64,120},{8,16},{72,64},{16,24},{80,72},{24,32},{88,80},{32,... | collective-permute-start | bytes 3551240 | tf_op jit(solution)/shard_map/ppermute | solution.py:153
  81.0 16.7 %collective-permute-start.12 = (f32[4104,128]{1,0:T(8,128)}, f32[4104,128]{1,0:T(8,128)}, u32[]{:S(2)}, u32[]{:S(2)}) collective-permute-start(f32[4104,128]{1,0:T(8,128)} %collective-permute-done.refs_6_), channel_id=1, source_target_pairs={{0,64},{64,0},{1,65},{65,1},{2,66},{66,2},{3,67},{67,3},{4,68},{68... | collective-permute-start | bytes 6303752 | tf_op jit(solution)/shard_map/ppermute | solution.py:20
  81.0 16.7 %collective-permute-start.13 = (f32[4104,128]{1,0:T(8,128)}, f32[4104,128]{1,0:T(8,128)}, u32[]{:S(2)}, u32[]{:S(2)}) collective-permute-start(f32[4104,128]{1,0:T(8,128)} %collective-permute-done.2.refs_7_), channel_id=1, source_target_pairs={{0,64},{64,0},{1,65},{65,1},{2,66},{66,2},{3,67},{67,3},{4,68},{68... | collective-permute-start | bytes 6303752 | tf_op jit(solution)/shard_map/ppermute | solution.py:20
  89.4 8.3 %collective-permute-start.14 = (f32[4104,128]{1,0:T(8,128)}, f32[4104,128]{1,0:T(8,128)}, u32[]{:S(2)}, u32[]{:S(2)}) collective-permute-start(f32[4104,128]{1,0:T(8,128)} %collective-permute-done.11.refs_8_), channel_id=1, source_target_pairs={{0,64},{64,0},{1,65},{65,1},{2,66},{66,2},{3,67},{67,3},{4,68},{68... | collective-permute-start | bytes 6303752 | tf_op jit(solution)/shard_map/ppermute | solution.py:20
  89.7 5.6 %collective-permute-start.19 = (f32[2312,128]{1,0:T(8,128)S(1)}, f32[2312,128]{1,0:T(8,128)}, u32[]{:S(2)}, u32[]{:S(2)}) collective-permute-start(f32[2312,128]{1,0:T(8,128)S(1)} %collective-permute-done.6), channel_id=1, source_target_pairs={{0,64},{64,0},{1,65},{65,1},{2,66},{66,2},{3,67},{67,3},{4,68},{68... | collective-permute-start | bytes 3551240 | tf_op jit(solution)/shard_map/ppermute | solution.py:20
  93.6 3.5 %collective-permute-start.21 = (f32[2312,128]{1,0:T(8,128)S(1)}, f32[2312,128]{1,0:T(8,128)}, u32[]{:S(2)}, u32[]{:S(2)}) collective-permute-start(f32[2312,128]{1,0:T(8,128)S(1)} %collective-permute-done.20), channel_id=1, source_target_pairs={{0,64},{64,0},{1,65},{65,1},{2,66},{66,2},{3,67},{67,3},{4,68},{68... | collective-permute-start | bytes 3551240 | tf_op jit(solution)/shard_map/ppermute | solution.py:20
  95.4 16.9 %collective-permute-start.8 = (f32[2312,128]{1,0:T(8,128)}, f32[2312,128]{1,0:T(8,128)}, u32[]{:S(2)}, u32[]{:S(2)}) collective-permute-start(f32[2312,128]{1,0:T(8,128)} %collective-permute-done.7), channel_id=1, source_target_pairs={{0,64},{64,0},{1,65},{65,1},{2,66},{66,2},{3,67},{67,3},{4,68},{68... | collective-permute-start | bytes 3551240 | tf_op jit(solution)/shard_map/ppermute | solution.py:20
  97.0 17.8 %collective-permute-start.10 = (f32[2312,128]{1,0:T(8,128)}, f32[2312,128]{1,0:T(8,128)}, u32[]{:S(2)}, u32[]{:S(2)}) collective-permute-start(f32[2312,128]{1,0:T(8,128)} %collective-permute-done.9.refs_2_), channel_id=1, source_target_pairs={{0,8},{64,120},{8,16},{72,64},{16,24},{80,72},{24,32},{88,80},{32,... | collective-permute-start | bytes 3551240 | tf_op jit(solution)/shard_map/ppermute | solution.py:153
  108.9 34.8 %collective-permute-start.22 = (f32[12,128,128]{2,1,0:T(8,128)}, f32[12,128,128]{2,1,0:T(8,128)S(1)}, u32[]{:S(2)}, u32[]{:S(2)}) collective-permute-start(f32[12,128,128]{2,1,0:T(8,128)} %get-tuple-element.51), channel_id=1, source_target_pairs={{0,1},{1,2},{2,3},{3,0},{4,5},{5,6},{6,7},{7,4},{8,9},{9,10},{10,1... | collective-permute-start | bytes 2359304 | tf_op jit(solution)/shard_map/ppermute | solution.py:20
  110.5 33.1 %collective-permute-start.23 = (f32[12,128,128]{2,1,0:T(8,128)}, f32[12,128,128]{2,1,0:T(8,128)S(1)}, u32[]{:S(2)}, u32[]{:S(2)}) collective-permute-start(f32[12,128,128]{2,1,0:T(8,128)} %get-tuple-element.52), channel_id=1, source_target_pairs={{0,3},{1,0},{2,1},{3,2},{4,7},{5,4},{6,5},{7,6},{8,11},{9,8},{10,9... | collective-permute-start | bytes 2359304 | tf_op jit(solution)/shard_map/ppermute | solution.py:20
  126.0 12.9 %collective-permute-start.17 = (f32[6,128,128]{2,1,0:T(8,128)}, f32[6,128,128]{2,1,0:T(8,128)S(1)}, u32[]{:S(2)}, u32[]{:S(2)}) collective-permute-start(f32[6,128,128]{2,1,0:T(8,128)} %get-tuple-element.46), channel_id=1, source_target_pairs={{0,3},{1,0},{2,1},{3,2},{4,7},{5,4},{6,5},{7,6},{8,11},{9,8},{10,9... | collective-permute-start | bytes 1179656 | tf_op jit(solution)/shard_map/ppermute | solution.py:20
  129.1 15.0 %collective-permute-start.15 = (f32[6,128,128]{2,1,0:T(8,128)}, f32[6,128,128]{2,1,0:T(8,128)S(1)}, u32[]{:S(2)}, u32[]{:S(2)}) collective-permute-start(f32[6,128,128]{2,1,0:T(8,128)} %get-tuple-element.43), channel_id=1, source_target_pairs={{0,1},{1,2},{2,3},{3,0},{4,5},{5,6},{6,7},{7,4},{8,9},{9,10},{10,1... | collective-permute-start | bytes 1179656 | tf_op jit(solution)/shard_map/ppermute | solution.py:20
  129.1 19.1 %collective-permute-start.25 = (f32[6,128,128]{2,1,0:T(8,128)}, f32[6,128,128]{2,1,0:T(8,128)S(1)}, u32[]{:S(2)}, u32[]{:S(2)}) collective-permute-start(f32[6,128,128]{2,1,0:T(8,128)} %get-tuple-element.56), channel_id=1, source_target_pairs={{0,1},{1,2},{2,3},{3,0},{4,5},{5,6},{6,7},{7,4},{8,9},{9,10},{10,1... | collective-permute-start | bytes 1179656 | tf_op jit(solution)/shard_map/ppermute | solution.py:20
  140.0 13.2 %collective-permute-start.26 = (f32[6,128,128]{2,1,0:T(8,128)S(1)}, f32[6,128,128]{2,1,0:T(8,128)S(1)}, u32[]{:S(2)}, u32[]{:S(2)}) collective-permute-start(f32[6,128,128]{2,1,0:T(8,128)S(1)} %add.58), channel_id=1, source_target_pairs={{0,3},{1,0},{2,1},{3,2},{4,7},{5,4},{6,5},{7,6},{8,11},{9,8},{10,9... | collective-permute-start | bytes 1179656 | tf_op jit(solution)/shard_map/ppermute | solution.py:20
  143.7 17.8 %collective-permute-start.28 = (f32[6,128,128]{2,1,0:T(8,128)S(1)}, f32[6,128,128]{2,1,0:T(8,128)S(1)}, u32[]{:S(2)}, u32[]{:S(2)}) collective-permute-start(f32[6,128,128]{2,1,0:T(8,128)S(1)} %slice_add_fusion), channel_id=1, source_target_pairs={{0,3},{1,0},{2,1},{3,2},{4,7},{5,4},{6,5},{7,6},{8,11},{9,8},{10,9... | collective-permute-start | bytes 1179656 | tf_op jit(solution)/shard_map/ppermute | solution.py:20
  144.9 21.0 %collective-permute-start.16 = (f32[6,128,128]{2,1,0:T(8,128)}, f32[6,128,128]{2,1,0:T(8,128)S(1)}, u32[]{:S(2)}, u32[]{:S(2)}) collective-permute-start(f32[6,128,128]{2,1,0:T(8,128)} %add.51), channel_id=1, source_target_pairs={{0,1},{1,2},{2,3},{3,0},{4,5},{5,6},{6,7},{7,4},{8,9},{9,10},{10,1... | collective-permute-start | bytes 1179656 | tf_op jit(solution)/shard_map/ppermute | solution.py:20
  146.9 22.4 %collective-permute-start.18 = (f32[6,128,128]{2,1,0:T(8,128)}, f32[6,128,128]{2,1,0:T(8,128)S(1)}, u32[]{:S(2)}, u32[]{:S(2)}) collective-permute-start(f32[6,128,128]{2,1,0:T(8,128)} %get-tuple-element.47), channel_id=1, source_target_pairs={{0,3},{1,0},{2,1},{3,2},{4,7},{5,4},{6,5},{7,6},{8,11},{9,8},{10,9... | collective-permute-start | bytes 1179656 | tf_op jit(solution)/shard_map/ppermute | solution.py:20
  154.0 15.3 %collective-permute-start.27 = (f32[6,128,128]{2,1,0:T(8,128)}, f32[6,128,128]{2,1,0:T(8,128)S(1)}, u32[]{:S(2)}, u32[]{:S(2)}) collective-permute-start(f32[6,128,128]{2,1,0:T(8,128)} %add_add_fusion.1), channel_id=1, source_target_pairs={{0,4},{4,0},{1,5},{5,1},{2,6},{6,2},{3,7},{7,3},{8,12},{12,8},{9,1... | collective-permute-start | bytes 1179656 | tf_op jit(solution)/shard_map/ppermute | solution.py:20
  162.6 11.5 %collective-permute-start.24 = (f32[6,128,128]{2,1,0:T(8,128)}, f32[6,128,128]{2,1,0:T(8,128)S(1)}, u32[]{:S(2)}, u32[]{:S(2)}) collective-permute-start(f32[6,128,128]{2,1,0:T(8,128)} %get-tuple-element.67), channel_id=1, source_target_pairs={{0,1},{1,2},{2,3},{3,0},{4,5},{5,6},{6,7},{7,4},{8,9},{9,10},{10,1... | collective-permute-start | bytes 1179656 | tf_op jit(solution)/shard_map/ppermute | solution.py:20
  162.6 12.8 %collective-permute-start.29 = (f32[6,128,128]{2,1,0:T(8,128)}, f32[6,128,128]{2,1,0:T(8,128)S(1)}, u32[]{:S(2)}, u32[]{:S(2)}) collective-permute-start(f32[6,128,128]{2,1,0:T(8,128)} %get-tuple-element.68), channel_id=1, source_target_pairs={{0,4},{4,0},{1,5},{5,1},{2,6},{6,2},{3,7},{7,3},{8,12},{12,8},{9,1... | collective-permute-start | bytes 1179656 | tf_op jit(solution)/shard_map/ppermute | solution.py:20
  (10 other events, 215.5 us)

commit v5 on v4

--- a/solution.py
+++ b/solution.py
@@ -195,10 +195,11 @@
     q_far_1, q_plain_1, q_far_0 = down(q[5]), up(q[3]), up(q[4])
     q7, q6, q_far_1 = together(q[7], q[6], q_far_1)
     p_other = shift(p_1 + p_up[ROWS:] + p_near_1, "xh", 2, 1)
-    p_mine = p_0 + p_near_0 + p_down[ROWS:]
     q_near_1, q_plain_0 = down(q7 + q_far_1), down(q6)
     q_other = shift(q[1] + q_plain_1 + q_near_1, "xh", 2, 1)
+    q_far_0, p_near_0 = together(q_far_0, p_near_0)
     q_near_0 = up(q[2] + q_far_0)
+    p_mine = p_0 + p_near_0 + p_down[ROWS:]
     q_mine = q[0] + q_near_0 + q_plain_0
     own_parity = lax.axis_index("z") % 2
     own_half = lax.axis_index("xh")

time: 178 us -> 183 us (1.028); the launches traced: 177 us -> 179 us
  transfers between devices with their start and end apart: 30 -> 30, of which waited for: 17 -> 20; matrix products, arithmetic and copies ran while one was open for 4% -> 3% of each run, Pallas kernels for 13% -> 12%
where the time goes in v5:
time: 183 us; the launch traced here: 179 us
  waiting for transfers between devices  116 us (63%)
  starting transfers between devices  30.3 us (17%)
  Pallas kernels  22.3 us (12%)
  other arithmetic  8.72 us (5%)
    ppermute x7, waiting for transfers between devices, pass_z(): return lax.ppermute(value, ('co', 'z'), pairs)  73.5 us
    ppermute x20, waiting for transfers between devices, shift(): lax.ppermute(value, axis, [(i, (i + step) % size) for i in range(size)])  34.8 us
    ppermute x20, starting transfers between devices, shift(): lax.ppermute(value, axis, [(i, (i + step) % size) for i in range(size)])  22.9 us
    pallas_call x2, Pallas kernels, products(): pl.pallas_call(functools.partial(product_kernel, spans, routes, len(b_par...  22.3 us
    ppermute x3, waiting for transfers between devices, pass_on(): return lax.ppermute(value, ('xl', 'co', 'xh'), pairs)  7.84 us
    ppermute x7, starting transfers between devices, pass_z(): return lax.ppermute(value, ('co', 'z'), pairs)  4.97 us
  transfers between devices with their start and end apart: 30, of which 20 were waited for; matrix products, arithmetic and copies ran while one was open for 3% of the time, Pallas kernels for 12%

profile of v5, /device:TPU:6, one launch (start us, length us, event | category | flops | bytes accessed | tf_op | source)
XLA Modules:
  0.0 179.2 jit_solution(4140736021703575344)
XLA Ops:
  0.7 1.7 select_maximum_fusion.refs_4_
  2.7 1.8 %select_maximum_fusion.1.refs_0_ = f32[2312,128]{1,0:T(8,128)S(1)} fusion(f32[1,128]{1,0:T(1,128)S(1)} %convert_bitcast_fusion, f32[2304,128]{1,0:T(8,128)} %bitcast.27), kind=kLoop, calls=%fused_computation.3 | loop fusion | flops 887808 | bytes 2363904 | tf_op jit(solution)/shard_map/concatenate | solution.py:32
  4.7 2.0 %collective-permute-start.3 = (f32[2312,128]{1,0:T(8,128)S(1)}, f32[2312,128]{1,0:T(8,128)S(1)}, u32[]{:S(2)}, u32[]{:S(2)}) collective-permute-start(f32[2312,128]{1,0:T(8,128)S(1)} %select_maximum_fusion.1.refs_0_), channel_id=1, source_target_pairs={{0,8},{64,120},{8,16},{72,64},{16,24},{80,72},{24,32},{88,80},{32,... | collective-permute-start | bytes 3551240 | tf_op jit(solution)/shard_map/ppermute | solution.py:153
  6.6 1.7 collective-permute-done.5
  8.4 1.9 %collective-permute-start.6 = (f32[2312,128]{1,0:T(8,128)S(1)}, f32[2312,128]{1,0:T(8,128)S(1)}, u32[]{:S(2)}, u32[]{:S(2)}) collective-permute-start(f32[2312,128]{1,0:T(8,128)S(1)} %collective-permute-done.5), channel_id=1, source_target_pairs={{0,8},{64,120},{8,16},{72,64},{16,24},{80,72},{24,32},{88,80},{32,... | collective-permute-start | bytes 3551240 | tf_op jit(solution)/shard_map/ppermute | solution.py:153
  10.8 1.5 collective-permute-start.2
  12.3 12.5 %collective-permute-done.3.refs_0_ = f32[2312,128]{1,0:T(8,128)S(1)} collective-permute-done((f32[2312,128]{1,0:T(8,128)S(1)}, f32[2312,128]{1,0:T(8,128)S(1)}, u32[]{:S(2)}, u32[]{:S(2)}) %collective-permute-start.3) | collective-permute-done | bytes 1183776 | tf_op jit(solution)/shard_map/ppermute | solution.py:153
  24.8 12.7 %collective-permute-done.6 = f32[2312,128]{1,0:T(8,128)S(1)} collective-permute-done((f32[2312,128]{1,0:T(8,128)S(1)}, f32[2312,128]{1,0:T(8,128)S(1)}, u32[]{:S(2)}, u32[]{:S(2)}) %collective-permute-start.6) | collective-permute-done | bytes 1183776 | tf_op jit(solution)/shard_map/ppermute | solution.py:153
  37.5 12.7 %collective-permute-done.4.refs_1_ = f32[2312,128]{1,0:T(8,128)S(1)} collective-permute-done((f32[2312,128]{1,0:T(8,128)S(1)}, f32[2312,128]{1,0:T(8,128)S(1)}, u32[]{:S(2)}, u32[]{:S(2)}) %collective-permute-start.4) | collective-permute-done | bytes 1183776 | tf_op jit(solution)/shard_map/ppermute | solution.py:153
  50.2 12.8 %collective-permute-done.7 = f32[2312,128]{1,0:T(8,128)} collective-permute-done((f32[2312,128]{1,0:T(8,128)S(1)}, f32[2312,128]{1,0:T(8,128)}, u32[]{:S(2)}, u32[]{:S(2)}) %collective-permute-start.7) | collective-permute-done | bytes 1183776 | tf_op jit(solution)/shard_map/ppermute | solution.py:153
  64.5 16.5 %collective-permute-done.9.refs_2_ = f32[2312,128]{1,0:T(8,128)} collective-permute-done((f32[2312,128]{1,0:T(8,128)S(1)}, f32[2312,128]{1,0:T(8,128)}, u32[]{:S(2)}, u32[]{:S(2)}) %collective-permute-start.9) | collective-permute-done | bytes 1183776 | tf_op jit(solution)/shard_map/ppermute | solution.py:153
  81.5 7.8 %collective-permute-done.11.refs_8_ = f32[4104,128]{1,0:T(8,128)} collective-permute-done((f32[4104,128]{1,0:T(8,128)}, f32[4104,128]{1,0:T(8,128)}, u32[]{:S(2)}, u32[]{:S(2)}) %collective-permute-start.11) | collective-permute-done | bytes 2101280 | tf_op jit(solution)/shard_map/ppermute | solution.py:148
  89.9 3.7 %collective-permute-done.17 = f32[2312,128]{1,0:T(8,128)S(1)} collective-permute-done((f32[2312,128]{1,0:T(8,128)}, f32[2312,128]{1,0:T(8,128)S(1)}, u32[]{:S(2)}, u32[]{:S(2)}) %collective-permute-start.17) | collective-permute-done | bytes 1183776 | tf_op jit(solution)/shard_map/ppermute | solution.py:153
  93.6 1.8 collective-permute-done.16.refs_1_
  95.7 1.3 collective-permute-done.18.refs_3_
  97.7 11.2 %shard_map.56 = (f32[12,128,128]{2,1,0:T(8,128)}, f32[12,128,128]{2,1,0:T(8,128)}, f32[6,128,128]{2,1,0:T(8,128)}, f32[6,128,128]{2,1,0:T(8,128)}, f32[6,128,128]{2,1,0:T(8,128)}, /*index=5*/f32[6,128,128]{2,1,0:T(8,128)}) custom-call(s32[5]{0:T(128)} %stack.48.place, f32[2312,128]{1,0:T(8,128)} %copy-done.3, f32[2312,128]{1,0:T(8,128)} %collective-permute-done.16.refs_1_, ...), custom_call_target="tpu_custom_call" | custom-call | flops 1811939328 | bytes 24641536 | tf_op jit(solution)/shard_map/pallas_call | solution.py:118
  108.9 1.6 collective-permute-start.19
  110.5 1.7 collective-permute-start.20
  112.2 2.6 %collective-permute-done.10.refs_3_ = f32[2312,128]{1,0:T(8,128)} collective-permute-done((f32[2312,128]{1,0:T(8,128)}, f32[2312,128]{1,0:T(8,128)}, u32[]{:S(2)}, u32[]{:S(2)}) %collective-permute-start.10) | collective-permute-done | bytes 1183776 | tf_op jit(solution)/shard_map/ppermute | solution.py:153
  114.8 11.2 %shard_map.55 = (f32[6,128,128]{2,1,0:T(8,128)}, f32[6,128,128]{2,1,0:T(8,128)}, f32[6,128,128]{2,1,0:T(8,128)}, f32[6,128,128]{2,1,0:T(8,128)}, f32[6,128,128]{...) custom-call(s32[5]{0:T(128)} %stack.48.place, f32[2312,128]{1,0:T(8,128)} %copy-done.1, ...), custom_call_target="tpu_custom_call" | custom-call | flops 1811939328 | bytes 24641536 | tf_op jit(solution)/shard_map/pallas_call | solution.py:118
  126.0 3.1 %collective-permute-start.23 = (f32[6,128,128]{2,1,0:T(8,128)}, f32[6,128,128]{2,1,0:T(8,128)S(1)}, u32[]{:S(2)}, u32[]{:S(2)}) collective-permute-start(f32[6,128,128]{2,1,0:T(8,128)} %get-tuple-element.54), channel_id=1, source_target_pairs={{0,3},{1,0},{2,1},{3,2},{4,7},{5,4},{6,5},{7,6},{8,11},{9,8},{10,9... | collective-permute-start | bytes 1179656 | tf_op jit(solution)/shard_map/ppermute | solution.py:20
  129.7 2.8 %collective-permute-start.28 = (f32[6,128,128]{2,1,0:T(8,128)S(1)}, f32[6,128,128]{2,1,0:T(8,128)S(1)}, u32[]{:S(2)}, u32[]{:S(2)}) collective-permute-start(f32[6,128,128]{2,1,0:T(8,128)S(1)} %slice_add_fusion), channel_id=1, source_target_pairs={{0,3},{1,0},{2,1},{3,2},{4,7},{5,4},{6,5},{7,6},{8,11},{9,8},{10,9... | collective-permute-start | bytes 1179656 | tf_op jit(solution)/shard_map/ppermute | solution.py:20
  133.4 5.5 %collective-permute-done.23 = f32[6,128,128]{2,1,0:T(8,128)S(1)} collective-permute-done((f32[6,128,128]{2,1,0:T(8,128)}, f32[6,128,128]{2,1,0:T(8,128)S(1)}, u32[]{:S(2)}, u32[]{:S(2)}) %collective-permute-start.23) | collective-permute-done | bytes 393248 | tf_op jit(solution)/shard_map/ppermute | solution.py:20
  140.0 3.9 %collective-permute-start.26 = (f32[6,128,128]{2,1,0:T(8,128)S(1)}, f32[6,128,128]{2,1,0:T(8,128)S(1)}, u32[]{:S(2)}, u32[]{:S(2)}) collective-permute-start(f32[6,128,128]{2,1,0:T(8,128)S(1)} %add.58), channel_id=1, source_target_pairs={{0,3},{1,0},{2,1},{3,2},{4,7},{5,4},{6,5},{7,6},{8,11},{9,8},{10,9... | collective-permute-start | bytes 1179656 | tf_op jit(solution)/shard_map/ppermute | solution.py:20
  143.9 3.4 %collective-permute-done.28 = f32[6,128,128]{2,1,0:T(8,128)S(1)} collective-permute-done((f32[6,128,128]{2,1,0:T(8,128)S(1)}, f32[6,128,128]{2,1,0:T(8,128)S(1)}, u32[]{:S(2)}, u32[]{:S(2)}) %collective-permute-start.28) | collective-permute-done | bytes 393248 | tf_op jit(solution)/shard_map/ppermute | solution.py:20
  149.2 2.6 %collective-permute-start.24 = (f32[6,128,128]{2,1,0:T(8,128)}, f32[6,128,128]{2,1,0:T(8,128)S(1)}, u32[]{:S(2)}, u32[]{:S(2)}) collective-permute-start(f32[6,128,128]{2,1,0:T(8,128)} %get-tuple-element.55), channel_id=1, source_target_pairs={{0,3},{1,0},{2,1},{3,2},{4,7},{5,4},{6,5},{7,6},{8,11},{9,8},{10,9... | collective-permute-start | bytes 1179656 | tf_op jit(solution)/shard_map/ppermute | solution.py:20
  151.8 2.2 %collective-permute-done.25 = f32[6,128,128]{2,1,0:T(8,128)S(1)} collective-permute-done((f32[6,128,128]{2,1,0:T(8,128)}, f32[6,128,128]{2,1,0:T(8,128)S(1)}, u32[]{:S(2)}, u32[]{:S(2)}) %collective-permute-start.25) | collective-permute-done | bytes 393248 | tf_op jit(solution)/shard_map/ppermute | solution.py:20
  154.1 1.6 collective-permute-done.26
  156.5 3.1 %collective-permute-start.27 = (f32[6,128,128]{2,1,0:T(8,128)}, f32[6,128,128]{2,1,0:T(8,128)S(1)}, u32[]{:S(2)}, u32[]{:S(2)}) collective-permute-start(f32[6,128,128]{2,1,0:T(8,128)} %add_add_fusion.1), channel_id=1, source_target_pairs={{0,4},{4,0},{1,5},{5,1},{2,6},{6,2},{3,7},{7,3},{8,12},{12,8},{9,1... | collective-permute-start | bytes 1179656 | tf_op jit(solution)/shard_map/ppermute | solution.py:20
  160.1 2.5 %collective-permute-done.21 = f32[6,128,128]{2,1,0:T(8,128)S(1)} collective-permute-done((f32[6,128,128]{2,1,0:T(8,128)S(1)}, f32[6,128,128]{2,1,0:T(8,128)S(1)}, u32[]{:S(2)}, u32[]{:S(2)}) %collective-permute-start.21) | collective-permute-done | bytes 393248 | tf_op jit(solution)/shard_map/ppermute | solution.py:20
  164.2 5.3 %collective-permute-done.27 = f32[6,128,128]{2,1,0:T(8,128)S(1)} collective-permute-done((f32[6,128,128]{2,1,0:T(8,128)}, f32[6,128,128]{2,1,0:T(8,128)S(1)}, u32[]{:S(2)}, u32[]{:S(2)}) %collective-permute-start.27) | collective-permute-done | bytes 393248 | tf_op jit(solution)/shard_map/ppermute | solution.py:20
  169.5 8.1 %collective-permute-done.29 = f32[6,128,128]{2,1,0:T(8,128)S(1)} collective-permute-done((f32[6,128,128]{2,1,0:T(8,128)}, f32[6,128,128]{2,1,0:T(8,128)S(1)}, u32[]{:S(2)}, u32[]{:S(2)}) %collective-permute-start.29) | collective-permute-done | bytes 393248 | tf_op jit(solution)/shard_map/ppermute | solution.py:20
  (70 shorter events, 14.2 us)
Async XLA Ops:
  2.4 95.3 %copy-start = (f32[4104,128]{1,0:T(8,128)}, f32[4104,128]{1,0:T(8,128)S(1)}, u32[]{:S(2)}) copy-start(f32[4104,128]{1,0:T(8,128)S(1)} %select_maximum_fusion.refs_4_) | copy-start | bytes 6303748
  2.4 8.3 %collective-permute-start.1 = (f32[4104,128]{1,0:T(8,128)S(1)}, f32[4104,128]{1,0:T(8,128)}, u32[]{:S(2)}, u32[]{:S(2)}) collective-permute-start(f32[4104,128]{1,0:T(8,128)S(1)} %select_maximum_fusion.refs_4_), channel_id=1, source_target_pairs={{0,64},{64,0},{1,65},{65,1},{2,66},{66,2},{3,67},{67,3},{4,68},{68... | collective-permute-start | bytes 6303752 | tf_op jit(solution)/shard_map/ppermute | solution.py:20
  4.5 104.4 %copy-start.1 = (f32[2312,128]{1,0:T(8,128)}, f32[2312,128]{1,0:T(8,128)S(1)}, u32[]{:S(2)}) copy-start(f32[2312,128]{1,0:T(8,128)S(1)} %select_maximum_fusion.1.refs_0_) | copy-start | bytes 3551236
  4.5 3.8 %collective-permute-start.5 = (f32[2312,128]{1,0:T(8,128)S(1)}, f32[2312,128]{1,0:T(8,128)S(1)}, u32[]{:S(2)}, u32[]{:S(2)}) collective-permute-start(f32[2312,128]{1,0:T(8,128)S(1)} %select_maximum_fusion.1.refs_0_), channel_id=1, source_target_pairs={{0,64},{64,0},{1,65},{65,1},{2,66},{66,2},{3,67},{67,3},{4,68},{68... | collective-permute-start | bytes 3551240 | tf_op jit(solution)/shard_map/ppermute | solution.py:20
  4.7 20.1 %collective-permute-start.3 = (f32[2312,128]{1,0:T(8,128)S(1)}, f32[2312,128]{1,0:T(8,128)S(1)}, u32[]{:S(2)}, u32[]{:S(2)}) collective-permute-start(f32[2312,128]{1,0:T(8,128)S(1)} %select_maximum_fusion.1.refs_0_), channel_id=1, source_target_pairs={{0,8},{64,120},{8,16},{72,64},{16,24},{80,72},{24,32},{88,80},{32,... | collective-permute-start | bytes 3551240 | tf_op jit(solution)/shard_map/ppermute | solution.py:153
  8.4 29.1 %collective-permute-start.6 = (f32[2312,128]{1,0:T(8,128)S(1)}, f32[2312,128]{1,0:T(8,128)S(1)}, u32[]{:S(2)}, u32[]{:S(2)}) collective-permute-start(f32[2312,128]{1,0:T(8,128)S(1)} %collective-permute-done.5), channel_id=1, source_target_pairs={{0,8},{64,120},{8,16},{72,64},{16,24},{80,72},{24,32},{88,80},{32,... | collective-permute-start | bytes 3551240 | tf_op jit(solution)/shard_map/ppermute | solution.py:153
  10.3 27.2 %collective-permute-start = (f32[4104,128]{1,0:T(8,128)S(1)}, f32[4104,128]{1,0:T(8,128)}, u32[]{:S(2)}, u32[]{:S(2)}) collective-permute-start(f32[4104,128]{1,0:T(8,128)S(1)} %select_maximum_fusion.refs_4_), channel_id=1, source_target_pairs={{0,128},{64,196},{128,4},{192,64},{4,132},{68,192},{132,0},{196,68... | collective-permute-start | bytes 6303752 | tf_op jit(solution)/shard_map/ppermute | solution.py:148
  10.8 52.2 %collective-permute-start.2 = (f32[4104,128]{1,0:T(8,128)}, f32[4104,128]{1,0:T(8,128)}, u32[]{:S(2)}, u32[]{:S(2)}) collective-permute-start(f32[4104,128]{1,0:T(8,128)} %collective-permute-done.1.refs_5_), channel_id=1, source_target_pairs={{0,128},{64,196},{128,4},{192,64},{4,132},{68,192},{132,0},{196,68... | collective-permute-start | bytes 6303752 | tf_op jit(solution)/shard_map/ppermute | solution.py:148
  24.8 25.4 %collective-permute-start.4 = (f32[2312,128]{1,0:T(8,128)S(1)}, f32[2312,128]{1,0:T(8,128)S(1)}, u32[]{:S(2)}, u32[]{:S(2)}) collective-permute-start(f32[2312,128]{1,0:T(8,128)S(1)} %collective-permute-done.3.refs_0_), channel_id=1, source_target_pairs={{0,8},{64,120},{8,16},{72,64},{16,24},{80,72},{24,32},{88,80},{32,... | collective-permute-start | bytes 3551240 | tf_op jit(solution)/shard_map/ppermute | solution.py:153
  37.5 25.5 %collective-permute-start.7 = (f32[2312,128]{1,0:T(8,128)S(1)}, f32[2312,128]{1,0:T(8,128)}, u32[]{:S(2)}, u32[]{:S(2)}) collective-permute-start(f32[2312,128]{1,0:T(8,128)S(1)} %collective-permute-done.6), channel_id=1, source_target_pairs={{0,8},{64,120},{8,16},{72,64},{16,24},{80,72},{24,32},{88,80},{32,... | collective-permute-start | bytes 3551240 | tf_op jit(solution)/shard_map/ppermute | solution.py:153
  63.0 26.4 %collective-permute-start.11 = (f32[4104,128]{1,0:T(8,128)}, f32[4104,128]{1,0:T(8,128)}, u32[]{:S(2)}, u32[]{:S(2)}) collective-permute-start(f32[4104,128]{1,0:T(8,128)} %collective-permute-done.refs_6_), channel_id=1, source_target_pairs={{0,128},{64,196},{128,4},{192,64},{4,132},{68,192},{132,0},{196,68... | collective-permute-start | bytes 6303752 | tf_op jit(solution)/shard_map/ppermute | solution.py:148
  63.5 17.6 %collective-permute-start.9 = (f32[2312,128]{1,0:T(8,128)S(1)}, f32[2312,128]{1,0:T(8,128)}, u32[]{:S(2)}, u32[]{:S(2)}) collective-permute-start(f32[2312,128]{1,0:T(8,128)S(1)} %collective-permute-done.4.refs_1_), channel_id=1, source_target_pairs={{0,8},{64,120},{8,16},{72,64},{16,24},{80,72},{24,32},{88,80},{32,... | collective-permute-start | bytes 3551240 | tf_op jit(solution)/shard_map/ppermute | solution.py:153
  63.5 30.1 %collective-permute-start.17 = (f32[2312,128]{1,0:T(8,128)}, f32[2312,128]{1,0:T(8,128)S(1)}, u32[]{:S(2)}, u32[]{:S(2)}) collective-permute-start(f32[2312,128]{1,0:T(8,128)} %collective-permute-done.7), channel_id=1, source_target_pairs={{0,8},{64,120},{8,16},{72,64},{16,24},{80,72},{24,32},{88,80},{32,... | collective-permute-start | bytes 3551240 | tf_op jit(solution)/shard_map/ppermute | solution.py:153
  81.0 16.7 %collective-permute-start.12 = (f32[4104,128]{1,0:T(8,128)}, f32[4104,128]{1,0:T(8,128)}, u32[]{:S(2)}, u32[]{:S(2)}) collective-permute-start(f32[4104,128]{1,0:T(8,128)} %collective-permute-done.refs_6_), channel_id=1, source_target_pairs={{0,64},{64,0},{1,65},{65,1},{2,66},{66,2},{3,67},{67,3},{4,68},{68... | collective-permute-start | bytes 6303752 | tf_op jit(solution)/shard_map/ppermute | solution.py:20
  81.0 16.7 %collective-permute-start.13 = (f32[4104,128]{1,0:T(8,128)}, f32[4104,128]{1,0:T(8,128)}, u32[]{:S(2)}, u32[]{:S(2)}) collective-permute-start(f32[4104,128]{1,0:T(8,128)} %collective-permute-done.2.refs_7_), channel_id=1, source_target_pairs={{0,64},{64,0},{1,65},{65,1},{2,66},{66,2},{3,67},{67,3},{4,68},{68... | collective-permute-start | bytes 6303752 | tf_op jit(solution)/shard_map/ppermute | solution.py:20
  89.4 8.3 %collective-permute-start.14 = (f32[4104,128]{1,0:T(8,128)}, f32[4104,128]{1,0:T(8,128)}, u32[]{:S(2)}, u32[]{:S(2)}) collective-permute-start(f32[4104,128]{1,0:T(8,128)} %collective-permute-done.11.refs_8_), channel_id=1, source_target_pairs={{0,64},{64,0},{1,65},{65,1},{2,66},{66,2},{3,67},{67,3},{4,68},{68... | collective-permute-start | bytes 6303752 | tf_op jit(solution)/shard_map/ppermute | solution.py:20
  89.7 5.6 %collective-permute-start.16 = (f32[2312,128]{1,0:T(8,128)S(1)}, f32[2312,128]{1,0:T(8,128)}, u32[]{:S(2)}, u32[]{:S(2)}) collective-permute-start(f32[2312,128]{1,0:T(8,128)S(1)} %collective-permute-done.6), channel_id=1, source_target_pairs={{0,64},{64,0},{1,65},{65,1},{2,66},{66,2},{3,67},{67,3},{4,68},{68... | collective-permute-start | bytes 3551240 | tf_op jit(solution)/shard_map/ppermute | solution.py:20
  93.6 3.5 %collective-permute-start.18 = (f32[2312,128]{1,0:T(8,128)S(1)}, f32[2312,128]{1,0:T(8,128)}, u32[]{:S(2)}, u32[]{:S(2)}) collective-permute-start(f32[2312,128]{1,0:T(8,128)S(1)} %collective-permute-done.17), channel_id=1, source_target_pairs={{0,64},{64,0},{1,65},{65,1},{2,66},{66,2},{3,67},{67,3},{4,68},{68... | collective-permute-start | bytes 3551240 | tf_op jit(solution)/shard_map/ppermute | solution.py:20
  95.4 16.9 %collective-permute-start.8 = (f32[2312,128]{1,0:T(8,128)}, f32[2312,128]{1,0:T(8,128)}, u32[]{:S(2)}, u32[]{:S(2)}) collective-permute-start(f32[2312,128]{1,0:T(8,128)} %collective-permute-done.7), channel_id=1, source_target_pairs={{0,64},{64,0},{1,65},{65,1},{2,66},{66,2},{3,67},{67,3},{4,68},{68... | collective-permute-start | bytes 3551240 | tf_op jit(solution)/shard_map/ppermute | solution.py:20
  97.0 17.8 %collective-permute-start.10 = (f32[2312,128]{1,0:T(8,128)}, f32[2312,128]{1,0:T(8,128)}, u32[]{:S(2)}, u32[]{:S(2)}) collective-permute-start(f32[2312,128]{1,0:T(8,128)} %collective-permute-done.9.refs_2_), channel_id=1, source_target_pairs={{0,8},{64,120},{8,16},{72,64},{16,24},{80,72},{24,32},{88,80},{32,... | collective-permute-start | bytes 3551240 | tf_op jit(solution)/shard_map/ppermute | solution.py:153
  108.9 20.2 %collective-permute-start.19 = (f32[12,128,128]{2,1,0:T(8,128)}, f32[12,128,128]{2,1,0:T(8,128)S(1)}, u32[]{:S(2)}, u32[]{:S(2)}) collective-permute-start(f32[12,128,128]{2,1,0:T(8,128)} %get-tuple-element.48), channel_id=1, source_target_pairs={{0,1},{1,2},{2,3},{3,0},{4,5},{5,6},{6,7},{7,4},{8,9},{9,10},{10,1... | collective-permute-start | bytes 2359304 | tf_op jit(solution)/shard_map/ppermute | solution.py:20
  110.5 19.1 %collective-permute-start.20 = (f32[12,128,128]{2,1,0:T(8,128)}, f32[12,128,128]{2,1,0:T(8,128)S(1)}, u32[]{:S(2)}, u32[]{:S(2)}) collective-permute-start(f32[12,128,128]{2,1,0:T(8,128)} %get-tuple-element.49), channel_id=1, source_target_pairs={{0,3},{1,0},{2,1},{3,2},{4,7},{5,4},{6,5},{7,6},{8,11},{9,8},{10,9... | collective-permute-start | bytes 2359304 | tf_op jit(solution)/shard_map/ppermute | solution.py:20
  126.0 13.0 %collective-permute-start.23 = (f32[6,128,128]{2,1,0:T(8,128)}, f32[6,128,128]{2,1,0:T(8,128)S(1)}, u32[]{:S(2)}, u32[]{:S(2)}) collective-permute-start(f32[6,128,128]{2,1,0:T(8,128)} %get-tuple-element.54), channel_id=1, source_target_pairs={{0,3},{1,0},{2,1},{3,2},{4,7},{5,4},{6,5},{7,6},{8,11},{9,8},{10,9... | collective-permute-start | bytes 1179656 | tf_op jit(solution)/shard_map/ppermute | solution.py:20
  129.7 17.6 %collective-permute-start.28 = (f32[6,128,128]{2,1,0:T(8,128)S(1)}, f32[6,128,128]{2,1,0:T(8,128)S(1)}, u32[]{:S(2)}, u32[]{:S(2)}) collective-permute-start(f32[6,128,128]{2,1,0:T(8,128)S(1)} %slice_add_fusion), channel_id=1, source_target_pairs={{0,3},{1,0},{2,1},{3,2},{4,7},{5,4},{6,5},{7,6},{8,11},{9,8},{10,9... | collective-permute-start | bytes 1179656 | tf_op jit(solution)/shard_map/ppermute | solution.py:20
  132.5 27.5 %collective-permute-start.15 = (f32[6,128,128]{2,1,0:T(8,128)}, f32[6,128,128]{2,1,0:T(8,128)S(1)}, u32[]{:S(2)}, u32[]{:S(2)}) collective-permute-start(f32[6,128,128]{2,1,0:T(8,128)} %get-tuple-element.45), channel_id=1, source_target_pairs={{0,1},{1,2},{2,3},{3,0},{4,5},{5,6},{6,7},{7,4},{8,9},{9,10},{10,1... | collective-permute-start | bytes 1179656 | tf_op jit(solution)/shard_map/ppermute | solution.py:20
  132.5 21.6 %collective-permute-start.25 = (f32[6,128,128]{2,1,0:T(8,128)}, f32[6,128,128]{2,1,0:T(8,128)S(1)}, u32[]{:S(2)}, u32[]{:S(2)}) collective-permute-start(f32[6,128,128]{2,1,0:T(8,128)} %get-tuple-element.60), channel_id=1, source_target_pairs={{0,1},{1,2},{2,3},{3,0},{4,5},{5,6},{6,7},{7,4},{8,9},{9,10},{10,1... | collective-permute-start | bytes 1179656 | tf_op jit(solution)/shard_map/ppermute | solution.py:20
  140.0 15.7 %collective-permute-start.26 = (f32[6,128,128]{2,1,0:T(8,128)S(1)}, f32[6,128,128]{2,1,0:T(8,128)S(1)}, u32[]{:S(2)}, u32[]{:S(2)}) collective-permute-start(f32[6,128,128]{2,1,0:T(8,128)S(1)} %add.58), channel_id=1, source_target_pairs={{0,3},{1,0},{2,1},{3,2},{4,7},{5,4},{6,5},{7,6},{8,11},{9,8},{10,9... | collective-permute-start | bytes 1179656 | tf_op jit(solution)/shard_map/ppermute | solution.py:20
  148.2 14.4 %collective-permute-start.21 = (f32[6,128,128]{2,1,0:T(8,128)S(1)}, f32[6,128,128]{2,1,0:T(8,128)S(1)}, u32[]{:S(2)}, u32[]{:S(2)}) collective-permute-start(f32[6,128,128]{2,1,0:T(8,128)S(1)} %get-tuple-element.71), channel_id=1, source_target_pairs={{0,1},{1,2},{2,3},{3,0},{4,5},{5,6},{6,7},{7,4},{8,9},{9,10},{10,1... | collective-permute-start | bytes 1179656 | tf_op jit(solution)/shard_map/ppermute | solution.py:20
  149.2 15.0 %collective-permute-start.24 = (f32[6,128,128]{2,1,0:T(8,128)}, f32[6,128,128]{2,1,0:T(8,128)S(1)}, u32[]{:S(2)}, u32[]{:S(2)}) collective-permute-start(f32[6,128,128]{2,1,0:T(8,128)} %get-tuple-element.55), channel_id=1, source_target_pairs={{0,3},{1,0},{2,1},{3,2},{4,7},{5,4},{6,5},{7,6},{8,11},{9,8},{10,9... | collective-permute-start | bytes 1179656 | tf_op jit(solution)/shard_map/ppermute | solution.py:20
  156.5 13.0 %collective-permute-start.27 = (f32[6,128,128]{2,1,0:T(8,128)}, f32[6,128,128]{2,1,0:T(8,128)S(1)}, u32[]{:S(2)}, u32[]{:S(2)}) collective-permute-start(f32[6,128,128]{2,1,0:T(8,128)} %add_add_fusion.1), channel_id=1, source_target_pairs={{0,4},{4,0},{1,5},{5,1},{2,6},{6,2},{3,7},{7,3},{8,12},{12,8},{9,1... | collective-permute-start | bytes 1179656 | tf_op jit(solution)/shard_map/ppermute | solution.py:20
  159.6 17.9 %collective-permute-start.29 = (f32[6,128,128]{2,1,0:T(8,128)}, f32[6,128,128]{2,1,0:T(8,128)S(1)}, u32[]{:S(2)}, u32[]{:S(2)}) collective-permute-start(f32[6,128,128]{2,1,0:T(8,128)} %get-tuple-element.72), channel_id=1, source_target_pairs={{0,4},{4,0},{1,5},{5,1},{2,6},{6,2},{3,7},{7,3},{8,12},{12,8},{9,1... | collective-permute-start | bytes 1179656 | tf_op jit(solution)/shard_map/ppermute | solution.py:20
  163.3 14.2 %collective-permute-start.22 = (f32[6,128,128]{2,1,0:T(8,128)}, f32[6,128,128]{2,1,0:T(8,128)S(1)}, u32[]{:S(2)}, u32[]{:S(2)}) collective-permute-start(f32[6,128,128]{2,1,0:T(8,128)} %add.52), channel_id=1, source_target_pairs={{0,1},{1,2},{2,3},{3,0},{4,5},{5,6},{6,7},{7,4},{8,9},{9,10},{10,1... | collective-permute-start | bytes 1179656 | tf_op jit(solution)/shard_map/ppermute | solution.py:20
  (10 other events, 222.7 us)
